TPU v7x, 512 devices: a whole 4x8x8 slice. The times are simulated.
512 devices in a mesh: row: 32 (over z, y_hi), col: 16 (over x, y_lo, core).
Axes of the slice: x: 4, y: 8 (y_hi: 4, y_lo: 2; y = y_hi * 2 + y_lo), z: 8, core: 2. Of those that a mesh axis runs over, the one named last changes fastest.
Arguments:
- constraint: bfloat16 [4096, 24576], P('row', 'col'), may hold values from -0.23925781 to 0.23925781
- pattern: int32 [32, 192], P('row', 'col'), may hold values 0 or 1
- scaling: float32 [24576], P('col'), may hold values from 0.1 to 10
- period: int32 [32], P('row'), may hold values from 0 to 15, never falling along the last dimension, each value on 1 to 4 neighbouring positions
- column_period: int32 [192], P('col'), may hold values from 0 to 15, never falling along the last dimension, each value on 1 to 24 neighbouring positions
- damping: float32 [16], replicated, may hold values from 0.5 to 5
Outputs:
- normal_lower: float32 [4096, 4096], P('col', 'row')
Inputs may be any that keep to these rules, and one draw needn't show every extreme that they name: Never falling along the block rows; each period covers 1 to 4 block rows, and at least one covers exactly 4. `column_period`: never falling along the block columns; each period covers 1 to 24 block columns, one exactly that many.
All inputs are finite; a program needn't handle non-finite values. No bound on the sum of `pattern` on one device may be relied on, other than what follows from the above.
Results may differ from a plain program's by a relative error of at most 0.0011.
Values may be sent and summed in bfloat16 or wider, within the bound.
No kernel may reach another device: no remote copies, remote signals or barrier semaphores. Data moves between devices by JAX's collectives and lax.ppermute only.
A program may use at most 64 MiB of HBM per device.

v0:
```python
import jax
import jax.numpy as jnp
from jax import lax
from jax.sharding import PartitionSpec as P


def body(constraint, pattern, scaling, period, column_period, damping):
    block_size = constraint.shape[0] // pattern.shape[0]
    own_rows = constraint.shape[0]
    same = column_period[None, :] == period[:, None]
    before = column_period[None, :] == period[:, None] - 1
    present = jnp.where(same | before | (pattern > 0), 1, 0).astype(jnp.int32)
    expanded = jnp.repeat(jnp.repeat(present, block_size, axis=0), block_size, axis=1)
    masked = constraint * expanded.astype(constraint.dtype)
    scaled = (masked.astype(jnp.float32) * scaling[None, :]).astype(jnp.bfloat16)
    my_row = lax.axis_index("row")
    my_col = lax.axis_index("col")
    gathered = lax.all_gather(masked, "row", axis=0, tiled=True)
    out_rows = gathered.shape[0] // lax.axis_size("col")
    summed = lax.psum_scatter(
        lax.dot_general(
            gathered, scaled, (((1,), (1,)), ((), ())), preferred_element_type=jnp.float32
        ),
        "col",
        scatter_dimension=0,
        tiled=True,
    )
    out_rows = summed.shape[0]
    row_global = my_col * out_rows + jnp.arange(out_rows, dtype=jnp.int32)
    col_global = my_row * own_rows + jnp.arange(own_rows, dtype=jnp.int32)
    lower_keep = (row_global // block_size)[:, None] >= (col_global // block_size)[None, :]
    result = jnp.where(lower_keep, summed, jnp.float32(0.0))
    onehot = (period[:, None] == jnp.arange(damping.shape[0], dtype=jnp.int32)[None, :]).astype(
        jnp.float32
    )
    per_block = jnp.sum(onehot * damping[None, :], axis=1)
    per_column = jnp.repeat(per_block, block_size)
    on_diagonal = row_global[:, None] == col_global[None, :]
    return result + jnp.where(on_diagonal, per_column[None, :], jnp.float32(0.0))


def solution(mesh):
    return jax.shard_map(
        body,
        mesh=mesh,
        in_specs=(P("row", "col"), P("row", "col"), P("col"), P("row"), P("col"), P()),
        out_specs=P("col", "row"),
        check_vma=False,
    )
```

profile of v0, /device:TPU:16, one launch (start us, length us, event | category | flops | bytes accessed | tf_op | source)
XLA Modules:
  0.0 278.5 jit_solution(4480207740269242601)
XLA Ops:
  6.5 0.0 copy-start
  6.5 0.0 all-gather.2.cloned.1.call-start
  7.2 0.7 convert_bitcast_fusion
  7.9 0.1 broadcast_bitcast_fusion
  8.0 1.8 broadcast_multiply_fusion
  9.7 0.0 all-gather.2.cloned.1.call-update
  9.8 0.0 reduce-scatter.2.cloned.1.call-start
  9.8 184.1 %all-gather.2.cloned.1.call-done = bf16[4096,1536]{1,0:T(8,128)(2,1)} async-done(((bf16[128,1536]{1,0:T(8,128)(2,1)}), bf16[4096,1536]{1,0:T(8,128)(2,1)}) %all-gather.2.cloned.1.call-update) | async-done | bytes 12582928 | tf_op jit(solution)/shard_map/all_gather | solution.py:18
  193.9 9.5 %fusion = f32[4096,128]{1,0:T(8,128)} fusion(bf16[4096,1536]{1,0:T(8,128)(2,1)} %all-gather.2.cloned.1.call-done, bf16[128,1536]{1,0:T(8,128)(2,1)} %broadcast_multiply_fusion, f32[1536]{0:T(1024)} %param.8), kind=kOutput, calls=%fused_computation.1 | convolution fusion | flops 1611202560 | bytes 15079424 | tf_op jit(solution)/shard_map/dot_general | solution.py:21
  203.4 0.0 reduce-scatter.2.cloned.1.call-update
  203.5 0.0 copy-done
  203.5 0.7 fusion.3
  204.1 65.2 %reduce-scatter.2.cloned.1.call-done = f32[256,128]{1,0:T(8,128)} async-done(((f32[4096,128]{1,0:T(8,128)}), f32[256,128]{1,0:T(8,128)}) %reduce-scatter.2.cloned.1.call-update) | async-done | bytes 131088 | tf_op jit(solution)/shard_map/reduce_scatter | solution.py:20
  269.4 2.3 select_add_fusion
  (2 shorter events, 0.0 us)
Async XLA Ops:
  6.5 196.9 %copy-start = (f32[16]{0:T(128)S(1)}, f32[16]{0:T(128)}, u32[]{:S(2)}) copy-start(f32[16]{0:T(128)} %param.11) | copy-start | bytes 196
  6.5 187.4 %all-gather.2.cloned.1.call-start = ((), (), s32[]{:S(2)}) async-start(), calls=%async_computation.1 | async-start | bytes 12976128 | tf_op jit(solution)/shard_map/all_gather | solution.py:18
  9.8 259.6 %reduce-scatter.2.cloned.1.call-start = ((), (), s32[]{:S(2)}) async-start(), calls=%async_computation.2 | async-start | bytes 2228224 | tf_op jit(solution)/shard_map/reduce_scatter | solution.py:20
Sparse Core Ops, SparseCore 0:
  10.5 183.3 all-gather.1
  203.5 65.7 reduce-scatter.1
where the time goes:
time: 279 us
  waiting for transfers between devices  249 us (89%)
  between operations  14.1 us (5%)
  matrix products  9.5 us (3%)
  other arithmetic  5.47 us (2%)
    all_gather x1, waiting for transfers between devices, body(): gathered = lax.all_gather(masked, 'row', axis=0, tiled=True)  184 us
    reduce_scatter x1, waiting for transfers between devices, body(): lax.psum_scatter(lax.dot_general(gathered, scaled, (((1,), (1,)), ((), ()...  65.2 us
    dot_general x1, matrix products, body(): lax.dot_general(gathered, scaled, (((1,), (1,)), ((), ())), preferred_ele...  9.5 us
  transfers between devices with their start and end apart: 2, of which 2 were waited for; matrix products, arithmetic and copies ran while one was open for 0% of the time, Pallas kernels for 0%

commit v1 on v0

v1 whole, which is shorter than its diff:
```python
import jax
import jax.numpy as jnp
import numpy as np
from jax import lax
from jax.experimental import pallas as pl
from jax.experimental.pallas import tpu as pltpu
from jax.sharding import Mesh, PartitionSpec as P

ROW = ("z", "yh")
COL = ("x", "yl", "core")
NZ, NY, NX, NL, NK = 8, 4, 4, 2, 2
NR, NCOL = NZ * NY, NX * NL * NK
BLK = 128
KC = 1536

HELD = ((0, 0), (0, 1), (1, 0), (7, 0), (1, 2), (5, 0), (3, 3))


def place(z, y):
    return (z % NZ) * NY + y % NY


def col_distance(a, b):
    ax, al, ak = a // (NL * NK), a // NK % NL, a % NK
    bx, bl, bk = b // (NL * NK), b // NK % NL, b % NK
    dx = abs(ax - bx)
    return min(dx, NX - dx) * 4 + abs(al - bl) * 4 + abs(ak - bk)


def plan():
    chosen = {}
    for t in range(len(HELD)):
        for s in range(t):
            dz, dy = (HELD[t][0] - HELD[s][0]) % NZ, (HELD[t][1] - HELD[s][1]) % NY
            if (dz, dy) not in chosen and (-dz % NZ, -dy % NY) not in chosen:
                chosen[(dz, dy)] = (s, t)
    left = np.zeros((NR, NCOL), np.int32)
    right = np.zeros((NR, NCOL), np.int32)
    sends = ([], [])
    seen = set()
    for z in range(NZ):
        for y in range(NY):
            g = place(z, y)
            todo = []
            for (dz, dy), (s, t) in chosen.items():
                if (dz, dy) == (4, 0) and z >= 4:
                    continue
                if (dz, dy) == (4, 2) and z < 4:
                    continue
                if (dz, dy) == (0, 2) and y >= 2:
                    continue
                a = place(z + HELD[s][0], y + HELD[s][1])
                b = place(z + HELD[t][0], y + HELD[t][1])
                todo.append((a, b, s, t) if a > b else (b, a, t, s))
            free = list(range(NCOL))
            cand = sorted(
                (col_distance(c, blk[0] // 2), i, c) for i, blk in enumerate(todo) for c in free
            )
            slot, used = {}, set()
            for _, i, c in cand:
                if i not in slot and c not in used:
                    slot[i] = c
                    used.add(c)
            for i, (p, q, l, r) in enumerate(todo):
                c = slot[i]
                left[g, c], right[g, c] = l, r
                sends[p % 2].append((g * NCOL + c, q * NCOL + p // 2))
                assert (p, q) not in seen
                seen.add((p, q))
    assert len(seen) == NR * (NR - 1) // 2
    return left, right, sends


def pairs_kernel(left, right, d_ref, *refs):
    rows, out, masked, scaled = refs[:7], refs[7], refs[8], refs[9]
    d = d_ref[...]
    for i in range(7):
        m = rows[i][...]
        masked[i] = m
        scaled[i] = (m.astype(jnp.float32) * d).astype(jnp.bfloat16)
    for c in range(NCOL):
        out[c] = lax.dot_general(
            masked[left[c]], scaled[right[c]], (((1,), (1,)), ((), ())), preferred_element_type=jnp.float32
        )


def diag_kernel(d_ref, m_ref, out):
    m = m_ref[...]
    s = (m.astype(jnp.float32) * d_ref[...]).astype(jnp.bfloat16)
    out[...] = lax.dot_general(m, s, (((1,), (1,)), ((), ())), preferred_element_type=jnp.float32)


def final_kernel(ids, period, damping, even, odd, diag, out):
    row, col = ids[0], ids[1]
    damp = damping[period[0]]
    i = lax.broadcasted_iota(jnp.int32, (BLK, BLK), 0)
    j = lax.broadcasted_iota(jnp.int32, (BLK, BLK), 1)
    full = diag[...] + jnp.where(i == j, damp, 0.0)
    own = row // 2 == col
    out[0:BLK] = jnp.where(own & (row % 2 == 0), full, even[...])
    out[BLK : 2 * BLK] = jnp.where(own & (row % 2 == 1), full, odd[...])


def body(constraint, pattern, scaling, period, column_period, damping):
    left, right, sends = plan()
    row, col = lax.axis_index(ROW), lax.axis_index(COL)
    vmem = pl.BlockSpec(memory_space=pltpu.VMEM)
    smem = pl.BlockSpec(memory_space=pltpu.SMEM)

    same = column_period[None, :] == period[:, None]
    before = column_period[None, :] == period[:, None] - 1
    present = jnp.where(same | before | (pattern > 0), 1, 0).astype(constraint.dtype)
    masked = constraint * jnp.repeat(present, BLK, axis=1)

    held = [masked]
    for dz, dy in HELD[1:]:
        pairs = [(place(z + dz, y + dy), place(z, y)) for z in range(NZ) for y in range(NY)]
        held.append(lax.ppermute(masked, ROW, pairs))

    d = scaling.reshape(1, KC)
    diag = pl.pallas_call(
        diag_kernel,
        out_shape=jax.ShapeDtypeStruct((BLK, BLK), jnp.float32),
        in_specs=[vmem, vmem],
        out_specs=vmem,
        name="diag",
    )(d, masked)
    strips = lax.all_to_all(diag, COL, 0, 0, tiled=True).reshape(NCOL, BLK // NCOL, BLK)
    strip = jnp.sum(strips, axis=0)
    diag = lax.all_to_all(jnp.tile(strip, (NCOL, 1)), COL, 0, 0, tiled=True)

    lt = lax.dynamic_index_in_dim(jnp.asarray(left), row, 0, keepdims=False)
    rt = lax.dynamic_index_in_dim(jnp.asarray(right), row, 0, keepdims=False)
    part = pl.pallas_call(
        pairs_kernel,
        out_shape=jax.ShapeDtypeStruct((NCOL, BLK, BLK), jnp.float32),
        in_specs=[smem, smem] + [vmem] * 8,
        out_specs=vmem,
        scratch_shapes=[pltpu.VMEM((7, BLK, KC), jnp.bfloat16)] * 2,
        compiler_params=pltpu.CompilerParams(vmem_limit_bytes=40 * 2**20),
        name="pairs",
    )(lt, rt, d, *held)

    parts = lax.all_to_all(part.astype(jnp.float16), COL, 0, 0, tiled=True)
    mine = jnp.sum(parts.astype(jnp.float32), axis=0)
    even = lax.ppermute(mine, ROW + COL, sends[0])
    odd = lax.ppermute(mine, ROW + COL, sends[1])
    return pl.pallas_call(
        final_kernel,
        out_shape=jax.ShapeDtypeStruct((2 * BLK, BLK), jnp.float32),
        in_specs=[smem] * 3 + [vmem] * 3,
        out_specs=vmem,
        name="final",
    )(jnp.stack([row, col]), period, damping, even, odd, diag)


def solution(mesh):
    split = Mesh(mesh.devices.reshape(NZ, NY, NX, NL, NK), ROW + COL)
    return jax.shard_map(
        body,
        mesh=split,
        in_specs=(P(ROW, COL), P(ROW, COL), P(COL), P(ROW), P(COL), P()),
        out_specs=P(COL, ROW),
        check_vma=False,
    )
```

time: 279 us -> 150 us (0.54)
  the two profiles are of different devices: /device:TPU:16 before, /device:TPU:6 now
where the time goes in v1:
time: 150 us; the launch traced here: 149 us
  waiting for transfers between devices  72.3 us (48%)
  starting transfers between devices  62.5 us (42%)
  Pallas kernels  6.81 us (5%)
  local copies, waits for them, and re-layouts  4.32 us (3%)
  other arithmetic  2.68 us (2%)
    ppermute x6, waiting for transfers between devices, body(): held.append(lax.ppermute(masked, ROW, pairs))  51.6 us
    ppermute x6, starting transfers between devices, body(): held.append(lax.ppermute(masked, ROW, pairs))  43.2 us
    all_to_all x1, waiting for transfers between devices, body(): parts = lax.all_to_all(part.astype(jnp.float16), COL, 0, 0, tiled=True)  8.55 us
    ppermute x1, waiting for transfers between devices, body(): odd = lax.ppermute(mine, ROW + COL, sends[1])  8.53 us
    all_to_all x1, starting transfers between devices, body(): diag = lax.all_to_all(jnp.tile(strip, (NCOL, 1)), COL, 0, 0, tiled=True)  6.45 us
    all_to_all x1, starting transfers between devices, body(): parts = lax.all_to_all(part.astype(jnp.float16), COL, 0, 0, tiled=True)  4.8 us
    all_to_all x1, starting transfers between devices, body(): lax.all_to_all(diag, COL, 0, 0, tiled=True).reshape(NCOL, BLK // NCOL, BLK)  4.8 us
    ppermute x1, waiting for transfers between devices, body(): even = lax.ppermute(mine, ROW + COL, sends[0])  3.34 us
  transfers between devices with their start and end apart: 11, of which 6 were waited for; matrix products, arithmetic and copies ran while one was open for 2% of the time, Pallas kernels for 3%

profile of v1, /device:TPU:6, one launch (start us, length us, event | category | flops | bytes accessed | tf_op | source)
XLA Modules:
  0.0 149.4 jit_solution(17545903980893172604)
XLA Ops:
  0.7 0.6 copy-done.7
  1.4 1.0 broadcast_multiply_fusion.refs_0_.m_ref
  2.5 6.2 %collective-permute-start = (bf16[128,1536]{1,0:T(8,128)(2,1)S(1)}, bf16[128,1536]{1,0:T(8,128)(2,1)S(1)}, u32[]{:S(2)}, u32[]{:S(2)}) collective-permute-start(bf16[128,1536]{1,0:T(8,128)(2,1)S(1)} %broadcast_multiply_fusion.refs_0_.m_ref), channel_id=1, source_target_pairs={{16,0},{32,16},{48,32},{0,48},{80,64},{96,80},{112,96},{64,112},{1... | collective-permute-start | bytes 1179656 | tf_op jit(solution)/shard_map/ppermute | solution.py:118
  8.6 10.9 %collective-permute-start.1 = (bf16[128,1536]{1,0:T(8,128)(2,1)S(1)}, bf16[128,1536]{1,0:T(8,128)(2,1)S(1)}, u32[]{:S(2)}, u32[]{:S(2)}) collective-permute-start(bf16[128,1536]{1,0:T(8,128)(2,1)S(1)} %broadcast_multiply_fusion.refs_0_.m_ref), channel_id=1, source_target_pairs={{64,0},{80,16},{96,32},{112,48},{128,64},{144,80},{160,96},{176,11... | collective-permute-start | bytes 1179656 | tf_op jit(solution)/shard_map/ppermute | solution.py:118
  19.6 1.9 %collective-permute-start.2 = (bf16[128,1536]{1,0:T(8,128)(2,1)S(1)}, bf16[128,1536]{1,0:T(8,128)(2,1)S(1)}, u32[]{:S(2)}, u32[]{:S(2)}) collective-permute-start(bf16[128,1536]{1,0:T(8,128)(2,1)S(1)} %broadcast_multiply_fusion.refs_0_.m_ref), channel_id=1, source_target_pairs={{448,0},{464,16},{480,32},{496,48},{0,64},{16,80},{32,96},{48,112}... | collective-permute-start | bytes 1179656 | tf_op jit(solution)/shard_map/ppermute | solution.py:118
  21.5 6.5 %collective-permute-start.3 = (bf16[128,1536]{1,0:T(8,128)(2,1)S(1)}, bf16[128,1536]{1,0:T(8,128)(2,1)S(1)}, u32[]{:S(2)}, u32[]{:S(2)}) collective-permute-start(bf16[128,1536]{1,0:T(8,128)(2,1)S(1)} %broadcast_multiply_fusion.refs_0_.m_ref), channel_id=1, source_target_pairs={{96,0},{112,16},{64,32},{80,48},{160,64},{176,80},{128,96},{144,11... | collective-permute-start | bytes 1179656 | tf_op jit(solution)/shard_map/ppermute | solution.py:118
  28.0 1.9 %collective-permute-start.4 = (bf16[128,1536]{1,0:T(8,128)(2,1)S(1)}, bf16[128,1536]{1,0:T(8,128)(2,1)S(1)}, u32[]{:S(2)}, u32[]{:S(2)}) collective-permute-start(bf16[128,1536]{1,0:T(8,128)(2,1)S(1)} %broadcast_multiply_fusion.refs_0_.m_ref), channel_id=1, source_target_pairs={{320,0},{336,16},{352,32},{368,48},{384,64},{400,80},{416,96},{432... | collective-permute-start | bytes 1179656 | tf_op jit(solution)/shard_map/ppermute | solution.py:118
  29.9 15.8 %collective-permute-start.5 = (bf16[128,1536]{1,0:T(8,128)(2,1)S(1)}, bf16[128,1536]{1,0:T(8,128)(2,1)S(1)}, u32[]{:S(2)}, u32[]{:S(2)}) collective-permute-start(bf16[128,1536]{1,0:T(8,128)(2,1)S(1)} %broadcast_multiply_fusion.refs_0_.m_ref), channel_id=1, source_target_pairs={{240,0},{192,16},{208,32},{224,48},{304,64},{256,80},{272,96},{288... | collective-permute-start | bytes 1179656 | tf_op jit(solution)/shard_map/ppermute | solution.py:118
  46.4 1.9 %diag.1 = f32[128,128]{1,0:T(8,128)} custom-call(f32[1,1536]{1,0:T(1,128)} %reshape.30.d_ref, bf16[128,1536]{1,0:T(8,128)(2,1)} %copy-done), custom_call_target="tpu_custom_call" | custom-call | tf_op jit(solution)/shard_map/diag/pallas_call | solution.py:121
  48.3 4.8 %all-to-all-start.1 = ((f32[16,8,128]{2,1,0:T(8,128)}), f32[16,8,128]{2,1,0:T(8,128)S(1)}, u32[]{:S(2)}, u32[]{:S(2)}) async-start(f32[16,8,128]{2,1,0:T(8,128)} %bitcast.21), calls=%async_computation.1 | async-start | bytes 131072 | tf_op jit(solution)/shard_map/all_to_all | solution.py:128
  53.1 0.7 dynamic-slice_bitcast_fusion
  53.8 4.0 %collective-permute-done.4.refs_5_ = bf16[128,1536]{1,0:T(8,128)(2,1)S(1)} collective-permute-done((bf16[128,1536]{1,0:T(8,128)(2,1)S(1)}, bf16[128,1536]{1,0:T(8,128)(2,1)S(1)}, u32[]{:S(2)}, u32[]{:S(2)}) %collective-permute-start.4) | collective-permute-done | bytes 393248 | tf_op jit(solution)/shard_map/ppermute | solution.py:118
  57.8 47.7 %collective-permute-done.5.refs_6_ = bf16[128,1536]{1,0:T(8,128)(2,1)S(1)} collective-permute-done((bf16[128,1536]{1,0:T(8,128)(2,1)S(1)}, bf16[128,1536]{1,0:T(8,128)(2,1)S(1)}, u32[]{:S(2)}, u32[]{:S(2)}) %collective-permute-start.5) | collective-permute-done | bytes 393248 | tf_op jit(solution)/shard_map/ppermute | solution.py:118
  105.5 1.0 copy-done.1
  106.5 3.3 %pairs.1 = f32[16,128,128]{2,1,0:T(8,128)S(1)} custom-call(s32[16]{0:T(128)S(1)} %get-tuple-element.6.left, s32[16]{0:T(128)S(1)} %get-tuple-element.5.right, f32[1,1536]{1,0:T(1,128)S(1)} %copy-done.2, bf16[128,1536]{1,0:T(8,128)(2,1)S(1)} %copy-done.1, bf16[128,1536]{1,0:T(8,128)(2,1)S(1)} %collective-permute-done.refs_1_, ...), custom_call_target="tpu_custom_call" | custom-call | tf_op jit(solution)/shard_map/pairs/pallas_call | solution.py:134
  109.8 0.9 convert_element_type.13
  110.7 4.8 %all-to-all-start = ((f16[16,128,128]{2,1,0:T(8,128)(2,1)}), f16[16,128,128]{2,1,0:T(8,128)(2,1)S(1)}, u32[]{:S(2)}, u32[]{:S(2)}) async-start(f16[16,128,128]{2,1,0:T(8,128)(2,1)} %convert_element_type.13), calls=%async_computation | async-start | bytes 1048576 | tf_op jit(solution)/shard_map/all_to_all | solution.py:144
  115.5 8.6 %all-to-all-done = f16[16,128,128]{2,1,0:T(8,128)(2,1)S(1)} async-done(((f16[16,128,128]{2,1,0:T(8,128)(2,1)}), f16[16,128,128]{2,1,0:T(8,128)(2,1)S(1)}, u32[]{:S(2)}, u32[]{:S(2)}) %all-to-all-start) | async-done | bytes 524320 | tf_op jit(solution)/shard_map/all_to_all | solution.py:144
  124.7 6.4 %all-to-all-start.2 = ((f32[16,8,128]{2,1,0:T(8,128)}), f32[16,8,128]{2,1,0:T(8,128)S(1)}, u32[]{:S(2)}, u32[]{:S(2)}) async-start(f32[16,8,128]{2,1,0:T(8,128)} %tile.2), calls=%async_computation.2 | async-start | bytes 131072 | tf_op jit(solution)/shard_map/all_to_all | solution.py:130
  131.2 1.9 %collective-permute-start.6 = (f32[128,128]{1,0:T(8,128)S(1)}, f32[128,128]{1,0:T(8,128)S(1)}, u32[]{:S(2)}, u32[]{:S(2)}) collective-permute-start(f32[128,128]{1,0:T(8,128)S(1)} %convert_reduce_fusion), channel_id=1, source_target_pairs={{2,2},{9,18},{14,30},{15,78},{3,3},{1,67},{12,110},{10,10},{11,26}... | collective-permute-start | bytes 196616 | tf_op jit(solution)/shard_map/ppermute | solution.py:146
  133.2 1.3 collective-permute-start.7
  135.3 3.3 %collective-permute-done.6.even = f32[128,128]{1,0:T(8,128)S(1)} collective-permute-done((f32[128,128]{1,0:T(8,128)S(1)}, f32[128,128]{1,0:T(8,128)S(1)}, u32[]{:S(2)}, u32[]{:S(2)}) %collective-permute-start.6) | collective-permute-done | bytes 65568 | tf_op jit(solution)/shard_map/ppermute | solution.py:146
  138.6 8.5 %collective-permute-done.7.odd = f32[128,128]{1,0:T(8,128)S(1)} collective-permute-done((f32[128,128]{1,0:T(8,128)S(1)}, f32[128,128]{1,0:T(8,128)S(1)}, u32[]{:S(2)}, u32[]{:S(2)}) %collective-permute-start.7) | collective-permute-done | bytes 65568 | tf_op jit(solution)/shard_map/ppermute | solution.py:147
  147.8 1.6 %final.1 = f32[256,128]{1,0:T(8,128)} custom-call(s32[2]{0:T(128)} %pad_add_fusion.ids, s32[1]{0:T(128)} %copy.9.period, f32[16]{0:T(128)} %damping.1, f32[128,128]{1,0:T(8,128)} %copy-done.4, f32[128,128]{1,0:T(8,128)} %copy-done.5, f32[128,128]{1,0:T(8,128)} %bitcast.22), custom_call_target="tpu_custom_call" | custom-call | tf_op jit(solution)/shard_map/final/pallas_call | solution.py:148
  (29 shorter events, 2.9 us)
Async XLA Ops:
  0.7 0.7 copy-start.7
  0.7 0.7 copy-start.8
  1.4 44.4 %copy-start.6 = (f32[1536]{0:T(1024)S(1)}, f32[1536]{0:T(1024)}, u32[]{:S(2)}) copy-start(f32[1536]{0:T(1024)} %param.10) | copy-start | bytes 18436
  2.5 43.9 %copy-start = (bf16[128,1536]{1,0:T(8,128)(2,1)}, bf16[128,1536]{1,0:T(8,128)(2,1)S(1)}, u32[]{:S(2)}) copy-start(bf16[128,1536]{1,0:T(8,128)(2,1)S(1)} %broadcast_multiply_fusion.refs_0_.m_ref) | copy-start | bytes 1179652
  2.5 27.5 %collective-permute-start = (bf16[128,1536]{1,0:T(8,128)(2,1)S(1)}, bf16[128,1536]{1,0:T(8,128)(2,1)S(1)}, u32[]{:S(2)}, u32[]{:S(2)}) collective-permute-start(bf16[128,1536]{1,0:T(8,128)(2,1)S(1)} %broadcast_multiply_fusion.refs_0_.m_ref), channel_id=1, source_target_pairs={{16,0},{32,16},{48,32},{0,48},{80,64},{96,80},{112,96},{64,112},{1... | collective-permute-start | bytes 1179656 | tf_op jit(solution)/shard_map/ppermute | solution.py:118
  8.6 45.2 %collective-permute-start.1 = (bf16[128,1536]{1,0:T(8,128)(2,1)S(1)}, bf16[128,1536]{1,0:T(8,128)(2,1)S(1)}, u32[]{:S(2)}, u32[]{:S(2)}) collective-permute-start(bf16[128,1536]{1,0:T(8,128)(2,1)S(1)} %broadcast_multiply_fusion.refs_0_.m_ref), channel_id=1, source_target_pairs={{64,0},{80,16},{96,32},{112,48},{128,64},{144,80},{160,96},{176,11... | collective-permute-start | bytes 1179656 | tf_op jit(solution)/shard_map/ppermute | solution.py:118
  19.6 34.2 %collective-permute-start.2 = (bf16[128,1536]{1,0:T(8,128)(2,1)S(1)}, bf16[128,1536]{1,0:T(8,128)(2,1)S(1)}, u32[]{:S(2)}, u32[]{:S(2)}) collective-permute-start(bf16[128,1536]{1,0:T(8,128)(2,1)S(1)} %broadcast_multiply_fusion.refs_0_.m_ref), channel_id=1, source_target_pairs={{448,0},{464,16},{480,32},{496,48},{0,64},{16,80},{32,96},{48,112}... | collective-permute-start | bytes 1179656 | tf_op jit(solution)/shard_map/ppermute | solution.py:118
  21.5 32.3 %collective-permute-start.3 = (bf16[128,1536]{1,0:T(8,128)(2,1)S(1)}, bf16[128,1536]{1,0:T(8,128)(2,1)S(1)}, u32[]{:S(2)}, u32[]{:S(2)}) collective-permute-start(bf16[128,1536]{1,0:T(8,128)(2,1)S(1)} %broadcast_multiply_fusion.refs_0_.m_ref), channel_id=1, source_target_pairs={{96,0},{112,16},{64,32},{80,48},{160,64},{176,80},{128,96},{144,11... | collective-permute-start | bytes 1179656 | tf_op jit(solution)/shard_map/ppermute | solution.py:118
  28.0 29.8 %collective-permute-start.4 = (bf16[128,1536]{1,0:T(8,128)(2,1)S(1)}, bf16[128,1536]{1,0:T(8,128)(2,1)S(1)}, u32[]{:S(2)}, u32[]{:S(2)}) collective-permute-start(bf16[128,1536]{1,0:T(8,128)(2,1)S(1)} %broadcast_multiply_fusion.refs_0_.m_ref), channel_id=1, source_target_pairs={{320,0},{336,16},{352,32},{368,48},{384,64},{400,80},{416,96},{432... | collective-permute-start | bytes 1179656 | tf_op jit(solution)/shard_map/ppermute | solution.py:118
  29.9 75.5 %collective-permute-start.5 = (bf16[128,1536]{1,0:T(8,128)(2,1)S(1)}, bf16[128,1536]{1,0:T(8,128)(2,1)S(1)}, u32[]{:S(2)}, u32[]{:S(2)}) collective-permute-start(bf16[128,1536]{1,0:T(8,128)(2,1)S(1)} %broadcast_multiply_fusion.refs_0_.m_ref), channel_id=1, source_target_pairs={{240,0},{192,16},{208,32},{224,48},{304,64},{256,80},{272,96},{288... | collective-permute-start | bytes 1179656 | tf_op jit(solution)/shard_map/ppermute | solution.py:118
  48.3 62.4 %all-to-all-start.1 = ((f32[16,8,128]{2,1,0:T(8,128)}), f32[16,8,128]{2,1,0:T(8,128)S(1)}, u32[]{:S(2)}, u32[]{:S(2)}) async-start(f32[16,8,128]{2,1,0:T(8,128)} %bitcast.21), calls=%async_computation.1 | async-start | bytes 131072 | tf_op jit(solution)/shard_map/all_to_all | solution.py:128
  53.1 52.4 %copy-start.2 = (f32[1,1536]{1,0:T(1,128)S(1)}, f32[1,1536]{1,0:T(1,128)}, u32[]{:S(2)}) copy-start(f32[1,1536]{1,0:T(1,128)} %reshape.30.d_ref) | copy-start | bytes 18436
  105.5 1.0 copy-start.1
  110.7 13.4 %all-to-all-start = ((f16[16,128,128]{2,1,0:T(8,128)(2,1)}), f16[16,128,128]{2,1,0:T(8,128)(2,1)S(1)}, u32[]{:S(2)}, u32[]{:S(2)}) async-start(f16[16,128,128]{2,1,0:T(8,128)(2,1)} %convert_element_type.13), calls=%async_computation | async-start | bytes 1048576 | tf_op jit(solution)/shard_map/all_to_all | solution.py:144
  124.7 10.6 %all-to-all-start.2 = ((f32[16,8,128]{2,1,0:T(8,128)}), f32[16,8,128]{2,1,0:T(8,128)S(1)}, u32[]{:S(2)}, u32[]{:S(2)}) async-start(f32[16,8,128]{2,1,0:T(8,128)} %tile.2), calls=%async_computation.2 | async-start | bytes 131072 | tf_op jit(solution)/shard_map/all_to_all | solution.py:130
  131.2 7.4 %collective-permute-start.6 = (f32[128,128]{1,0:T(8,128)S(1)}, f32[128,128]{1,0:T(8,128)S(1)}, u32[]{:S(2)}, u32[]{:S(2)}) collective-permute-start(f32[128,128]{1,0:T(8,128)S(1)} %convert_reduce_fusion), channel_id=1, source_target_pairs={{2,2},{9,18},{14,30},{15,78},{3,3},{1,67},{12,110},{10,10},{11,26}... | collective-permute-start | bytes 196616 | tf_op jit(solution)/shard_map/ppermute | solution.py:146
  133.2 14.0 %collective-permute-start.7 = (f32[128,128]{1,0:T(8,128)S(1)}, f32[128,128]{1,0:T(8,128)S(1)}, u32[]{:S(2)}, u32[]{:S(2)}) collective-permute-start(f32[128,128]{1,0:T(8,128)S(1)} %convert_reduce_fusion), channel_id=1, source_target_pairs={{0,0},{7,7},{6,23},{5,71},{4,103},{18,18},{16,34},{30,46},{31,94},... | collective-permute-start | bytes 196616 | tf_op jit(solution)/shard_map/ppermute | solution.py:147
  135.3 11.9 %copy-start.3 = (f32[16,8,128]{2,1,0:T(8,128)}, f32[16,8,128]{2,1,0:T(8,128)S(1)}, u32[]{:S(2)}) copy-start(f32[16,8,128]{2,1,0:T(8,128)S(1)} %all-to-all-done.2) | copy-start | bytes 196612
  138.6 8.5 %copy-start.4 = (f32[128,128]{1,0:T(8,128)}, f32[128,128]{1,0:T(8,128)S(1)}, u32[]{:S(2)}) copy-start(f32[128,128]{1,0:T(8,128)S(1)} %collective-permute-done.6.even) | copy-start | bytes 196612
  147.1 0.6 copy-start.5

commit v2 on v1

--- a/solution.py
+++ b/solution.py
@@ -13,7 +13,9 @@
 BLK = 128
 KC = 1536
 
-HELD = ((0, 0), (0, 1), (1, 0), (7, 0), (1, 2), (5, 0), (3, 3))
+HELD = ((0, 0), (0, 1), (1, 0), (0, 3), (5, 0), (0, 2), (2, 0), (4, 0))
+SOURCE = (0, 0, 0, 0, 0, 1, 2, 4)
+NH = len(HELD)
 
 
 def place(z, y):
@@ -72,9 +74,9 @@
 
 
 def pairs_kernel(left, right, d_ref, *refs):
-    rows, out, masked, scaled = refs[:7], refs[7], refs[8], refs[9]
+    rows, (out, masked, scaled) = refs[:NH], refs[NH:]
     d = d_ref[...]
-    for i in range(7):
+    for i in range(NH):
         m = rows[i][...]
         masked[i] = m
         scaled[i] = (m.astype(jnp.float32) * d).astype(jnp.bfloat16)
@@ -113,9 +115,10 @@
     masked = constraint * jnp.repeat(present, BLK, axis=1)
 
     held = [masked]
-    for dz, dy in HELD[1:]:
+    for i in range(1, NH):
+        dz, dy = HELD[i][0] - HELD[SOURCE[i]][0], HELD[i][1] - HELD[SOURCE[i]][1]
         pairs = [(place(z + dz, y + dy), place(z, y)) for z in range(NZ) for y in range(NY)]
-        held.append(lax.ppermute(masked, ROW, pairs))
+        held.append(lax.ppermute(held[SOURCE[i]], ROW, pairs))
 
     d = scaling.reshape(1, KC)
     diag = pl.pallas_call(
@@ -127,22 +130,27 @@
     )(d, masked)
     strips = lax.all_to_all(diag, COL, 0, 0, tiled=True).reshape(NCOL, BLK // NCOL, BLK)
     strip = jnp.sum(strips, axis=0)
-    diag = lax.all_to_all(jnp.tile(strip, (NCOL, 1)), COL, 0, 0, tiled=True)
+    high = strip.astype(jnp.float16)
+    low = (strip - high.astype(jnp.float32)).astype(jnp.float16)
+    riders = jnp.broadcast_to(jnp.concatenate([high, low], axis=0), (NCOL, 2 * BLK // NCOL, BLK))
 
     lt = lax.dynamic_index_in_dim(jnp.asarray(left), row, 0, keepdims=False)
     rt = lax.dynamic_index_in_dim(jnp.asarray(right), row, 0, keepdims=False)
     part = pl.pallas_call(
         pairs_kernel,
         out_shape=jax.ShapeDtypeStruct((NCOL, BLK, BLK), jnp.float32),
-        in_specs=[smem, smem] + [vmem] * 8,
+        in_specs=[smem, smem] + [vmem] * (1 + NH),
         out_specs=vmem,
-        scratch_shapes=[pltpu.VMEM((7, BLK, KC), jnp.bfloat16)] * 2,
+        scratch_shapes=[pltpu.VMEM((NH, BLK, KC), jnp.bfloat16)] * 2,
         compiler_params=pltpu.CompilerParams(vmem_limit_bytes=40 * 2**20),
         name="pairs",
     )(lt, rt, d, *held)
 
-    parts = lax.all_to_all(part.astype(jnp.float16), COL, 0, 0, tiled=True)
-    mine = jnp.sum(parts.astype(jnp.float32), axis=0)
+    parts = jnp.concatenate([part.astype(jnp.float16), riders], axis=1)
+    parts = lax.all_to_all(parts, COL, 0, 0, tiled=True).astype(jnp.float32)
+    mine = jnp.sum(parts[:, :BLK], axis=0)
+    step = BLK // NCOL
+    diag = (parts[:, BLK : BLK + step] + parts[:, BLK + step :]).reshape(BLK, BLK)
     even = lax.ppermute(mine, ROW + COL, sends[0])
     odd = lax.ppermute(mine, ROW + COL, sends[1])
     return pl.pallas_call(

time: 150 us -> 101 us (0.67)
  waiting for transfers between devices: 72.3 us -> 32.6 us
  starting transfers between devices: 62.5 us -> 51.6 us
  other arithmetic: 2.68 us -> 4.2 us
    ppermute x6 -> x7, waiting for transfers between devices: 51.6 us -> 14.1 us  [body(): held.append(lax.ppermute(held[SOURCE[i]], ROW, pairs))]
    ppermute x6 -> x7, starting transfers between devices: 43.2 us -> 35.9 us  [body(): held.append(lax.ppermute(held[SOURCE[i]], ROW, pairs))]
    all_to_all x2 -> x1, starting transfers between devices: 11.2 us -> 4.91 us  [body(): parts = lax.all_to_all(parts, COL, 0, 0, tiled=True).astype(jnp.float32)]
    ppermute x1, waiting for transfers between devices: 8.53 us -> 5.78 us  [body(): odd = lax.ppermute(mine, ROW + COL, sends[1])]
    ppermute x1, starting transfers between devices: 1.92 us -> 4.65 us  [body(): even = lax.ppermute(mine, ROW + COL, sends[0])]
    all_to_all x2 -> x1, waiting for transfers between devices: 8.74 us -> 8.67 us  [body(): parts = lax.all_to_all(parts, COL, 0, 0, tiled=True).astype(jnp.float32)]
  transfers between devices with their start and end apart: 11 -> 11, of which waited for: 6 -> 6; matrix products, arithmetic and copies ran while one was open for 2% -> 3% of each run, Pallas kernels for 3% -> 2%
where the time goes in v2:
time: 101 us
  starting transfers between devices  51.6 us (51%)
  waiting for transfers between devices  32.6 us (32%)
  Pallas kernels  6.95 us (7%)
  local copies, waits for them, and re-layouts  4.43 us (4%)
  other arithmetic  4.2 us (4%)
    ppermute x7, starting transfers between devices, body(): held.append(lax.ppermute(held[SOURCE[i]], ROW, pairs))  35.9 us
    ppermute x7, waiting for transfers between devices, body(): held.append(lax.ppermute(held[SOURCE[i]], ROW, pairs))  14.1 us
    all_to_all x1, waiting for transfers between devices, body(): parts = lax.all_to_all(parts, COL, 0, 0, tiled=True).astype(jnp.float32)  8.67 us
    ppermute x1, waiting for transfers between devices, body(): odd = lax.ppermute(mine, ROW + COL, sends[1])  5.78 us
    all_to_all x1, starting transfers between devices, body(): lax.all_to_all(diag, COL, 0, 0, tiled=True).reshape(NCOL, BLK // NCOL, BLK)  4.91 us
    all_to_all x1, starting transfers between devices, body(): parts = lax.all_to_all(parts, COL, 0, 0, tiled=True).astype(jnp.float32)  4.91 us
    ppermute x1, starting transfers between devices, body(): even = lax.ppermute(mine, ROW + COL, sends[0])  4.65 us
    ppermute x1, waiting for transfers between devices, body(): even = lax.ppermute(mine, ROW + COL, sends[0])  4.08 us
  transfers between devices with their start and end apart: 11, of which 6 were waited for; matrix products, arithmetic and copies ran while one was open for 3% of the time, Pallas kernels for 2%

profile of v2, /device:TPU:6, one launch (start us, length us, event | category | flops | bytes accessed | tf_op | source)
XLA Modules:
  0.0 100.6 jit_solution(17598683685889564275)
XLA Ops:
  1.4 1.0 %broadcast_multiply_fusion.refs_0_.m_ref = bf16[128,1536]{1,0:T(8,128)(2,1)S(1)} fusion(bf16[128,1536]{1,0:T(8,128)(2,1)} %param.8, bf16[1536]{0:T(1024)(128)(2,1)S(1)} %broadcast_bitcast_fusion), kind=kLoop, calls=%fused_computation.2 | loop fusion | flops 196608 | bytes 789504 | tf_op jit(solution)/shard_map/mul | solution.py:115
  2.4 6.2 %collective-permute-start = (bf16[128,1536]{1,0:T(8,128)(2,1)S(1)}, bf16[128,1536]{1,0:T(8,128)(2,1)S(1)}, u32[]{:S(2)}, u32[]{:S(2)}) collective-permute-start(bf16[128,1536]{1,0:T(8,128)(2,1)S(1)} %broadcast_multiply_fusion.refs_0_.m_ref), channel_id=1, source_target_pairs={{16,0},{32,16},{48,32},{0,48},{80,64},{96,80},{112,96},{64,112},{1... | collective-permute-start | bytes 1179656 | tf_op jit(solution)/shard_map/ppermute | solution.py:121
  8.6 10.9 %collective-permute-start.1 = (bf16[128,1536]{1,0:T(8,128)(2,1)S(1)}, bf16[128,1536]{1,0:T(8,128)(2,1)S(1)}, u32[]{:S(2)}, u32[]{:S(2)}) collective-permute-start(bf16[128,1536]{1,0:T(8,128)(2,1)S(1)} %broadcast_multiply_fusion.refs_0_.m_ref), channel_id=1, source_target_pairs={{64,0},{80,16},{96,32},{112,48},{128,64},{144,80},{160,96},{176,11... | collective-permute-start | bytes 1179656 | tf_op jit(solution)/shard_map/ppermute | solution.py:121
  19.6 1.9 %collective-permute-start.3 = (bf16[128,1536]{1,0:T(8,128)(2,1)S(1)}, bf16[128,1536]{1,0:T(8,128)(2,1)S(1)}, u32[]{:S(2)}, u32[]{:S(2)}) collective-permute-start(bf16[128,1536]{1,0:T(8,128)(2,1)S(1)} %broadcast_multiply_fusion.refs_0_.m_ref), channel_id=1, source_target_pairs={{320,0},{336,16},{352,32},{368,48},{384,64},{400,80},{416,96},{432... | collective-permute-start | bytes 1179656 | tf_op jit(solution)/shard_map/ppermute | solution.py:121
  21.5 1.3 %reshape.26.d_ref = f32[1,1536]{1,0:T(1,128)} reshape(f32[1536]{0:T(1024)} %param.10) | data formatting | bytes 12288 | tf_op jit(solution)/shard_map/reshape | solution.py:123
  22.8 1.9 %diag.1 = f32[128,128]{1,0:T(8,128)} custom-call(f32[1,1536]{1,0:T(1,128)} %reshape.26.d_ref, bf16[128,1536]{1,0:T(8,128)(2,1)} %copy-done), custom_call_target="tpu_custom_call" | custom-call | tf_op jit(solution)/shard_map/diag/pallas_call | solution.py:124
  24.7 4.9 %all-to-all-start = ((f32[16,8,128]{2,1,0:T(8,128)}), f32[16,8,128]{2,1,0:T(8,128)S(1)}, u32[]{:S(2)}, u32[]{:S(2)}) async-start(f32[16,8,128]{2,1,0:T(8,128)} %bitcast.22), calls=%async_computation | async-start | bytes 131072 | tf_op jit(solution)/shard_map/all_to_all | solution.py:131
  29.6 1.9 %collective-permute-start.2 = (bf16[128,1536]{1,0:T(8,128)(2,1)}, bf16[128,1536]{1,0:T(8,128)(2,1)S(1)}, u32[]{:S(2)}, u32[]{:S(2)}) collective-permute-start(bf16[128,1536]{1,0:T(8,128)(2,1)} %copy-done), channel_id=1, source_target_pairs={{48,0},{0,16},{16,32},{32,48},{112,64},{64,80},{80,96},{96,112},{1... | collective-permute-start | bytes 1179656 | tf_op jit(solution)/shard_map/ppermute | solution.py:121
  31.6 6.0 %collective-permute-start.4 = (bf16[128,1536]{1,0:T(8,128)(2,1)S(1)}, bf16[128,1536]{1,0:T(8,128)(2,1)S(1)}, u32[]{:S(2)}, u32[]{:S(2)}) collective-permute-start(bf16[128,1536]{1,0:T(8,128)(2,1)S(1)} %collective-permute-done.refs_1_), channel_id=1, source_target_pairs={{16,0},{32,16},{48,32},{0,48},{80,64},{96,80},{112,96},{64,112},{1... | collective-permute-start | bytes 1179656 | tf_op jit(solution)/shard_map/ppermute | solution.py:121
  37.6 5.2 %collective-permute-start.5 = (bf16[128,1536]{1,0:T(8,128)(2,1)S(1)}, bf16[128,1536]{1,0:T(8,128)(2,1)S(1)}, u32[]{:S(2)}, u32[]{:S(2)}) collective-permute-start(bf16[128,1536]{1,0:T(8,128)(2,1)S(1)} %collective-permute-done.1.refs_2_), channel_id=1, source_target_pairs={{64,0},{80,16},{96,32},{112,48},{128,64},{144,80},{160,96},{176,11... | collective-permute-start | bytes 1179656 | tf_op jit(solution)/shard_map/ppermute | solution.py:121
  42.9 4.4 %collective-permute-done.3.refs_4_ = bf16[128,1536]{1,0:T(8,128)(2,1)S(1)} collective-permute-done((bf16[128,1536]{1,0:T(8,128)(2,1)S(1)}, bf16[128,1536]{1,0:T(8,128)(2,1)S(1)}, u32[]{:S(2)}, u32[]{:S(2)}) %collective-permute-start.3) | collective-permute-done | bytes 393248 | tf_op jit(solution)/shard_map/ppermute | solution.py:121
  47.3 3.7 %collective-permute-start.6 = (bf16[128,1536]{1,0:T(8,128)(2,1)S(1)}, bf16[128,1536]{1,0:T(8,128)(2,1)S(1)}, u32[]{:S(2)}, u32[]{:S(2)}) collective-permute-start(bf16[128,1536]{1,0:T(8,128)(2,1)S(1)} %collective-permute-done.3.refs_4_), channel_id=1, source_target_pairs={{448,0},{464,16},{480,32},{496,48},{0,64},{16,80},{32,96},{48,112}... | collective-permute-start | bytes 1179656 | tf_op jit(solution)/shard_map/ppermute | solution.py:121
  51.7 2.9 %collective-permute-done.4.refs_5_ = bf16[128,1536]{1,0:T(8,128)(2,1)S(1)} collective-permute-done((bf16[128,1536]{1,0:T(8,128)(2,1)S(1)}, bf16[128,1536]{1,0:T(8,128)(2,1)S(1)}, u32[]{:S(2)}, u32[]{:S(2)}) %collective-permute-start.4) | collective-permute-done | bytes 393248 | tf_op jit(solution)/shard_map/ppermute | solution.py:121
  54.6 6.8 %collective-permute-done.6.refs_7_ = bf16[128,1536]{1,0:T(8,128)(2,1)S(1)} collective-permute-done((bf16[128,1536]{1,0:T(8,128)(2,1)S(1)}, bf16[128,1536]{1,0:T(8,128)(2,1)S(1)}, u32[]{:S(2)}, u32[]{:S(2)}) %collective-permute-start.6) | collective-permute-done | bytes 393248 | tf_op jit(solution)/shard_map/ppermute | solution.py:121
  61.4 1.0 copy-done.1
  63.1 3.5 %pairs.1 = f32[16,128,128]{2,1,0:T(8,128)S(1)} custom-call(s32[16]{0:T(128)S(1)} %get-tuple-element.8.left, s32[16]{0:T(128)S(1)} %get-tuple-element.7.right, f32[1,1536]{1,0:T(1,128)S(1)} %copy-done.2, bf16[128,1536]{1,0:T(8,128)(2,1)S(1)} %copy-done.1, bf16[128,1536]{1,0:T(8,128)(2,1)S(1)} %collective-permute-done.refs_1_, ...), custom_call_target="tpu_custom_call" | custom-call | tf_op jit(solution)/shard_map/pairs/pallas_call | solution.py:139
  66.7 1.0 pad_maximum_fusion
  67.6 4.9 %all-to-all-start.1 = ((f16[16,144,128]{2,1,0:T(8,128)(2,1)}), f16[16,144,128]{2,1,0:T(8,128)(2,1)S(1)}, u32[]{:S(2)}, u32[]{:S(2)}) async-start(f16[16,144,128]{2,1,0:T(8,128)(2,1)} %pad_maximum_fusion), calls=%async_computation.1 | async-start | bytes 1179648 | tf_op jit(solution)/shard_map/all_to_all | solution.py:150
  73.2 8.7 %all-to-all-done.1 = f16[16,144,128]{2,1,0:T(8,128)(2,1)S(1)} async-done(((f16[16,144,128]{2,1,0:T(8,128)(2,1)}), f16[16,144,128]{2,1,0:T(8,128)(2,1)S(1)}, u32[]{:S(2)}, u32[]{:S(2)}) %all-to-all-start.1) | async-done | bytes 589856 | tf_op jit(solution)/shard_map/all_to_all | solution.py:150
  82.0 4.6 %collective-permute-start.7 = (f32[128,128]{1,0:T(8,128)S(1)}, f32[128,128]{1,0:T(8,128)S(1)}, u32[]{:S(2)}, u32[]{:S(2)}) collective-permute-start(f32[128,128]{1,0:T(8,128)S(1)} %slice_reduce_fusion), channel_id=1, source_target_pairs={{2,2},{3,18},{6,50},{10,10},{11,26},{14,74},{7,58},{15,34},{9,42},... | collective-permute-start | bytes 196616 | tf_op jit(solution)/shard_map/ppermute | solution.py:154
  86.6 1.3 %collective-permute-start.8 = (f32[128,128]{1,0:T(8,128)S(1)}, f32[128,128]{1,0:T(8,128)S(1)}, u32[]{:S(2)}, u32[]{:S(2)}) collective-permute-start(f32[128,128]{1,0:T(8,128)S(1)} %slice_reduce_fusion), channel_id=1, source_target_pairs={{0,0},{1,17},{18,18},{19,34},{22,2},{26,26},{27,42},{30,90},{23,10... | collective-permute-start | bytes 196616 | tf_op jit(solution)/shard_map/ppermute | solution.py:155
  88.6 4.1 %collective-permute-done.7.even = f32[128,128]{1,0:T(8,128)S(1)} collective-permute-done((f32[128,128]{1,0:T(8,128)S(1)}, f32[128,128]{1,0:T(8,128)S(1)}, u32[]{:S(2)}, u32[]{:S(2)}) %collective-permute-start.7) | collective-permute-done | bytes 65568 | tf_op jit(solution)/shard_map/ppermute | solution.py:154
  92.6 5.8 %collective-permute-done.8.odd = f32[128,128]{1,0:T(8,128)S(1)} collective-permute-done((f32[128,128]{1,0:T(8,128)S(1)}, f32[128,128]{1,0:T(8,128)S(1)}, u32[]{:S(2)}, u32[]{:S(2)}) %collective-permute-start.8) | collective-permute-done | bytes 65568 | tf_op jit(solution)/shard_map/ppermute | solution.py:155
  99.1 1.6 %final.1 = f32[256,128]{1,0:T(8,128)} custom-call(s32[2]{0:T(128)} %pad_add_fusion.ids, s32[1]{0:T(128)} %copy.9.period, f32[16]{0:T(128)} %damping.1, f32[128,128]{1,0:T(8,128)} %copy-done.3, f32[128,128]{1,0:T(8,128)} %copy-done.4, f32[128,128]{1,0:T(8,128)} %fusion.diag), custom_call_target="tpu_custom_call" | custom-call | tf_op jit(solution)/shard_map/final/pallas_call | solution.py:156
  (26 shorter events, 4.3 us)
Async XLA Ops:
  2.4 20.4 %copy-start = (bf16[128,1536]{1,0:T(8,128)(2,1)}, bf16[128,1536]{1,0:T(8,128)(2,1)S(1)}, u32[]{:S(2)}) copy-start(bf16[128,1536]{1,0:T(8,128)(2,1)S(1)} %broadcast_multiply_fusion.refs_0_.m_ref) | copy-start | bytes 1179652
  2.4 29.1 %collective-permute-start = (bf16[128,1536]{1,0:T(8,128)(2,1)S(1)}, bf16[128,1536]{1,0:T(8,128)(2,1)S(1)}, u32[]{:S(2)}, u32[]{:S(2)}) collective-permute-start(bf16[128,1536]{1,0:T(8,128)(2,1)S(1)} %broadcast_multiply_fusion.refs_0_.m_ref), channel_id=1, source_target_pairs={{16,0},{32,16},{48,32},{0,48},{80,64},{96,80},{112,96},{64,112},{1... | collective-permute-start | bytes 1179656 | tf_op jit(solution)/shard_map/ppermute | solution.py:121
  8.6 29.0 %collective-permute-start.1 = (bf16[128,1536]{1,0:T(8,128)(2,1)S(1)}, bf16[128,1536]{1,0:T(8,128)(2,1)S(1)}, u32[]{:S(2)}, u32[]{:S(2)}) collective-permute-start(bf16[128,1536]{1,0:T(8,128)(2,1)S(1)} %broadcast_multiply_fusion.refs_0_.m_ref), channel_id=1, source_target_pairs={{64,0},{80,16},{96,32},{112,48},{128,64},{144,80},{160,96},{176,11... | collective-permute-start | bytes 1179656 | tf_op jit(solution)/shard_map/ppermute | solution.py:121
  19.6 27.7 %collective-permute-start.3 = (bf16[128,1536]{1,0:T(8,128)(2,1)S(1)}, bf16[128,1536]{1,0:T(8,128)(2,1)S(1)}, u32[]{:S(2)}, u32[]{:S(2)}) collective-permute-start(bf16[128,1536]{1,0:T(8,128)(2,1)S(1)} %broadcast_multiply_fusion.refs_0_.m_ref), channel_id=1, source_target_pairs={{320,0},{336,16},{352,32},{368,48},{384,64},{400,80},{416,96},{432... | collective-permute-start | bytes 1179656 | tf_op jit(solution)/shard_map/ppermute | solution.py:121
  24.7 26.9 %all-to-all-start = ((f32[16,8,128]{2,1,0:T(8,128)}), f32[16,8,128]{2,1,0:T(8,128)S(1)}, u32[]{:S(2)}, u32[]{:S(2)}) async-start(f32[16,8,128]{2,1,0:T(8,128)} %bitcast.22), calls=%async_computation | async-start | bytes 131072 | tf_op jit(solution)/shard_map/all_to_all | solution.py:131
  29.6 22.1 %collective-permute-start.2 = (bf16[128,1536]{1,0:T(8,128)(2,1)}, bf16[128,1536]{1,0:T(8,128)(2,1)S(1)}, u32[]{:S(2)}, u32[]{:S(2)}) collective-permute-start(bf16[128,1536]{1,0:T(8,128)(2,1)} %copy-done), channel_id=1, source_target_pairs={{48,0},{0,16},{16,32},{32,48},{112,64},{64,80},{80,96},{96,112},{1... | collective-permute-start | bytes 1179656 | tf_op jit(solution)/shard_map/ppermute | solution.py:121
  31.6 23.0 %collective-permute-start.4 = (bf16[128,1536]{1,0:T(8,128)(2,1)S(1)}, bf16[128,1536]{1,0:T(8,128)(2,1)S(1)}, u32[]{:S(2)}, u32[]{:S(2)}) collective-permute-start(bf16[128,1536]{1,0:T(8,128)(2,1)S(1)} %collective-permute-done.refs_1_), channel_id=1, source_target_pairs={{16,0},{32,16},{48,32},{0,48},{80,64},{96,80},{112,96},{64,112},{1... | collective-permute-start | bytes 1179656 | tf_op jit(solution)/shard_map/ppermute | solution.py:121
  37.6 17.0 %collective-permute-start.5 = (bf16[128,1536]{1,0:T(8,128)(2,1)S(1)}, bf16[128,1536]{1,0:T(8,128)(2,1)S(1)}, u32[]{:S(2)}, u32[]{:S(2)}) collective-permute-start(bf16[128,1536]{1,0:T(8,128)(2,1)S(1)} %collective-permute-done.1.refs_2_), channel_id=1, source_target_pairs={{64,0},{80,16},{96,32},{112,48},{128,64},{144,80},{160,96},{176,11... | collective-permute-start | bytes 1179656 | tf_op jit(solution)/shard_map/ppermute | solution.py:121
  47.3 14.1 %collective-permute-start.6 = (bf16[128,1536]{1,0:T(8,128)(2,1)S(1)}, bf16[128,1536]{1,0:T(8,128)(2,1)S(1)}, u32[]{:S(2)}, u32[]{:S(2)}) collective-permute-start(bf16[128,1536]{1,0:T(8,128)(2,1)S(1)} %collective-permute-done.3.refs_4_), channel_id=1, source_target_pairs={{448,0},{464,16},{480,32},{496,48},{0,64},{16,80},{32,96},{48,112}... | collective-permute-start | bytes 1179656 | tf_op jit(solution)/shard_map/ppermute | solution.py:121
  61.4 1.0 copy-start.1
  62.4 0.7 copy-start.2
  67.6 14.2 %all-to-all-start.1 = ((f16[16,144,128]{2,1,0:T(8,128)(2,1)}), f16[16,144,128]{2,1,0:T(8,128)(2,1)S(1)}, u32[]{:S(2)}, u32[]{:S(2)}) async-start(f16[16,144,128]{2,1,0:T(8,128)(2,1)} %pad_maximum_fusion), calls=%async_computation.1 | async-start | bytes 1179648 | tf_op jit(solution)/shard_map/all_to_all | solution.py:150
  82.0 10.7 %collective-permute-start.7 = (f32[128,128]{1,0:T(8,128)S(1)}, f32[128,128]{1,0:T(8,128)S(1)}, u32[]{:S(2)}, u32[]{:S(2)}) collective-permute-start(f32[128,128]{1,0:T(8,128)S(1)} %slice_reduce_fusion), channel_id=1, source_target_pairs={{2,2},{3,18},{6,50},{10,10},{11,26},{14,74},{7,58},{15,34},{9,42},... | collective-permute-start | bytes 196616 | tf_op jit(solution)/shard_map/ppermute | solution.py:154
  86.6 11.8 %collective-permute-start.8 = (f32[128,128]{1,0:T(8,128)S(1)}, f32[128,128]{1,0:T(8,128)S(1)}, u32[]{:S(2)}, u32[]{:S(2)}) collective-permute-start(f32[128,128]{1,0:T(8,128)S(1)} %slice_reduce_fusion), channel_id=1, source_target_pairs={{0,0},{1,17},{18,18},{19,34},{22,2},{26,26},{27,42},{30,90},{23,10... | collective-permute-start | bytes 196616 | tf_op jit(solution)/shard_map/ppermute | solution.py:155
  92.6 5.8 %copy-start.3 = (f32[128,128]{1,0:T(8,128)}, f32[128,128]{1,0:T(8,128)S(1)}, u32[]{:S(2)}) copy-start(f32[128,128]{1,0:T(8,128)S(1)} %collective-permute-done.7.even) | copy-start | bytes 196612
  98.4 0.6 copy-start.4

commit v3 on v2

v3 whole, which is shorter than its diff:
```python
import jax
import jax.numpy as jnp
import numpy as np
from jax import lax
from jax.experimental import pallas as pl
from jax.experimental.pallas import tpu as pltpu
from jax.sharding import Mesh, PartitionSpec as P

ROW = ("z", "yh")
COL = ("x", "yl", "core")
NZ, NY, NX, NL, NK = 8, 4, 4, 2, 2
NR, NCOL = NZ * NY, NX * NL * NK
BLK = 128
KC = 1536

HELD = ((0, 0), (5, 0), (1, 0), (0, 1), (0, 3), (2, 0), (0, 2), (4, 0))
NH = len(HELD)
EARLY = 5
HALF = NCOL // 2


def place(z, y):
    return (z % NZ) * NY + y % NY


def col_distance(a, b):
    ax, al, ak = a // (NL * NK), a // NK % NL, a % NK
    bx, bl, bk = b // (NL * NK), b // NK % NL, b % NK
    dx = abs(ax - bx)
    return min(dx, NX - dx) * 4 + abs(al - bl) * 4 + abs(ak - bk)


def plan():
    chosen = {}
    for t in range(NH):
        for s in range(t):
            dz, dy = (HELD[t][0] - HELD[s][0]) % NZ, (HELD[t][1] - HELD[s][1]) % NY
            if (dz, dy) not in chosen and (-dz % NZ, -dy % NY) not in chosen:
                chosen[(dz, dy)] = (s, t)
    left = np.zeros((NR, NCOL), np.int32)
    right = np.zeros((NR, NCOL), np.int32)
    sends = ([], [])
    seen = set()
    for z in range(NZ):
        for y in range(NY):
            g = place(z, y)
            early, late, either = [], [], []
            for (dz, dy), (s, t) in chosen.items():
                if (dz, dy) == (4, 0) and z >= 4 or (dz, dy) == (4, 2) and z < 4 or (dz, dy) == (0, 2) and y >= 2:
                    continue
                a = place(z + HELD[s][0], y + HELD[s][1])
                b = place(z + HELD[t][0], y + HELD[t][1])
                pair = (a, b, s, t) if a > b else (b, a, t, s)
                (either if (dz, dy) == (0, 2) else early if t < EARLY else late).append(pair)
            for pair in either:
                (early if len(early) < HALF else late).append(pair)
            assert len(early) <= HALF and len(late) <= HALF
            for base, todo in ((0, early), (1, late)):
                cand = sorted(
                    (col_distance(2 * i + base, blk[0] // 2), n, i) for n, blk in enumerate(todo) for i in range(HALF)
                )
                slot, used = {}, set()
                for _, n, i in cand:
                    if n not in slot and i not in used:
                        slot[n] = i
                        used.add(i)
                for n, (p, q, l, r) in enumerate(todo):
                    left[g, base * HALF + slot[n]], right[g, base * HALF + slot[n]] = l, r
                    sends[p % 2].append((g * NCOL + 2 * slot[n] + base, q * NCOL + p // 2))
                    assert (p, q) not in seen
                    seen.add((p, q))
    assert len(seen) == NR * (NR - 1) // 2
    return left, right, sends


def product(m, s):
    return lax.dot_general(m, s, (((1,), (1,)), ((), ())), preferred_element_type=jnp.float32)


def scale(m, d):
    return (m.astype(jnp.float32) * d).astype(jnp.bfloat16)


def early_kernel(left, right, d_ref, *refs):
    rows, (out, masked, scaled) = refs[:EARLY], refs[EARLY:]
    d = d_ref[...]
    for i in range(EARLY):
        m = rows[i][...]
        masked[i] = m
        scaled[i] = scale(m, d)
    for c in range(HALF):
        out[c] = product(masked[left[c]], scaled[right[c]])


def late_kernel(left, right, d_ref, masked_in, scaled_in, early, riders, *refs):
    rows, (out, masked, scaled) = refs[: NH - EARLY], refs[NH - EARLY :]
    d = d_ref[...]
    for i in range(EARLY):
        masked[i] = masked_in[i]
        scaled[i] = scaled_in[i]
    for i in range(EARLY, NH):
        m = rows[i - EARLY][...]
        masked[i] = m
        scaled[i] = scale(m, d)
    for c in range(HALF):
        out[2 * c, :BLK] = early[c]
        out[2 * c + 1, :BLK] = product(masked[left[HALF + c]], scaled[right[HALF + c]])
    for c in range(NCOL):
        out[c, BLK:] = riders[...]


def diag_kernel(ids, period, damping, d_ref, m_ref, out):
    m = m_ref[...]
    damp = jnp.where(ids[1] == 0, damping[period[0]], 0.0)
    i = lax.broadcasted_iota(jnp.int32, (BLK, BLK), 0)
    j = lax.broadcasted_iota(jnp.int32, (BLK, BLK), 1)
    out[...] = product(m, scale(m, d_ref[...])) + jnp.where(i == j, damp, 0.0)


def final_kernel(ids, even, odd, diag, out):
    row, col = ids[0], ids[1]
    own = row // 2 == col
    out[0:BLK] = jnp.where(own & (row % 2 == 0), diag[...], even[...])
    out[BLK : 2 * BLK] = jnp.where(own & (row % 2 == 1), diag[...], odd[...])


def body(constraint, pattern, scaling, period, column_period, damping):
    left, right, sends = plan()
    row, col = lax.axis_index(ROW), lax.axis_index(COL)
    vmem = pl.BlockSpec(memory_space=pltpu.VMEM)
    smem = pl.BlockSpec(memory_space=pltpu.SMEM)

    same = column_period[None, :] == period[:, None]
    before = column_period[None, :] == period[:, None] - 1
    present = jnp.where(same | before | (pattern > 0), 1, 0).astype(constraint.dtype)
    masked = constraint * jnp.repeat(present, BLK, axis=1)

    def move(x, dz, dy):
        pairs = [(place(z + dz, y + dy), place(z, y)) for z in range(NZ) for y in range(NY)]
        return lax.ppermute(x, ROW, pairs)

    held = [masked] + [move(masked, *at) for at in HELD[1:EARLY]]
    held.append(move(held[2], 1, 0))
    core = lax.axis_index("core")
    hops = [
        (place(z, y + 1 - 2 * k) * 2 + k, place(z, y) * 2 + k) for z in range(NZ) for y in range(NY) for k in range(2)
    ]
    held.append(lax.ppermute(jnp.where(core == 0, held[3], held[4]), ROW + ("core",), hops))
    held.append(move(held[1], -1, 0))

    small = pltpu.CompilerParams(vmem_limit_bytes=4 * 2**20)
    d = scaling.reshape(1, KC)
    ids = jnp.stack([row, col])
    diag = pl.pallas_call(
        diag_kernel,
        out_shape=jax.ShapeDtypeStruct((BLK, BLK), jnp.float32),
        in_specs=[smem] * 3 + [vmem] * 2,
        out_specs=vmem,
        compiler_params=small,
        name="diag",
    )(ids, period, damping, d, masked)
    strips = lax.all_to_all(diag, COL, 0, 0, tiled=True).reshape(NCOL, BLK // NCOL, BLK)
    strip = jnp.sum(strips, axis=0)
    high = lax.reduce_precision(strip, 5, 10)
    riders = jnp.concatenate([high, strip - high], axis=0)

    lt = lax.dynamic_index_in_dim(jnp.asarray(left), row, 0, keepdims=False)
    rt = lax.dynamic_index_in_dim(jnp.asarray(right), row, 0, keepdims=False)
    stack = jax.ShapeDtypeStruct((EARLY, BLK, KC), jnp.bfloat16)
    sums = jax.ShapeDtypeStruct((HALF, BLK, BLK), jnp.float32)
    params = pltpu.CompilerParams(vmem_limit_bytes=20 * 2**20)
    early, masked_rows, scaled_rows = pl.pallas_call(
        early_kernel,
        out_shape=(sums, stack, stack),
        in_specs=[smem] * 2 + [vmem] * (1 + EARLY),
        out_specs=(vmem,) * 3,
        compiler_params=params,
        name="early",
    )(lt, rt, d, *held[:EARLY])
    parts = pl.pallas_call(
        late_kernel,
        out_shape=jax.ShapeDtypeStruct((NCOL, BLK + 2 * BLK // NCOL, BLK), jnp.float32),
        in_specs=[smem] * 2 + [vmem] * (5 + NH - EARLY),
        out_specs=vmem,
        scratch_shapes=[pltpu.VMEM((NH, BLK, KC), jnp.bfloat16)] * 2,
        compiler_params=params,
        name="late",
    )(lt, rt, d, masked_rows, scaled_rows, early, riders, *held[EARLY:])
    parts = parts.astype(jnp.float16)
    parts = lax.all_to_all(parts, COL, 0, 0, tiled=True).astype(jnp.float32)
    mine = jnp.sum(parts[:, :BLK], axis=0)
    step = BLK // NCOL
    diag = (parts[:, BLK : BLK + step] + parts[:, BLK + step :]).reshape(BLK, BLK)
    even = lax.ppermute(mine, ROW + COL, sends[0])
    odd = lax.ppermute(mine, ROW + COL, sends[1])
    return pl.pallas_call(
        final_kernel,
        out_shape=jax.ShapeDtypeStruct((2 * BLK, BLK), jnp.float32),
        in_specs=[smem] + [vmem] * 3,
        out_specs=vmem,
        compiler_params=small,
        name="final",
    )(ids, even, odd, diag)


def solution(mesh):
    split = Mesh(mesh.devices.reshape(NZ, NY, NX, NL, NK), ROW + COL)
    return jax.shard_map(
        body,
        mesh=split,
        in_specs=(P(ROW, COL), P(ROW, COL), P(COL), P(ROW), P(COL), P()),
        out_specs=P(COL, ROW),
        check_vma=False,
    )
```

time: 101 us -> 94.7 us (0.938)
  the two profiles are of different devices: /device:TPU:6 before, /device:TPU:9 now
where the time goes in v3:
time: 94.7 us; the launch traced here: 94.1 us
  starting transfers between devices  50.8 us (54%)
  blocking collectives  17 us (18%)
  waiting for transfers between devices  13.4 us (14%)
  Pallas kernels  7.09 us (7%)
  other arithmetic  2.82 us (3%)
  local copies, waits for them, and re-layouts  2.15 us (2%)
    ppermute x6, starting transfers between devices, move(): return lax.ppermute(x, ROW, pairs)  31.8 us
    all_to_all x1, blocking collectives, body(): parts = lax.all_to_all(parts, COL, 0, 0, tiled=True).astype(jnp.float32)  17 us
    ppermute x1, waiting for transfers between devices, body(): odd = lax.ppermute(mine, ROW + COL, sends[1])  7.01 us
    all_to_all x1, starting transfers between devices, body(): lax.all_to_all(diag, COL, 0, 0, tiled=True).reshape(NCOL, BLK // NCOL, BLK)  6.65 us
    ppermute x1, starting transfers between devices, body(): even = lax.ppermute(mine, ROW + COL, sends[0])  6.11 us
    ppermute x1, starting transfers between devices, body(): lax.ppermute(jnp.where(core == 0, held[3], held[4]), ROW + ('core',), hops)  4.97 us
    ppermute x6, waiting for transfers between devices, move(): return lax.ppermute(x, ROW, pairs)  4.93 us
    pallas_call x1, Pallas kernels, body(): pl.pallas_call(early_kernel, out_shape=(sums, stack, stack), in_specs=[sm...  2.26 us
  transfers between devices with their start and end apart: 10, of which 3 were waited for; matrix products, arithmetic and copies ran while one was open for 2% of the time, Pallas kernels for 4%

profile of v3, /device:TPU:9, one launch (start us, length us, event | category | flops | bytes accessed | tf_op | source)
XLA Modules:
  0.0 94.1 jit_solution(13500119384722701218)
XLA Ops:
  0.7 0.7 convert_bitcast_fusion
  1.4 1.0 %broadcast_multiply_fusion.refs_0_.m_ref = bf16[128,1536]{1,0:T(8,128)(2,1)S(1)} fusion(bf16[128,1536]{1,0:T(8,128)(2,1)} %param.8, bf16[1536]{0:T(1024)(128)(2,1)S(1)} %broadcast_bitcast_fusion), kind=kLoop, calls=%fused_computation.2 | loop fusion | flops 196608 | bytes 789504 | tf_op jit(solution)/shard_map/mul | solution.py:136
  2.4 5.0 %collective-permute-start.2 = (bf16[128,1536]{1,0:T(8,128)(2,1)S(1)}, bf16[128,1536]{1,0:T(8,128)(2,1)S(1)}, u32[]{:S(2)}, u32[]{:S(2)}) collective-permute-start(bf16[128,1536]{1,0:T(8,128)(2,1)S(1)} %broadcast_multiply_fusion.refs_0_.m_ref), channel_id=1, source_target_pairs={{16,0},{32,16},{48,32},{0,48},{80,64},{96,80},{112,96},{64,112},{1... | collective-permute-start | bytes 1179656 | tf_op jit(solution)/shard_map/ppermute | solution.py:140
  7.4 1.9 %collective-permute-start.3 = (bf16[128,1536]{1,0:T(8,128)(2,1)S(1)}, bf16[128,1536]{1,0:T(8,128)(2,1)S(1)}, u32[]{:S(2)}, u32[]{:S(2)}) collective-permute-start(bf16[128,1536]{1,0:T(8,128)(2,1)S(1)} %broadcast_multiply_fusion.refs_0_.m_ref), channel_id=1, source_target_pairs={{48,0},{0,16},{16,32},{32,48},{112,64},{64,80},{80,96},{96,112},{1... | collective-permute-start | bytes 1179656 | tf_op jit(solution)/shard_map/ppermute | solution.py:140
  9.4 7.6 %collective-permute-start = (bf16[128,1536]{1,0:T(8,128)(2,1)S(1)}, bf16[128,1536]{1,0:T(8,128)(2,1)S(1)}, u32[]{:S(2)}, u32[]{:S(2)}) collective-permute-start(bf16[128,1536]{1,0:T(8,128)(2,1)S(1)} %broadcast_multiply_fusion.refs_0_.m_ref), channel_id=1, source_target_pairs={{320,0},{336,16},{352,32},{368,48},{384,64},{400,80},{416,96},{432... | collective-permute-start | bytes 1179656 | tf_op jit(solution)/shard_map/ppermute | solution.py:140
  17.0 5.0 %collective-permute-start.1 = (bf16[128,1536]{1,0:T(8,128)(2,1)S(1)}, bf16[128,1536]{1,0:T(8,128)(2,1)S(1)}, u32[]{:S(2)}, u32[]{:S(2)}) collective-permute-start(bf16[128,1536]{1,0:T(8,128)(2,1)S(1)} %broadcast_multiply_fusion.refs_0_.m_ref), channel_id=1, source_target_pairs={{64,0},{80,16},{96,32},{112,48},{128,64},{144,80},{160,96},{176,11... | collective-permute-start | bytes 1179656 | tf_op jit(solution)/shard_map/ppermute | solution.py:140
  22.0 0.7 reshape.26.d_ref
  22.8 0.7 copy-done
  23.4 1.4 %diag.1 = f32[128,128]{1,0:T(8,128)} custom-call(s32[2]{0:T(128)S(1)} %pad_add_fusion.ids, s32[1]{0:T(128)} %copy.9.period, f32[16]{0:T(128)S(1)} %copy-done, f32[1,1536]{1,0:T(1,128)S(1)} %reshape.26.d_ref, bf16[128,1536]{1,0:T(8,128)(2,1)S(1)} %broadcast_multiply_fusion.refs_0_.m_ref), custom_call_target="tpu_custom_call" | custom-call | tf_op jit(solution)/shard_map/diag/pallas_call | solution.py:154
  24.9 6.6 %all-to-all-start = ((f32[16,8,128]{2,1,0:T(8,128)}), f32[16,8,128]{2,1,0:T(8,128)S(1)}, u32[]{:S(2)}, u32[]{:S(2)}) async-start(f32[16,8,128]{2,1,0:T(8,128)} %bitcast.9), calls=%async_computation | async-start | bytes 131072 | tf_op jit(solution)/shard_map/all_to_all | solution.py:162
  31.5 0.8 broadcast_select_fusion
  32.3 5.0 %collective-permute-start.5 = (bf16[128,1536]{1,0:T(8,128)(2,1)}, bf16[128,1536]{1,0:T(8,128)(2,1)S(1)}, u32[]{:S(2)}, u32[]{:S(2)}) collective-permute-start(bf16[128,1536]{1,0:T(8,128)(2,1)} %broadcast_select_fusion), channel_id=1, source_target_pairs={{16,0},{49,1},{32,16},{1,17},{48,32},{17,33},{0,48},{33,49},{80,64... | collective-permute-start | bytes 1179656 | tf_op jit(solution)/shard_map/ppermute | solution.py:148
  37.3 5.7 %collective-permute-start.4 = (bf16[128,1536]{1,0:T(8,128)(2,1)S(1)}, bf16[128,1536]{1,0:T(8,128)(2,1)S(1)}, u32[]{:S(2)}, u32[]{:S(2)}) collective-permute-start(bf16[128,1536]{1,0:T(8,128)(2,1)S(1)} %collective-permute-done.1.refs_2_), channel_id=1, source_target_pairs={{64,0},{80,16},{96,32},{112,48},{128,64},{144,80},{160,96},{176,11... | collective-permute-start | bytes 1179656 | tf_op jit(solution)/shard_map/ppermute | solution.py:140
  43.0 6.6 %collective-permute-start.6 = (bf16[128,1536]{1,0:T(8,128)(2,1)S(1)}, bf16[128,1536]{1,0:T(8,128)(2,1)S(1)}, u32[]{:S(2)}, u32[]{:S(2)}) collective-permute-start(bf16[128,1536]{1,0:T(8,128)(2,1)S(1)} %collective-permute-done.refs_1_), channel_id=1, source_target_pairs={{448,0},{464,16},{480,32},{496,48},{0,64},{16,80},{32,96},{48,112}... | collective-permute-start | bytes 1179656 | tf_op jit(solution)/shard_map/ppermute | solution.py:140
  49.6 0.7 dynamic-slice_bitcast_fusion
  50.4 2.3 %early.1 = (f32[8,128,128]{2,1,0:T(8,128)S(1)}, bf16[5,128,1536]{2,1,0:T(8,128)(2,1)S(1)}, bf16[5,128,1536]{2,1,0:T(8,128)(2,1)S(1)}) custom-call(s32[16]{0:T(128)S(1)} %get-tuple-element.14.left, s32[16]{0:T(128)S(1)} %get-tuple-element.13.right, f32[1,1536]{1,0:T(1,128)S(1)} %reshape.26.d_ref, bf16[128,1536]{1,0:T(8,128)(2,1)S(1)} %broadcast_multiply_fusion.refs_0_.m_ref, ...), custom_call_target="tpu_custom_call" | custom-call | tf_op jit(solution)/shard_map/early/pallas_call | solution.py:172
  52.6 4.9 %collective-permute-done.6.refs_2_ = bf16[128,1536]{1,0:T(8,128)(2,1)S(1)} collective-permute-done((bf16[128,1536]{1,0:T(8,128)(2,1)S(1)}, bf16[128,1536]{1,0:T(8,128)(2,1)S(1)}, u32[]{:S(2)}, u32[]{:S(2)}) %collective-permute-start.6) | collective-permute-done | bytes 393248 | tf_op jit(solution)/shard_map/ppermute | solution.py:140
  57.6 2.2 %late.1 = f32[16,144,128]{2,1,0:T(8,128)S(1)} custom-call(s32[16]{0:T(128)S(1)} %get-tuple-element.14.left, s32[16]{0:T(128)S(1)} %get-tuple-element.13.right, f32[1,1536]{1,0:T(1,128)S(1)} %reshape.26.d_ref, bf16[5,128,1536]{2,1,0:T(8,128)(2,1)S(1)} %get-tuple-element.8.masked_in, bf16[5,128,1536]{2,1,0:T(8,128)(2,1)S(1)} %get-tuple-element.9.scaled_in, ...), custom_call_target="tpu_custom_call" | custom-call | tf_op jit(solution)/shard_map/late/pallas_call | solution.py:180
  59.8 17.0 %all_to_all.14 = f16[16,144,128]{2,1,0:T(8,128)(2,1)S(1)} all-to-all(f16[16,144,128]{2,1,0:T(8,128)(2,1)S(1)} %convert_element_type.13), channel_id=1, replica_groups=mesh['z'=8,'yh'=4,'x'=4,'yl'=2,'core'=2] {'x','yl','core'}, dimensions={0} | all-to-all | bytes 1179648 | tf_op jit(solution)/shard_map/all_to_all | solution.py:190
  76.9 6.1 %collective-permute-start.7 = (f32[128,128]{1,0:T(8,128)S(1)}, f32[128,128]{1,0:T(8,128)S(1)}, u32[]{:S(2)}, u32[]{:S(2)}) collective-permute-start(f32[128,128]{1,0:T(8,128)S(1)} %slice_reduce_fusion), channel_id=1, source_target_pairs={{10,10},{2,2},{6,74},{8,26},{14,18},{4,58},{12,50},{5,4},{7,20},{1... | collective-permute-start | bytes 196616 | tf_op jit(solution)/shard_map/ppermute | solution.py:194
  83.1 1.3 %collective-permute-start.8 = (f32[128,128]{1,0:T(8,128)S(1)}, f32[128,128]{1,0:T(8,128)S(1)}, u32[]{:S(2)}, u32[]{:S(2)}) collective-permute-start(f32[128,128]{1,0:T(8,128)S(1)} %slice_reduce_fusion), channel_id=1, source_target_pairs={{0,0},{1,17},{26,26},{18,18},{22,90},{24,42},{30,34},{20,10},{28,2... | collective-permute-start | bytes 196616 | tf_op jit(solution)/shard_map/ppermute | solution.py:195
  84.4 1.5 %collective-permute-done.7.even = f32[128,128]{1,0:T(8,128)S(1)} collective-permute-done((f32[128,128]{1,0:T(8,128)S(1)}, f32[128,128]{1,0:T(8,128)S(1)}, u32[]{:S(2)}, u32[]{:S(2)}) %collective-permute-start.7) | collective-permute-done | bytes 65568 | tf_op jit(solution)/shard_map/ppermute | solution.py:194
  85.9 7.0 %collective-permute-done.8.odd = f32[128,128]{1,0:T(8,128)S(1)} collective-permute-done((f32[128,128]{1,0:T(8,128)S(1)}, f32[128,128]{1,0:T(8,128)S(1)}, u32[]{:S(2)}, u32[]{:S(2)}) %collective-permute-start.8) | collective-permute-done | bytes 65568 | tf_op jit(solution)/shard_map/ppermute | solution.py:195
  92.9 1.2 %final.1 = f32[256,128]{1,0:T(8,128)} custom-call(s32[2]{0:T(128)S(1)} %pad_add_fusion.ids, f32[128,128]{1,0:T(8,128)S(1)} %collective-permute-done.7.even, f32[128,128]{1,0:T(8,128)S(1)} %collective-permute-done.8.odd, f32[128,128]{1,0:T(8,128)S(1)} %fusion.diag), custom_call_target="tpu_custom_call" | custom-call | tf_op jit(solution)/shard_map/final/pallas_call | solution.py:196
  (17 shorter events, 0.4 us)
Async XLA Ops:
  2.4 29.1 %collective-permute-start.2 = (bf16[128,1536]{1,0:T(8,128)(2,1)S(1)}, bf16[128,1536]{1,0:T(8,128)(2,1)S(1)}, u32[]{:S(2)}, u32[]{:S(2)}) collective-permute-start(bf16[128,1536]{1,0:T(8,128)(2,1)S(1)} %broadcast_multiply_fusion.refs_0_.m_ref), channel_id=1, source_target_pairs={{16,0},{32,16},{48,32},{0,48},{80,64},{96,80},{112,96},{64,112},{1... | collective-permute-start | bytes 1179656 | tf_op jit(solution)/shard_map/ppermute | solution.py:140
  7.4 24.1 %collective-permute-start.3 = (bf16[128,1536]{1,0:T(8,128)(2,1)S(1)}, bf16[128,1536]{1,0:T(8,128)(2,1)S(1)}, u32[]{:S(2)}, u32[]{:S(2)}) collective-permute-start(bf16[128,1536]{1,0:T(8,128)(2,1)S(1)} %broadcast_multiply_fusion.refs_0_.m_ref), channel_id=1, source_target_pairs={{48,0},{0,16},{16,32},{32,48},{112,64},{64,80},{80,96},{96,112},{1... | collective-permute-start | bytes 1179656 | tf_op jit(solution)/shard_map/ppermute | solution.py:140
  9.4 33.6 %collective-permute-start = (bf16[128,1536]{1,0:T(8,128)(2,1)S(1)}, bf16[128,1536]{1,0:T(8,128)(2,1)S(1)}, u32[]{:S(2)}, u32[]{:S(2)}) collective-permute-start(bf16[128,1536]{1,0:T(8,128)(2,1)S(1)} %broadcast_multiply_fusion.refs_0_.m_ref), channel_id=1, source_target_pairs={{320,0},{336,16},{352,32},{368,48},{384,64},{400,80},{416,96},{432... | collective-permute-start | bytes 1179656 | tf_op jit(solution)/shard_map/ppermute | solution.py:140
  17.0 20.3 %collective-permute-start.1 = (bf16[128,1536]{1,0:T(8,128)(2,1)S(1)}, bf16[128,1536]{1,0:T(8,128)(2,1)S(1)}, u32[]{:S(2)}, u32[]{:S(2)}) collective-permute-start(bf16[128,1536]{1,0:T(8,128)(2,1)S(1)} %broadcast_multiply_fusion.refs_0_.m_ref), channel_id=1, source_target_pairs={{64,0},{80,16},{96,32},{112,48},{128,64},{144,80},{160,96},{176,11... | collective-permute-start | bytes 1179656 | tf_op jit(solution)/shard_map/ppermute | solution.py:140
  22.7 0.7 copy-start
  24.9 25.5 %all-to-all-start = ((f32[16,8,128]{2,1,0:T(8,128)}), f32[16,8,128]{2,1,0:T(8,128)S(1)}, u32[]{:S(2)}, u32[]{:S(2)}) async-start(f32[16,8,128]{2,1,0:T(8,128)} %bitcast.9), calls=%async_computation | async-start | bytes 131072 | tf_op jit(solution)/shard_map/all_to_all | solution.py:162
  32.3 20.3 %collective-permute-start.5 = (bf16[128,1536]{1,0:T(8,128)(2,1)}, bf16[128,1536]{1,0:T(8,128)(2,1)S(1)}, u32[]{:S(2)}, u32[]{:S(2)}) collective-permute-start(bf16[128,1536]{1,0:T(8,128)(2,1)} %broadcast_select_fusion), channel_id=1, source_target_pairs={{16,0},{49,1},{32,16},{1,17},{48,32},{17,33},{0,48},{33,49},{80,64... | collective-permute-start | bytes 1179656 | tf_op jit(solution)/shard_map/ppermute | solution.py:148
  37.3 15.4 %collective-permute-start.4 = (bf16[128,1536]{1,0:T(8,128)(2,1)S(1)}, bf16[128,1536]{1,0:T(8,128)(2,1)S(1)}, u32[]{:S(2)}, u32[]{:S(2)}) collective-permute-start(bf16[128,1536]{1,0:T(8,128)(2,1)S(1)} %collective-permute-done.1.refs_2_), channel_id=1, source_target_pairs={{64,0},{80,16},{96,32},{112,48},{128,64},{144,80},{160,96},{176,11... | collective-permute-start | bytes 1179656 | tf_op jit(solution)/shard_map/ppermute | solution.py:140
  43.0 14.6 %collective-permute-start.6 = (bf16[128,1536]{1,0:T(8,128)(2,1)S(1)}, bf16[128,1536]{1,0:T(8,128)(2,1)S(1)}, u32[]{:S(2)}, u32[]{:S(2)}) collective-permute-start(bf16[128,1536]{1,0:T(8,128)(2,1)S(1)} %collective-permute-done.refs_1_), channel_id=1, source_target_pairs={{448,0},{464,16},{480,32},{496,48},{0,64},{16,80},{32,96},{48,112}... | collective-permute-start | bytes 1179656 | tf_op jit(solution)/shard_map/ppermute | solution.py:140
  76.9 8.9 %collective-permute-start.7 = (f32[128,128]{1,0:T(8,128)S(1)}, f32[128,128]{1,0:T(8,128)S(1)}, u32[]{:S(2)}, u32[]{:S(2)}) collective-permute-start(f32[128,128]{1,0:T(8,128)S(1)} %slice_reduce_fusion), channel_id=1, source_target_pairs={{10,10},{2,2},{6,74},{8,26},{14,18},{4,58},{12,50},{5,4},{7,20},{1... | collective-permute-start | bytes 196616 | tf_op jit(solution)/shard_map/ppermute | solution.py:194
  83.1 9.8 %collective-permute-start.8 = (f32[128,128]{1,0:T(8,128)S(1)}, f32[128,128]{1,0:T(8,128)S(1)}, u32[]{:S(2)}, u32[]{:S(2)}) collective-permute-start(f32[128,128]{1,0:T(8,128)S(1)} %slice_reduce_fusion), channel_id=1, source_target_pairs={{0,0},{1,17},{26,26},{18,18},{22,90},{24,42},{30,34},{20,10},{28,2... | collective-permute-start | bytes 196616 | tf_op jit(solution)/shard_map/ppermute | solution.py:195

commit v4 on v3

--- a/solution.py
+++ b/solution.py
@@ -13,7 +13,7 @@
 BLK = 128
 KC = 1536
 
-HELD = ((0, 0), (5, 0), (1, 0), (0, 1), (0, 3), (2, 0), (0, 2), (4, 0))
+HELD = ((0, 0), (6, 0), (1, 0), (0, 1), (0, 3), (3, 0), (0, 2), (4, 0))
 NH = len(HELD)
 EARLY = 5
 HALF = NCOL // 2
@@ -44,16 +44,14 @@
     for z in range(NZ):
         for y in range(NY):
             g = place(z, y)
-            early, late, either = [], [], []
+            early, late = [], []
             for (dz, dy), (s, t) in chosen.items():
                 if (dz, dy) == (4, 0) and z >= 4 or (dz, dy) == (4, 2) and z < 4 or (dz, dy) == (0, 2) and y >= 2:
                     continue
                 a = place(z + HELD[s][0], y + HELD[s][1])
                 b = place(z + HELD[t][0], y + HELD[t][1])
                 pair = (a, b, s, t) if a > b else (b, a, t, s)
-                (either if (dz, dy) == (0, 2) else early if t < EARLY else late).append(pair)
-            for pair in either:
-                (early if len(early) < HALF else late).append(pair)
+                (early if t < EARLY and (dz, dy) != (0, 2) else late).append(pair)
             assert len(early) <= HALF and len(late) <= HALF
             for base, todo in ((0, early), (1, late)):
                 cand = sorted(
@@ -140,13 +138,13 @@
         return lax.ppermute(x, ROW, pairs)
 
     held = [masked] + [move(masked, *at) for at in HELD[1:EARLY]]
-    held.append(move(held[2], 1, 0))
+    held.append(move(held[2], 2, 0))
     core = lax.axis_index("core")
     hops = [
         (place(z, y + 1 - 2 * k) * 2 + k, place(z, y) * 2 + k) for z in range(NZ) for y in range(NY) for k in range(2)
     ]
     held.append(lax.ppermute(jnp.where(core == 0, held[3], held[4]), ROW + ("core",), hops))
-    held.append(move(held[1], -1, 0))
+    held.append(move(jnp.where(core < 2, held[1], held[4]), -2, 0))
 
     small = pltpu.CompilerParams(vmem_limit_bytes=4 * 2**20)
     d = scaling.reshape(1, KC)

time: 94.7 us -> 104 us (1.098)
  the two profiles are of different devices: /device:TPU:9 before, /device:TPU:12 now
where the time goes in v4:
time: 104 us; the launch traced here: 103 us
  starting transfers between devices  46.7 us (45%)
  waiting for transfers between devices  29.7 us (29%)
  blocking collectives  14 us (13%)
  Pallas kernels  7.09 us (7%)
  other arithmetic  2.99 us (3%)
  local copies, waits for them, and re-layouts  2.15 us (2%)
    ppermute x6, starting transfers between devices, move(): return lax.ppermute(x, ROW, pairs)  29.2 us
    ppermute x6, waiting for transfers between devices, move(): return lax.ppermute(x, ROW, pairs)  20.1 us
    all_to_all x1, blocking collectives, body(): parts = lax.all_to_all(parts, COL, 0, 0, tiled=True).astype(jnp.float32)  14 us
    ppermute x1, waiting for transfers between devices, body(): odd = lax.ppermute(mine, ROW + COL, sends[1])  9.06 us
    ppermute x1, starting transfers between devices, body(): even = lax.ppermute(mine, ROW + COL, sends[0])  7.67 us
    all_to_all x1, starting transfers between devices, body(): lax.all_to_all(diag, COL, 0, 0, tiled=True).reshape(NCOL, BLK // NCOL, BLK)  5.72 us
    ppermute x1, starting transfers between devices, body(): lax.ppermute(jnp.where(core == 0, held[3], held[4]), ROW + ('core',), hops)  2.81 us
    pallas_call x1, Pallas kernels, body(): pl.pallas_call(early_kernel, out_shape=(sums, stack, stack), in_specs=[sm...  2.26 us
  transfers between devices with their start and end apart: 10, of which 5 were waited for; matrix products, arithmetic and copies ran while one was open for 2% of the time, Pallas kernels for 4%

profile of v4, /device:TPU:12, one launch (start us, length us, event | category | flops | bytes accessed | tf_op | source)
XLA Modules:
  0.0 103.5 jit_solution(25391422174489651)
XLA Ops:
  0.7 0.7 convert_bitcast_fusion
  1.4 1.0 broadcast_multiply_fusion.refs_0_.m_ref
  2.4 6.1 %collective-permute-start = (bf16[128,1536]{1,0:T(8,128)(2,1)S(1)}, bf16[128,1536]{1,0:T(8,128)(2,1)S(1)}, u32[]{:S(2)}, u32[]{:S(2)}) collective-permute-start(bf16[128,1536]{1,0:T(8,128)(2,1)S(1)} %broadcast_multiply_fusion.refs_0_.m_ref), channel_id=1, source_target_pairs={{384,0},{400,16},{416,32},{432,48},{448,64},{464,80},{480,96},{496... | collective-permute-start | bytes 1179656 | tf_op jit(solution)/shard_map/ppermute | solution.py:138
  8.5 5.3 %collective-permute-start.2 = (bf16[128,1536]{1,0:T(8,128)(2,1)S(1)}, bf16[128,1536]{1,0:T(8,128)(2,1)S(1)}, u32[]{:S(2)}, u32[]{:S(2)}) collective-permute-start(bf16[128,1536]{1,0:T(8,128)(2,1)S(1)} %broadcast_multiply_fusion.refs_0_.m_ref), channel_id=1, source_target_pairs={{16,0},{32,16},{48,32},{0,48},{80,64},{96,80},{112,96},{64,112},{1... | collective-permute-start | bytes 1179656 | tf_op jit(solution)/shard_map/ppermute | solution.py:138
  13.8 1.9 %collective-permute-start.3 = (bf16[128,1536]{1,0:T(8,128)(2,1)S(1)}, bf16[128,1536]{1,0:T(8,128)(2,1)S(1)}, u32[]{:S(2)}, u32[]{:S(2)}) collective-permute-start(bf16[128,1536]{1,0:T(8,128)(2,1)S(1)} %broadcast_multiply_fusion.refs_0_.m_ref), channel_id=1, source_target_pairs={{48,0},{0,16},{16,32},{32,48},{112,64},{64,80},{80,96},{96,112},{1... | collective-permute-start | bytes 1179656 | tf_op jit(solution)/shard_map/ppermute | solution.py:138
  15.7 6.8 %collective-permute-start.1 = (bf16[128,1536]{1,0:T(8,128)(2,1)S(1)}, bf16[128,1536]{1,0:T(8,128)(2,1)S(1)}, u32[]{:S(2)}, u32[]{:S(2)}) collective-permute-start(bf16[128,1536]{1,0:T(8,128)(2,1)S(1)} %broadcast_multiply_fusion.refs_0_.m_ref), channel_id=1, source_target_pairs={{64,0},{80,16},{96,32},{112,48},{128,64},{144,80},{160,96},{176,11... | collective-permute-start | bytes 1179656 | tf_op jit(solution)/shard_map/ppermute | solution.py:138
  22.5 0.7 reshape.26.d_ref
  24.0 1.4 %diag.1 = f32[128,128]{1,0:T(8,128)} custom-call(s32[2]{0:T(128)S(1)} %pad_add_fusion.ids, s32[1]{0:T(128)} %copy.9.period, f32[16]{0:T(128)S(1)} %copy-done, f32[1,1536]{1,0:T(1,128)S(1)} %reshape.26.d_ref, bf16[128,1536]{1,0:T(8,128)(2,1)S(1)} %broadcast_multiply_fusion.refs_0_.m_ref), custom_call_target="tpu_custom_call" | custom-call | tf_op jit(solution)/shard_map/diag/pallas_call | solution.py:152
  25.4 5.7 %all-to-all-start = ((f32[16,8,128]{2,1,0:T(8,128)}), f32[16,8,128]{2,1,0:T(8,128)S(1)}, u32[]{:S(2)}, u32[]{:S(2)}) async-start(f32[16,8,128]{2,1,0:T(8,128)} %bitcast.9), calls=%async_computation | async-start | bytes 131072 | tf_op jit(solution)/shard_map/all_to_all | solution.py:160
  31.1 5.5 %collective-permute-done.3.refs_4_ = bf16[128,1536]{1,0:T(8,128)(2,1)S(1)} collective-permute-done((bf16[128,1536]{1,0:T(8,128)(2,1)S(1)}, bf16[128,1536]{1,0:T(8,128)(2,1)S(1)}, u32[]{:S(2)}, u32[]{:S(2)}) %collective-permute-start.3) | collective-permute-done | bytes 393248 | tf_op jit(solution)/shard_map/ppermute | solution.py:138
  36.6 0.9 broadcast_select_fusion
  37.6 2.8 %collective-permute-start.5 = (bf16[128,1536]{1,0:T(8,128)(2,1)}, bf16[128,1536]{1,0:T(8,128)(2,1)S(1)}, u32[]{:S(2)}, u32[]{:S(2)}) collective-permute-start(bf16[128,1536]{1,0:T(8,128)(2,1)} %get-tuple-element.12), channel_id=1, source_target_pairs={{16,0},{49,1},{32,16},{1,17},{48,32},{17,33},{0,48},{33,49},{80,64... | collective-permute-start | bytes 1179656 | tf_op jit(solution)/shard_map/ppermute | solution.py:146
  40.4 7.2 %collective-permute-start.6 = (bf16[128,1536]{1,0:T(8,128)(2,1)}, bf16[128,1536]{1,0:T(8,128)(2,1)S(1)}, u32[]{:S(2)}, u32[]{:S(2)}) collective-permute-start(bf16[128,1536]{1,0:T(8,128)(2,1)} %get-tuple-element.11), channel_id=1, source_target_pairs={{384,0},{400,16},{416,32},{432,48},{448,64},{464,80},{480,96},{496... | collective-permute-start | bytes 1179656 | tf_op jit(solution)/shard_map/ppermute | solution.py:138
  47.6 1.9 %collective-permute-start.4 = (bf16[128,1536]{1,0:T(8,128)(2,1)S(1)}, bf16[128,1536]{1,0:T(8,128)(2,1)S(1)}, u32[]{:S(2)}, u32[]{:S(2)}) collective-permute-start(bf16[128,1536]{1,0:T(8,128)(2,1)S(1)} %collective-permute-done.1.refs_2_), channel_id=1, source_target_pairs={{128,0},{144,16},{160,32},{176,48},{192,64},{208,80},{224,96},{240... | collective-permute-start | bytes 1179656 | tf_op jit(solution)/shard_map/ppermute | solution.py:138
  49.5 0.7 dynamic-slice_bitcast_fusion
  50.3 2.3 %early.1 = (f32[8,128,128]{2,1,0:T(8,128)S(1)}, bf16[5,128,1536]{2,1,0:T(8,128)(2,1)S(1)}, bf16[5,128,1536]{2,1,0:T(8,128)(2,1)S(1)}) custom-call(s32[16]{0:T(128)S(1)} %get-tuple-element.16.left, s32[16]{0:T(128)S(1)} %get-tuple-element.15.right, f32[1,1536]{1,0:T(1,128)S(1)} %reshape.26.d_ref, bf16[128,1536]{1,0:T(8,128)(2,1)S(1)} %broadcast_multiply_fusion.refs_0_.m_ref, ...), custom_call_target="tpu_custom_call" | custom-call | tf_op jit(solution)/shard_map/early/pallas_call | solution.py:170
  52.6 2.7 %collective-permute-done.6.refs_2_ = bf16[128,1536]{1,0:T(8,128)(2,1)S(1)} collective-permute-done((bf16[128,1536]{1,0:T(8,128)(2,1)}, bf16[128,1536]{1,0:T(8,128)(2,1)S(1)}, u32[]{:S(2)}, u32[]{:S(2)}) %collective-permute-start.6) | collective-permute-done | bytes 393248 | tf_op jit(solution)/shard_map/ppermute | solution.py:138
  55.3 11.9 %collective-permute-done.4.refs_0_ = bf16[128,1536]{1,0:T(8,128)(2,1)S(1)} collective-permute-done((bf16[128,1536]{1,0:T(8,128)(2,1)S(1)}, bf16[128,1536]{1,0:T(8,128)(2,1)S(1)}, u32[]{:S(2)}, u32[]{:S(2)}) %collective-permute-start.4) | collective-permute-done | bytes 393248 | tf_op jit(solution)/shard_map/ppermute | solution.py:138
  67.2 2.2 %late.1 = f32[16,144,128]{2,1,0:T(8,128)S(1)} custom-call(s32[16]{0:T(128)S(1)} %get-tuple-element.16.left, s32[16]{0:T(128)S(1)} %get-tuple-element.15.right, f32[1,1536]{1,0:T(1,128)S(1)} %reshape.26.d_ref, bf16[5,128,1536]{2,1,0:T(8,128)(2,1)S(1)} %get-tuple-element.8.masked_in, bf16[5,128,1536]{2,1,0:T(8,128)(2,1)S(1)} %get-tuple-element.9.scaled_in, ...), custom_call_target="tpu_custom_call" | custom-call | tf_op jit(solution)/shard_map/late/pallas_call | solution.py:178
  69.4 14.0 %all_to_all.14 = f16[16,144,128]{2,1,0:T(8,128)(2,1)S(1)} all-to-all(f16[16,144,128]{2,1,0:T(8,128)(2,1)S(1)} %convert_element_type.13), channel_id=1, replica_groups=mesh['z'=8,'yh'=4,'x'=4,'yl'=2,'core'=2] {'x','yl','core'}, dimensions={0} | all-to-all | bytes 1179648 | tf_op jit(solution)/shard_map/all_to_all | solution.py:188
  83.6 7.7 %collective-permute-start.7 = (f32[128,128]{1,0:T(8,128)S(1)}, f32[128,128]{1,0:T(8,128)S(1)}, u32[]{:S(2)}, u32[]{:S(2)}) collective-permute-start(f32[128,128]{1,0:T(8,128)S(1)} %slice_reduce_fusion), channel_id=1, source_target_pairs={{12,12},{2,2},{8,76},{14,28},{6,18},{4,60},{10,50},{7,22},{5,54},{... | collective-permute-start | bytes 196616 | tf_op jit(solution)/shard_map/ppermute | solution.py:192
  91.3 1.3 %collective-permute-start.8 = (f32[128,128]{1,0:T(8,128)S(1)}, f32[128,128]{1,0:T(8,128)S(1)}, u32[]{:S(2)}, u32[]{:S(2)}) collective-permute-start(f32[128,128]{1,0:T(8,128)S(1)} %slice_reduce_fusion), channel_id=1, source_target_pairs={{0,0},{1,17},{28,28},{18,18},{24,92},{30,44},{22,34},{20,12},{26,2... | collective-permute-start | bytes 196616 | tf_op jit(solution)/shard_map/ppermute | solution.py:193
  93.2 9.1 %collective-permute-done.8.odd = f32[128,128]{1,0:T(8,128)S(1)} collective-permute-done((f32[128,128]{1,0:T(8,128)S(1)}, f32[128,128]{1,0:T(8,128)S(1)}, u32[]{:S(2)}, u32[]{:S(2)}) %collective-permute-start.8) | collective-permute-done | bytes 65568 | tf_op jit(solution)/shard_map/ppermute | solution.py:193
  102.3 1.2 %final.1 = f32[256,128]{1,0:T(8,128)} custom-call(s32[2]{0:T(128)S(1)} %pad_add_fusion.ids, f32[128,128]{1,0:T(8,128)S(1)} %collective-permute-done.7.even, f32[128,128]{1,0:T(8,128)S(1)} %collective-permute-done.8.odd, f32[128,128]{1,0:T(8,128)S(1)} %fusion.diag), custom_call_target="tpu_custom_call" | custom-call | tf_op jit(solution)/shard_map/final/pallas_call | solution.py:194
  (17 shorter events, 1.6 us)
Async XLA Ops:
  2.4 28.7 %collective-permute-start = (bf16[128,1536]{1,0:T(8,128)(2,1)S(1)}, bf16[128,1536]{1,0:T(8,128)(2,1)S(1)}, u32[]{:S(2)}, u32[]{:S(2)}) collective-permute-start(bf16[128,1536]{1,0:T(8,128)(2,1)S(1)} %broadcast_multiply_fusion.refs_0_.m_ref), channel_id=1, source_target_pairs={{384,0},{400,16},{416,32},{432,48},{448,64},{464,80},{480,96},{496... | collective-permute-start | bytes 1179656 | tf_op jit(solution)/shard_map/ppermute | solution.py:138
  8.5 22.6 %collective-permute-start.2 = (bf16[128,1536]{1,0:T(8,128)(2,1)S(1)}, bf16[128,1536]{1,0:T(8,128)(2,1)S(1)}, u32[]{:S(2)}, u32[]{:S(2)}) collective-permute-start(bf16[128,1536]{1,0:T(8,128)(2,1)S(1)} %broadcast_multiply_fusion.refs_0_.m_ref), channel_id=1, source_target_pairs={{16,0},{32,16},{48,32},{0,48},{80,64},{96,80},{112,96},{64,112},{1... | collective-permute-start | bytes 1179656 | tf_op jit(solution)/shard_map/ppermute | solution.py:138
  13.8 22.8 %collective-permute-start.3 = (bf16[128,1536]{1,0:T(8,128)(2,1)S(1)}, bf16[128,1536]{1,0:T(8,128)(2,1)S(1)}, u32[]{:S(2)}, u32[]{:S(2)}) collective-permute-start(bf16[128,1536]{1,0:T(8,128)(2,1)S(1)} %broadcast_multiply_fusion.refs_0_.m_ref), channel_id=1, source_target_pairs={{48,0},{0,16},{16,32},{32,48},{112,64},{64,80},{80,96},{96,112},{1... | collective-permute-start | bytes 1179656 | tf_op jit(solution)/shard_map/ppermute | solution.py:138
  15.7 31.9 %collective-permute-start.1 = (bf16[128,1536]{1,0:T(8,128)(2,1)S(1)}, bf16[128,1536]{1,0:T(8,128)(2,1)S(1)}, u32[]{:S(2)}, u32[]{:S(2)}) collective-permute-start(bf16[128,1536]{1,0:T(8,128)(2,1)S(1)} %broadcast_multiply_fusion.refs_0_.m_ref), channel_id=1, source_target_pairs={{64,0},{80,16},{96,32},{112,48},{128,64},{144,80},{160,96},{176,11... | collective-permute-start | bytes 1179656 | tf_op jit(solution)/shard_map/ppermute | solution.py:138
  23.3 0.7 copy-start
  25.4 24.9 %all-to-all-start = ((f32[16,8,128]{2,1,0:T(8,128)}), f32[16,8,128]{2,1,0:T(8,128)S(1)}, u32[]{:S(2)}, u32[]{:S(2)}) async-start(f32[16,8,128]{2,1,0:T(8,128)} %bitcast.9), calls=%async_computation | async-start | bytes 131072 | tf_op jit(solution)/shard_map/all_to_all | solution.py:160
  37.6 15.0 %collective-permute-start.5 = (bf16[128,1536]{1,0:T(8,128)(2,1)}, bf16[128,1536]{1,0:T(8,128)(2,1)S(1)}, u32[]{:S(2)}, u32[]{:S(2)}) collective-permute-start(bf16[128,1536]{1,0:T(8,128)(2,1)} %get-tuple-element.12), channel_id=1, source_target_pairs={{16,0},{49,1},{32,16},{1,17},{48,32},{17,33},{0,48},{33,49},{80,64... | collective-permute-start | bytes 1179656 | tf_op jit(solution)/shard_map/ppermute | solution.py:146
  40.4 14.9 %collective-permute-start.6 = (bf16[128,1536]{1,0:T(8,128)(2,1)}, bf16[128,1536]{1,0:T(8,128)(2,1)S(1)}, u32[]{:S(2)}, u32[]{:S(2)}) collective-permute-start(bf16[128,1536]{1,0:T(8,128)(2,1)} %get-tuple-element.11), channel_id=1, source_target_pairs={{384,0},{400,16},{416,32},{432,48},{448,64},{464,80},{480,96},{496... | collective-permute-start | bytes 1179656 | tf_op jit(solution)/shard_map/ppermute | solution.py:138
  47.6 19.6 %collective-permute-start.4 = (bf16[128,1536]{1,0:T(8,128)(2,1)S(1)}, bf16[128,1536]{1,0:T(8,128)(2,1)S(1)}, u32[]{:S(2)}, u32[]{:S(2)}) collective-permute-start(bf16[128,1536]{1,0:T(8,128)(2,1)S(1)} %collective-permute-done.1.refs_2_), channel_id=1, source_target_pairs={{128,0},{144,16},{160,32},{176,48},{192,64},{208,80},{224,96},{240... | collective-permute-start | bytes 1179656 | tf_op jit(solution)/shard_map/ppermute | solution.py:138
  83.6 9.6 %collective-permute-start.7 = (f32[128,128]{1,0:T(8,128)S(1)}, f32[128,128]{1,0:T(8,128)S(1)}, u32[]{:S(2)}, u32[]{:S(2)}) collective-permute-start(f32[128,128]{1,0:T(8,128)S(1)} %slice_reduce_fusion), channel_id=1, source_target_pairs={{12,12},{2,2},{8,76},{14,28},{6,18},{4,60},{10,50},{7,22},{5,54},{... | collective-permute-start | bytes 196616 | tf_op jit(solution)/shard_map/ppermute | solution.py:192
  91.3 10.9 %collective-permute-start.8 = (f32[128,128]{1,0:T(8,128)S(1)}, f32[128,128]{1,0:T(8,128)S(1)}, u32[]{:S(2)}, u32[]{:S(2)}) collective-permute-start(f32[128,128]{1,0:T(8,128)S(1)} %slice_reduce_fusion), channel_id=1, source_target_pairs={{0,0},{1,17},{28,28},{18,18},{24,92},{30,44},{22,34},{20,12},{26,2... | collective-permute-start | bytes 196616 | tf_op jit(solution)/shard_map/ppermute | solution.py:193

commit v5 on v3

--- a/solution.py
+++ b/solution.py
@@ -13,8 +13,9 @@
 BLK = 128
 KC = 1536
 
-HELD = ((0, 0), (5, 0), (1, 0), (0, 1), (0, 3), (2, 0), (0, 2), (4, 0))
+HELD = ((0, 0), (1, 0), (5, 0), (0, 1), (0, 3), (2, 0), (4, 0), (0, 2))
 NH = len(HELD)
+SWAP = (0, 1, 2, 4, 3, 5, 6, 7)
 EARLY = 5
 HALF = NCOL // 2
 
@@ -70,7 +71,8 @@
                     assert (p, q) not in seen
                     seen.add((p, q))
     assert len(seen) == NR * (NR - 1) // 2
-    return left, right, sends
+    swap = np.asarray(SWAP, np.int32)
+    return np.stack([left, swap[left]], 1), np.stack([right, swap[right]], 1), sends
 
 
 def product(m, s):
@@ -136,17 +138,16 @@
     masked = constraint * jnp.repeat(present, BLK, axis=1)
 
     def move(x, dz, dy):
-        pairs = [(place(z + dz, y + dy), place(z, y)) for z in range(NZ) for y in range(NY)]
-        return lax.ppermute(x, ROW, pairs)
+        pairs = [
+            (place(z + dz, y + (1 - 2 * k) * dy) * 2 + k, place(z, y) * 2 + k)
+            for z in range(NZ)
+            for y in range(NY)
+            for k in range(2)
+        ]
+        return lax.ppermute(x, ROW + ("core",), pairs)
 
     held = [masked] + [move(masked, *at) for at in HELD[1:EARLY]]
-    held.append(move(held[2], 1, 0))
-    core = lax.axis_index("core")
-    hops = [
-        (place(z, y + 1 - 2 * k) * 2 + k, place(z, y) * 2 + k) for z in range(NZ) for y in range(NY) for k in range(2)
-    ]
-    held.append(lax.ppermute(jnp.where(core == 0, held[3], held[4]), ROW + ("core",), hops))
-    held.append(move(held[1], -1, 0))
+    held += [move(held[1], 1, 0), move(held[2], -1, 0), move(held[3], 0, 1)]
 
     small = pltpu.CompilerParams(vmem_limit_bytes=4 * 2**20)
     d = scaling.reshape(1, KC)
@@ -164,8 +165,8 @@
     high = lax.reduce_precision(strip, 5, 10)
     riders = jnp.concatenate([high, strip - high], axis=0)
 
-    lt = lax.dynamic_index_in_dim(jnp.asarray(left), row, 0, keepdims=False)
-    rt = lax.dynamic_index_in_dim(jnp.asarray(right), row, 0, keepdims=False)
+    lt = lax.dynamic_slice(jnp.asarray(left), (row, lax.axis_index("core"), 0), (1, 1, NCOL)).reshape(NCOL)
+    rt = lax.dynamic_slice(jnp.asarray(right), (row, lax.axis_index("core"), 0), (1, 1, NCOL)).reshape(NCOL)
     stack = jax.ShapeDtypeStruct((EARLY, BLK, KC), jnp.bfloat16)
     sums = jax.ShapeDtypeStruct((HALF, BLK, BLK), jnp.float32)
     params = pltpu.CompilerParams(vmem_limit_bytes=20 * 2**20)

time: 94.7 us -> 96.8 us (1.022)
  waiting for transfers between devices: 13.4 us -> 22.1 us
  starting transfers between devices: 50.8 us -> 44.4 us
    ppermute x7, waiting for transfers between devices: 4.94 us -> 13.6 us  [move(): return lax.ppermute(x, ROW + ('core',), pairs)]
    ppermute x7, starting transfers between devices: 36.8 us -> 28.9 us  [move(): return lax.ppermute(x, ROW + ('core',), pairs)]
  transfers between devices with their start and end apart: 10 -> 10, of which waited for: 3 -> 5; matrix products, arithmetic and copies ran while one was open for 2% -> 2% of each run, Pallas kernels for 4% -> 4%
where the time goes in v5:
time: 96.8 us; the launch traced here: 96.3 us
  starting transfers between devices  44.4 us (46%)
  waiting for transfers between devices  22.1 us (23%)
  blocking collectives  17.7 us (18%)
  Pallas kernels  7.09 us (7%)
  local copies, waits for them, and re-layouts  2.14 us (2%)
  other arithmetic  2.04 us (2%)
    ppermute x7, starting transfers between devices, move(): return lax.ppermute(x, ROW + ('core',), pairs)  28.9 us
    all_to_all x1, blocking collectives, body(): parts = lax.all_to_all(parts, COL, 0, 0, tiled=True).astype(jnp.float32)  17.7 us
    ppermute x7, waiting for transfers between devices, move(): return lax.ppermute(x, ROW + ('core',), pairs)  13.6 us
    ppermute x1, waiting for transfers between devices, body(): odd = lax.ppermute(mine, ROW + COL, sends[1])  7.72 us
    all_to_all x1, starting transfers between devices, body(): lax.all_to_all(diag, COL, 0, 0, tiled=True).reshape(NCOL, BLK // NCOL, BLK)  7.41 us
    ppermute x1, starting transfers between devices, body(): even = lax.ppermute(mine, ROW + COL, sends[0])  6.82 us
    pallas_call x1, Pallas kernels, body(): pl.pallas_call(early_kernel, out_shape=(sums, stack, stack), in_specs=[sm...  2.26 us
    pallas_call x1, Pallas kernels, body(): pl.pallas_call(late_kernel, out_shape=jax.ShapeDtypeStruct((NCOL, BLK + 2...  2.17 us
  transfers between devices with their start and end apart: 10, of which 5 were waited for; matrix products, arithmetic and copies ran while one was open for 2% of the time, Pallas kernels for 4%

profile of v5, /device:TPU:9, one launch (start us, length us, event | category | flops | bytes accessed | tf_op | source)
XLA Modules:
  0.0 96.3 jit_solution(15474862633964063179)
XLA Ops:
  0.7 0.7 convert_bitcast_fusion
  1.4 1.0 %broadcast_multiply_fusion.refs_0_.m_ref = bf16[128,1536]{1,0:T(8,128)(2,1)S(1)} fusion(bf16[128,1536]{1,0:T(8,128)(2,1)} %param.8, bf16[1536]{0:T(1024)(128)(2,1)S(1)} %broadcast_bitcast_fusion), kind=kLoop, calls=%fused_computation.1 | loop fusion | flops 196608 | bytes 789504 | tf_op jit(solution)/shard_map/mul | solution.py:138
  2.4 10.7 %collective-permute-start = (bf16[128,1536]{1,0:T(8,128)(2,1)S(1)}, bf16[128,1536]{1,0:T(8,128)(2,1)S(1)}, u32[]{:S(2)}, u32[]{:S(2)}) collective-permute-start(bf16[128,1536]{1,0:T(8,128)(2,1)S(1)} %broadcast_multiply_fusion.refs_0_.m_ref), channel_id=1, source_target_pairs={{64,0},{65,1},{80,16},{81,17},{96,32},{97,33},{112,48},{113,49},{1... | collective-permute-start | bytes 1179656 | tf_op jit(solution)/shard_map/ppermute | solution.py:147
  13.1 1.9 %collective-permute-start.1 = (bf16[128,1536]{1,0:T(8,128)(2,1)S(1)}, bf16[128,1536]{1,0:T(8,128)(2,1)S(1)}, u32[]{:S(2)}, u32[]{:S(2)}) collective-permute-start(bf16[128,1536]{1,0:T(8,128)(2,1)S(1)} %broadcast_multiply_fusion.refs_0_.m_ref), channel_id=1, source_target_pairs={{320,0},{321,1},{336,16},{337,17},{352,32},{353,33},{368,48},{369,... | collective-permute-start | bytes 1179656 | tf_op jit(solution)/shard_map/ppermute | solution.py:147
  15.0 4.2 %collective-permute-start.2 = (bf16[128,1536]{1,0:T(8,128)(2,1)S(1)}, bf16[128,1536]{1,0:T(8,128)(2,1)S(1)}, u32[]{:S(2)}, u32[]{:S(2)}) collective-permute-start(bf16[128,1536]{1,0:T(8,128)(2,1)S(1)} %broadcast_multiply_fusion.refs_0_.m_ref), channel_id=1, source_target_pairs={{16,0},{49,1},{32,16},{1,17},{48,32},{17,33},{0,48},{33,49},{80,64... | collective-permute-start | bytes 1179656 | tf_op jit(solution)/shard_map/ppermute | solution.py:147
  19.3 0.7 reshape.34.d_ref
  20.7 1.4 %diag.1 = f32[128,128]{1,0:T(8,128)} custom-call(s32[2]{0:T(128)S(1)} %pad_add_fusion.ids, s32[1]{0:T(128)} %copy.9.period, f32[16]{0:T(128)S(1)} %copy-done, f32[1,1536]{1,0:T(1,128)S(1)} %reshape.34.d_ref, bf16[128,1536]{1,0:T(8,128)(2,1)S(1)} %broadcast_multiply_fusion.refs_0_.m_ref), custom_call_target="tpu_custom_call" | custom-call | tf_op jit(solution)/shard_map/diag/pallas_call | solution.py:155
  22.2 7.4 %all-to-all-start = ((f32[16,8,128]{2,1,0:T(8,128)}), f32[16,8,128]{2,1,0:T(8,128)S(1)}, u32[]{:S(2)}, u32[]{:S(2)}) async-start(f32[16,8,128]{2,1,0:T(8,128)} %bitcast.9), calls=%async_computation | async-start | bytes 131072 | tf_op jit(solution)/shard_map/all_to_all | solution.py:163
  29.6 3.8 %collective-permute-start.3 = (bf16[128,1536]{1,0:T(8,128)(2,1)S(1)}, bf16[128,1536]{1,0:T(8,128)(2,1)S(1)}, u32[]{:S(2)}, u32[]{:S(2)}) collective-permute-start(bf16[128,1536]{1,0:T(8,128)(2,1)S(1)} %broadcast_multiply_fusion.refs_0_.m_ref), channel_id=1, source_target_pairs={{48,0},{17,1},{0,16},{33,17},{16,32},{49,33},{32,48},{1,49},{112,6... | collective-permute-start | bytes 1179656 | tf_op jit(solution)/shard_map/ppermute | solution.py:147
  33.3 2.2 %collective-permute-start.4 = (bf16[128,1536]{1,0:T(8,128)(2,1)S(1)}, bf16[128,1536]{1,0:T(8,128)(2,1)S(1)}, u32[]{:S(2)}, u32[]{:S(2)}) collective-permute-start(bf16[128,1536]{1,0:T(8,128)(2,1)S(1)} %collective-permute-done.refs_1_), channel_id=1, source_target_pairs={{64,0},{65,1},{80,16},{81,17},{96,32},{97,33},{112,48},{113,49},{1... | collective-permute-start | bytes 1179656 | tf_op jit(solution)/shard_map/ppermute | solution.py:147
  35.5 6.0 %collective-permute-done.1.refs_2_ = bf16[128,1536]{1,0:T(8,128)(2,1)S(1)} collective-permute-done((bf16[128,1536]{1,0:T(8,128)(2,1)S(1)}, bf16[128,1536]{1,0:T(8,128)(2,1)S(1)}, u32[]{:S(2)}, u32[]{:S(2)}) %collective-permute-start.1) | collective-permute-done | bytes 393248 | tf_op jit(solution)/shard_map/ppermute | solution.py:147
  41.5 1.9 %collective-permute-start.5 = (bf16[128,1536]{1,0:T(8,128)(2,1)S(1)}, bf16[128,1536]{1,0:T(8,128)(2,1)S(1)}, u32[]{:S(2)}, u32[]{:S(2)}) collective-permute-start(bf16[128,1536]{1,0:T(8,128)(2,1)S(1)} %collective-permute-done.1.refs_2_), channel_id=1, source_target_pairs={{448,0},{449,1},{464,16},{465,17},{480,32},{481,33},{496,48},{497,... | collective-permute-start | bytes 1179656 | tf_op jit(solution)/shard_map/ppermute | solution.py:147
  43.5 4.2 %collective-permute-start.6 = (bf16[128,1536]{1,0:T(8,128)(2,1)S(1)}, bf16[128,1536]{1,0:T(8,128)(2,1)S(1)}, u32[]{:S(2)}, u32[]{:S(2)}) collective-permute-start(bf16[128,1536]{1,0:T(8,128)(2,1)S(1)} %collective-permute-done.2.refs_3_), channel_id=1, source_target_pairs={{16,0},{49,1},{32,16},{1,17},{48,32},{17,33},{0,48},{33,49},{80,64... | collective-permute-start | bytes 1179656 | tf_op jit(solution)/shard_map/ppermute | solution.py:147
  47.7 0.7 dynamic-slice_bitcast_fusion
  48.5 2.3 %early.1 = (f32[8,128,128]{2,1,0:T(8,128)S(1)}, bf16[5,128,1536]{2,1,0:T(8,128)(2,1)S(1)}, bf16[5,128,1536]{2,1,0:T(8,128)(2,1)S(1)}) custom-call(s32[16]{0:T(128)S(1)} %get-tuple-element.14.left, s32[16]{0:T(128)S(1)} %get-tuple-element.13.right, f32[1,1536]{1,0:T(1,128)S(1)} %reshape.34.d_ref, bf16[128,1536]{1,0:T(8,128)(2,1)S(1)} %broadcast_multiply_fusion.refs_0_.m_ref, ...), custom_call_target="tpu_custom_call" | custom-call | tf_op jit(solution)/shard_map/early/pallas_call | solution.py:173
  50.7 4.1 %collective-permute-done.5.refs_1_ = bf16[128,1536]{1,0:T(8,128)(2,1)S(1)} collective-permute-done((bf16[128,1536]{1,0:T(8,128)(2,1)S(1)}, bf16[128,1536]{1,0:T(8,128)(2,1)S(1)}, u32[]{:S(2)}, u32[]{:S(2)}) %collective-permute-start.5) | collective-permute-done | bytes 393248 | tf_op jit(solution)/shard_map/ppermute | solution.py:147
  54.8 3.5 %collective-permute-done.6.refs_2_ = bf16[128,1536]{1,0:T(8,128)(2,1)S(1)} collective-permute-done((bf16[128,1536]{1,0:T(8,128)(2,1)S(1)}, bf16[128,1536]{1,0:T(8,128)(2,1)S(1)}, u32[]{:S(2)}, u32[]{:S(2)}) %collective-permute-start.6) | collective-permute-done | bytes 393248 | tf_op jit(solution)/shard_map/ppermute | solution.py:147
  58.3 2.2 %late.1 = f32[16,144,128]{2,1,0:T(8,128)S(1)} custom-call(s32[16]{0:T(128)S(1)} %get-tuple-element.14.left, s32[16]{0:T(128)S(1)} %get-tuple-element.13.right, f32[1,1536]{1,0:T(1,128)S(1)} %reshape.34.d_ref, bf16[5,128,1536]{2,1,0:T(8,128)(2,1)S(1)} %get-tuple-element.8.masked_in, bf16[5,128,1536]{2,1,0:T(8,128)(2,1)S(1)} %get-tuple-element.9.scaled_in, ...), custom_call_target="tpu_custom_call" | custom-call | tf_op jit(solution)/shard_map/late/pallas_call | solution.py:181
  60.6 17.7 %all_to_all.14 = f16[16,144,128]{2,1,0:T(8,128)(2,1)S(1)} all-to-all(f16[16,144,128]{2,1,0:T(8,128)(2,1)S(1)} %convert_element_type.13), channel_id=1, replica_groups=mesh['z'=8,'yh'=4,'x'=4,'yl'=2,'core'=2] {'x','yl','core'}, dimensions={0} | all-to-all | bytes 1179648 | tf_op jit(solution)/shard_map/all_to_all | solution.py:191
  78.4 6.8 %collective-permute-start.7 = (f32[128,128]{1,0:T(8,128)S(1)}, f32[128,128]{1,0:T(8,128)S(1)}, u32[]{:S(2)}, u32[]{:S(2)}) collective-permute-start(f32[128,128]{1,0:T(8,128)S(1)} %slice_reduce_fusion), channel_id=1, source_target_pairs={{2,2},{10,10},{6,74},{14,18},{8,26},{4,50},{12,58},{5,4},{7,20},{1... | collective-permute-start | bytes 196616 | tf_op jit(solution)/shard_map/ppermute | solution.py:195
  85.3 1.3 %collective-permute-start.8 = (f32[128,128]{1,0:T(8,128)S(1)}, f32[128,128]{1,0:T(8,128)S(1)}, u32[]{:S(2)}, u32[]{:S(2)}) collective-permute-start(f32[128,128]{1,0:T(8,128)S(1)} %slice_reduce_fusion), channel_id=1, source_target_pairs={{0,0},{1,17},{18,18},{26,26},{22,90},{30,34},{24,42},{20,2},{28,10... | collective-permute-start | bytes 196616 | tf_op jit(solution)/shard_map/ppermute | solution.py:196
  86.6 0.8 collective-permute-done.7.even
  87.3 7.7 %collective-permute-done.8.odd = f32[128,128]{1,0:T(8,128)S(1)} collective-permute-done((f32[128,128]{1,0:T(8,128)S(1)}, f32[128,128]{1,0:T(8,128)S(1)}, u32[]{:S(2)}, u32[]{:S(2)}) %collective-permute-start.8) | collective-permute-done | bytes 65568 | tf_op jit(solution)/shard_map/ppermute | solution.py:196
  95.1 1.2 %final.1 = f32[256,128]{1,0:T(8,128)} custom-call(s32[2]{0:T(128)S(1)} %pad_add_fusion.ids, f32[128,128]{1,0:T(8,128)S(1)} %collective-permute-done.7.even, f32[128,128]{1,0:T(8,128)S(1)} %collective-permute-done.8.odd, f32[128,128]{1,0:T(8,128)S(1)} %fusion.diag), custom_call_target="tpu_custom_call" | custom-call | tf_op jit(solution)/shard_map/final/pallas_call | solution.py:197
  (16 shorter events, 1.1 us)
Async XLA Ops:
  2.4 30.9 %collective-permute-start = (bf16[128,1536]{1,0:T(8,128)(2,1)S(1)}, bf16[128,1536]{1,0:T(8,128)(2,1)S(1)}, u32[]{:S(2)}, u32[]{:S(2)}) collective-permute-start(bf16[128,1536]{1,0:T(8,128)(2,1)S(1)} %broadcast_multiply_fusion.refs_0_.m_ref), channel_id=1, source_target_pairs={{64,0},{65,1},{80,16},{81,17},{96,32},{97,33},{112,48},{113,49},{1... | collective-permute-start | bytes 1179656 | tf_op jit(solution)/shard_map/ppermute | solution.py:147
  13.1 28.4 %collective-permute-start.1 = (bf16[128,1536]{1,0:T(8,128)(2,1)S(1)}, bf16[128,1536]{1,0:T(8,128)(2,1)S(1)}, u32[]{:S(2)}, u32[]{:S(2)}) collective-permute-start(bf16[128,1536]{1,0:T(8,128)(2,1)S(1)} %broadcast_multiply_fusion.refs_0_.m_ref), channel_id=1, source_target_pairs={{320,0},{321,1},{336,16},{337,17},{352,32},{353,33},{368,48},{369,... | collective-permute-start | bytes 1179656 | tf_op jit(solution)/shard_map/ppermute | solution.py:147
  15.0 28.4 %collective-permute-start.2 = (bf16[128,1536]{1,0:T(8,128)(2,1)S(1)}, bf16[128,1536]{1,0:T(8,128)(2,1)S(1)}, u32[]{:S(2)}, u32[]{:S(2)}) collective-permute-start(bf16[128,1536]{1,0:T(8,128)(2,1)S(1)} %broadcast_multiply_fusion.refs_0_.m_ref), channel_id=1, source_target_pairs={{16,0},{49,1},{32,16},{1,17},{48,32},{17,33},{0,48},{33,49},{80,64... | collective-permute-start | bytes 1179656 | tf_op jit(solution)/shard_map/ppermute | solution.py:147
  20.1 0.7 copy-start
  22.2 26.2 %all-to-all-start = ((f32[16,8,128]{2,1,0:T(8,128)}), f32[16,8,128]{2,1,0:T(8,128)S(1)}, u32[]{:S(2)}, u32[]{:S(2)}) async-start(f32[16,8,128]{2,1,0:T(8,128)} %bitcast.9), calls=%async_computation | async-start | bytes 131072 | tf_op jit(solution)/shard_map/all_to_all | solution.py:163
  29.6 18.9 %collective-permute-start.3 = (bf16[128,1536]{1,0:T(8,128)(2,1)S(1)}, bf16[128,1536]{1,0:T(8,128)(2,1)S(1)}, u32[]{:S(2)}, u32[]{:S(2)}) collective-permute-start(bf16[128,1536]{1,0:T(8,128)(2,1)S(1)} %broadcast_multiply_fusion.refs_0_.m_ref), channel_id=1, source_target_pairs={{48,0},{17,1},{0,16},{33,17},{16,32},{49,33},{32,48},{1,49},{112,6... | collective-permute-start | bytes 1179656 | tf_op jit(solution)/shard_map/ppermute | solution.py:147
  33.3 17.4 %collective-permute-start.4 = (bf16[128,1536]{1,0:T(8,128)(2,1)S(1)}, bf16[128,1536]{1,0:T(8,128)(2,1)S(1)}, u32[]{:S(2)}, u32[]{:S(2)}) collective-permute-start(bf16[128,1536]{1,0:T(8,128)(2,1)S(1)} %collective-permute-done.refs_1_), channel_id=1, source_target_pairs={{64,0},{65,1},{80,16},{81,17},{96,32},{97,33},{112,48},{113,49},{1... | collective-permute-start | bytes 1179656 | tf_op jit(solution)/shard_map/ppermute | solution.py:147
  41.5 13.3 %collective-permute-start.5 = (bf16[128,1536]{1,0:T(8,128)(2,1)S(1)}, bf16[128,1536]{1,0:T(8,128)(2,1)S(1)}, u32[]{:S(2)}, u32[]{:S(2)}) collective-permute-start(bf16[128,1536]{1,0:T(8,128)(2,1)S(1)} %collective-permute-done.1.refs_2_), channel_id=1, source_target_pairs={{448,0},{449,1},{464,16},{465,17},{480,32},{481,33},{496,48},{497,... | collective-permute-start | bytes 1179656 | tf_op jit(solution)/shard_map/ppermute | solution.py:147
  43.5 14.8 %collective-permute-start.6 = (bf16[128,1536]{1,0:T(8,128)(2,1)S(1)}, bf16[128,1536]{1,0:T(8,128)(2,1)S(1)}, u32[]{:S(2)}, u32[]{:S(2)}) collective-permute-start(bf16[128,1536]{1,0:T(8,128)(2,1)S(1)} %collective-permute-done.2.refs_3_), channel_id=1, source_target_pairs={{16,0},{49,1},{32,16},{1,17},{48,32},{17,33},{0,48},{33,49},{80,64... | collective-permute-start | bytes 1179656 | tf_op jit(solution)/shard_map/ppermute | solution.py:147
  78.4 8.9 %collective-permute-start.7 = (f32[128,128]{1,0:T(8,128)S(1)}, f32[128,128]{1,0:T(8,128)S(1)}, u32[]{:S(2)}, u32[]{:S(2)}) collective-permute-start(f32[128,128]{1,0:T(8,128)S(1)} %slice_reduce_fusion), channel_id=1, source_target_pairs={{2,2},{10,10},{6,74},{14,18},{8,26},{4,50},{12,58},{5,4},{7,20},{1... | collective-permute-start | bytes 196616 | tf_op jit(solution)/shard_map/ppermute | solution.py:195
  85.3 9.8 %collective-permute-start.8 = (f32[128,128]{1,0:T(8,128)S(1)}, f32[128,128]{1,0:T(8,128)S(1)}, u32[]{:S(2)}, u32[]{:S(2)}) collective-permute-start(f32[128,128]{1,0:T(8,128)S(1)} %slice_reduce_fusion), channel_id=1, source_target_pairs={{0,0},{1,17},{18,18},{26,26},{22,90},{30,34},{24,42},{20,2},{28,10... | collective-permute-start | bytes 196616 | tf_op jit(solution)/shard_map/ppermute | solution.py:196

commit v6 on v4

v6 whole, which is shorter than its diff:
```python
import jax
import jax.numpy as jnp
import numpy as np
from jax import lax
from jax.experimental import pallas as pl
from jax.experimental.pallas import tpu as pltpu
from jax.sharding import Mesh, PartitionSpec as P

ROW = ("z", "yh")
CHIP = ("x", "yl")
COL = CHIP + ("core",)
NZ, NY, NX, NL, NK = 8, 4, 4, 2, 2
NR, NCHIP, NCOL = NZ * NY, NX * NL, NX * NL * NK
BLK = 128
KC = 1536
STEP = BLK // NCOL

HELD = ((0, 0), (2, 0), (0, 1), (1, 0), (0, 3), (4, 0), (0, 2), (3, 0))
NH = len(HELD)
EARLY = 5
NSEND = 4


def place(z, y):
    return (z % NZ) * NY + y % NY


def chip_distance(a, b):
    dx = abs(a // NL - b // NL)
    return min(dx, NX - dx) + abs(a % NL - b % NL)


def colour(edges):
    at = ([[-1] * NSEND for _ in range(NR * NCOL)], [[-1] * NSEND for _ in range(NR * NCOL)])
    colours = [-1] * len(edges)
    for e, ends in enumerate(edges):
        a = at[0][ends[0]].index(-1)
        b = at[1][ends[1]].index(-1)
        path, side, node, want = [], 1, ends[1], a
        while at[side][node][want] >= 0:
            f = at[side][node][want]
            path.append(f)
            side = 1 - side
            node = edges[f][side]
            want = a + b - want
        for f in path:
            for s in (0, 1):
                at[s][edges[f][s]][colours[f]] = -1
        for f in path:
            colours[f] = a + b - colours[f]
        colours[e] = a
        for f in path + [e]:
            for s in (0, 1):
                at[s][edges[f][s]][colours[f]] = f
    return colours


def plan():
    chosen = {}
    for t in range(NH):
        for s in range(t):
            dz, dy = (HELD[t][0] - HELD[s][0]) % NZ, (HELD[t][1] - HELD[s][1]) % NY
            if (dz, dy) not in chosen and (-dz % NZ, -dy % NY) not in chosen:
                chosen[(dz, dy)] = (s, t)
    table = np.zeros((NR * NCOL, 4 * NCHIP + 2 * NSEND), np.int32)
    edges, marks = [], []
    for k in range(NK):
        seen = set()
        for z in range(NZ):
            for y in range(NY):
                g = place(z, y)
                kinds = ([], [])
                for (dz, dy), (s, t) in chosen.items():
                    if (dz, dy) == (4, 0) and z >= 4 or (dz, dy) == (4, 2) and z < 4 or (dz, dy) == (0, 2) and y >= 2:
                        continue
                    a = place(z + (1 - 2 * k) * HELD[s][0], y + (1 - 2 * k) * HELD[s][1])
                    b = place(z + (1 - 2 * k) * HELD[t][0], y + (1 - 2 * k) * HELD[t][1])
                    kinds[t >= EARLY].append((a, b, s, t) if a > b else (b, a, t, s))
                for kind, todo in enumerate(kinds):
                    assert len(todo) <= NCHIP
                    cand = sorted(
                        (chip_distance(i, blk[0] // 4), n, i) for n, blk in enumerate(todo) for i in range(NCHIP)
                    )
                    slot, used = {}, set()
                    for _, n, i in cand:
                        if n not in slot and i not in used:
                            slot[n] = i
                            used.add(i)
                    for n, (p, q, l, r) in enumerate(todo):
                        for i in range(NCHIP):
                            device = g * NCOL + i * NK + k
                            table[device, kind * NCHIP + slot[n]] = l
                            table[device, (2 + kind) * NCHIP + slot[n]] = r
                        edges.append((g * NCOL + slot[n] * NK + k, q * NCOL + p // 2))
                        marks.append((kind, p % 2))
                        assert (p, q) not in seen
                        seen.add((p, q))
        assert len(seen) == NR * (NR - 1) // 2
    sends = [[] for _ in range(NSEND)]
    for (source, owner), (kind, half), c in zip(edges, marks, colour(edges)):
        sends[c].append((source, owner))
        table[source, 4 * NCHIP + c] = kind
        table[owner, 4 * NCHIP + NSEND + c] = half
    return table, sends


def product(m, s):
    return lax.dot_general(m, s, (((1,), (1,)), ((), ())), preferred_element_type=jnp.float32)


def scale(m, d):
    return (m.astype(jnp.float32) * d).astype(jnp.bfloat16)


def early_kernel(table, d_ref, *refs):
    rows, (out, masked, scaled) = refs[:EARLY], refs[EARLY:]
    d = d_ref[...]
    for i in range(EARLY):
        m = rows[i][...]
        masked[i] = m
        scaled[i] = scale(m, d)
    for c in range(NCHIP):
        out[c] = product(masked[table[c]], scaled[table[2 * NCHIP + c]])


def late_kernel(table, d_ref, masked_in, scaled_in, early, riders, *refs):
    rows, (out, masked, scaled) = refs[: NH - EARLY], refs[NH - EARLY :]
    d = d_ref[...]
    for i in range(EARLY):
        masked[i] = masked_in[i]
        scaled[i] = scaled_in[i]
    for i in range(EARLY, NH):
        m = rows[i - EARLY][...]
        masked[i] = m
        scaled[i] = scale(m, d)
    for c in range(NCHIP):
        out[c, :BLK] = early[c]
        out[c, BLK : 2 * BLK] = product(masked[table[NCHIP + c]], scaled[table[3 * NCHIP + c]])
        out[c, 2 * BLK :] = riders[...]


def diag_kernel(ids, period, damping, d_ref, m_ref, out):
    m = m_ref[...]
    damp = jnp.where(ids[1] == 0, damping[period[0]], 0.0)
    i = lax.broadcasted_iota(jnp.int32, (BLK, BLK), 0)
    j = lax.broadcasted_iota(jnp.int32, (BLK, BLK), 1)
    out[...] = product(m, scale(m, d_ref[...])) + jnp.where(i == j, damp, 0.0)


def pick_kernel(table, sums, *outs):
    for c in range(NSEND):
        outs[c][...] = jnp.where(table[4 * NCHIP + c] == 1, sums[BLK:], sums[:BLK])


def final_kernel(ids, table, near, far, *refs):
    got, (out, diag) = refs[:NSEND], refs[NSEND:]
    row, col = ids[0], ids[1]
    own = row // 2 == col
    first = col % NK == 0
    for i in range(NCHIP):
        diag[2 * i * STEP : (2 * i + 1) * STEP] = jnp.where(first, near[i], far[i])
        diag[(2 * i + 1) * STEP : (2 * i + 2) * STEP] = jnp.where(first, far[i], near[i])
    for half in range(2):
        total = jnp.where(own & (row % 2 == half), diag[...], 0.0)
        for c in range(NSEND):
            total = total + jnp.where(table[4 * NCHIP + NSEND + c] == half, got[c][...], 0.0)
        out[half * BLK : (half + 1) * BLK] = total


def body(constraint, pattern, scaling, period, column_period, damping):
    table, sends = plan()
    row, col = lax.axis_index(ROW), lax.axis_index(COL)
    vmem = pl.BlockSpec(memory_space=pltpu.VMEM)
    smem = pl.BlockSpec(memory_space=pltpu.SMEM)
    small = pltpu.CompilerParams(vmem_limit_bytes=4 * 2**20)
    large = pltpu.CompilerParams(vmem_limit_bytes=20 * 2**20)
    block = jax.ShapeDtypeStruct((BLK, BLK), jnp.float32)

    same = column_period[None, :] == period[:, None]
    before = column_period[None, :] == period[:, None] - 1
    present = jnp.where(same | before | (pattern > 0), 1, 0).astype(constraint.dtype)
    masked = constraint * jnp.repeat(present, BLK, axis=1)

    def move(x, dz, dy):
        pairs = []
        for z in range(NZ):
            for y in range(NY):
                for k in range(NK):
                    source = place(z + (1 - 2 * k) * dz, y + (1 - 2 * k) * dy)
                    pairs.append((source * NK + k, place(z, y) * NK + k))
        return lax.ppermute(x, ROW + ("core",), pairs)

    held = [masked] + [move(masked, *at) for at in HELD[1:EARLY]]
    held += [move(held[1], 2, 0), move(held[2], 0, 1), move(held[1], 1, 0)]

    d = scaling.reshape(1, KC)
    ids = jnp.stack([row, col])
    mine = lax.dynamic_slice(jnp.asarray(table), (row * NCOL + col, 0), (1, table.shape[1])).reshape(-1)
    diag = pl.pallas_call(
        diag_kernel,
        out_shape=block,
        in_specs=[smem] * 3 + [vmem] * 2,
        out_specs=vmem,
        compiler_params=small,
        name="diag",
    )(ids, period, damping, d, masked)
    strips = lax.all_to_all(diag, COL, 0, 0, tiled=True).reshape(NCOL, STEP, BLK)
    strip = jnp.sum(strips, axis=0)
    high = lax.reduce_precision(strip, 5, 10)
    riders = jnp.concatenate([high, strip - high], axis=0)

    stack = jax.ShapeDtypeStruct((EARLY, BLK, KC), jnp.bfloat16)
    early, masked_rows, scaled_rows = pl.pallas_call(
        early_kernel,
        out_shape=(jax.ShapeDtypeStruct((NCHIP, BLK, BLK), jnp.float32), stack, stack),
        in_specs=[smem] + [vmem] * (1 + EARLY),
        out_specs=(vmem,) * 3,
        compiler_params=large,
        name="early",
    )(mine, d, *held[:EARLY])
    parts = pl.pallas_call(
        late_kernel,
        out_shape=jax.ShapeDtypeStruct((NCHIP, 2 * BLK + 2 * STEP, BLK), jnp.float32),
        in_specs=[smem] + [vmem] * (5 + NH - EARLY),
        out_specs=vmem,
        scratch_shapes=[pltpu.VMEM((NH, BLK, KC), jnp.bfloat16)] * 2,
        compiler_params=large,
        name="late",
    )(mine, d, masked_rows, scaled_rows, early, riders, *held[EARLY:])
    parts = lax.all_to_all(parts.astype(jnp.float16), CHIP, 0, 0, tiled=True).astype(jnp.float32)
    sums = jnp.sum(parts[:, : 2 * BLK], axis=0)
    near = parts[:, 2 * BLK : 2 * BLK + STEP] + parts[:, 2 * BLK + STEP :]
    leaving = pl.pallas_call(
        pick_kernel,
        out_shape=(block,) * NSEND,
        in_specs=[smem, vmem],
        out_specs=(vmem,) * NSEND,
        compiler_params=small,
        name="pick",
    )(mine, sums)
    got = [lax.ppermute(x, ROW + COL, pairs) for x, pairs in zip(leaving, sends)]
    far = lax.ppermute(near, "core", [(0, 1), (1, 0)])
    return pl.pallas_call(
        final_kernel,
        out_shape=jax.ShapeDtypeStruct((2 * BLK, BLK), jnp.float32),
        in_specs=[smem] * 2 + [vmem] * (2 + NSEND),
        out_specs=vmem,
        scratch_shapes=[pltpu.VMEM((BLK, BLK), jnp.float32)],
        compiler_params=small,
        name="final",
    )(ids, mine, near, far, *got)


def solution(mesh):
    split = Mesh(mesh.devices.reshape(NZ, NY, NX, NL, NK), ROW + COL)
    return jax.shard_map(
        body,
        mesh=split,
        in_specs=(P(ROW, COL), P(ROW, COL), P(COL), P(ROW), P(COL), P()),
        out_specs=P(COL, ROW),
        check_vma=False,
    )
```

time: 104 us -> 95.7 us (0.920)
  the two profiles are of different devices: /device:TPU:12 before, /device:TPU:15 now
where the time goes in v6:
time: 95.7 us; the launch traced here: 95.1 us
  starting transfers between devices  52.8 us (55%)
  waiting for transfers between devices  16.6 us (17%)
  blocking collectives  13 us (14%)
  Pallas kernels  7.71 us (8%)
  local copies, waits for them, and re-layouts  2.13 us (2%)
  other arithmetic  2.03 us (2%)
    ppermute x7, starting transfers between devices, move(): return lax.ppermute(x, ROW + ('core',), pairs)  23.1 us
    ppermute x4, starting transfers between devices, body(): lax.ppermute(x, ROW + COL, pairs)  15.5 us
    all_to_all x1, blocking collectives, body(): lax.all_to_all(parts.astype(jnp.float16), CHIP, 0, 0, tiled=True)  13 us
    all_to_all x1, starting transfers between devices, body(): lax.all_to_all(diag, COL, 0, 0, tiled=True).reshape(NCOL, STEP, BLK)  12.2 us
    ppermute x7, waiting for transfers between devices, move(): return lax.ppermute(x, ROW + ('core',), pairs)  8.73 us
    ppermute x4, waiting for transfers between devices, body(): lax.ppermute(x, ROW + COL, pairs)  6.67 us
    pallas_call x1, Pallas kernels, body(): pl.pallas_call(early_kernel, out_shape=(jax.ShapeDtypeStruct((NCHIP, BLK,...  2.25 us
    pallas_call x1, Pallas kernels, body(): pl.pallas_call(late_kernel, out_shape=jax.ShapeDtypeStruct((NCHIP, 2 * BL...  2.19 us
  transfers between devices with their start and end apart: 13, of which 6 were waited for; matrix products, arithmetic and copies ran while one was open for 2% of the time, Pallas kernels for 4%

profile of v6, /device:TPU:15, one launch (start us, length us, event | category | flops | bytes accessed | tf_op | source)
XLA Modules:
  0.0 95.1 jit_solution(1118812952519144957)
XLA Ops:
  2.4 5.8 %collective-permute-start = (bf16[128,1536]{1,0:T(8,128)(2,1)S(1)}, bf16[128,1536]{1,0:T(8,128)(2,1)S(1)}, u32[]{:S(2)}, u32[]{:S(2)}) collective-permute-start(bf16[128,1536]{1,0:T(8,128)(2,1)S(1)} %broadcast_multiply_fusion.refs_0_.m_ref), channel_id=1, source_target_pairs={{128,0},{385,1},{144,16},{401,17},{160,32},{417,33},{176,48},{433,... | collective-permute-start | bytes 1179656 | tf_op jit(solution)/shard_map/ppermute | solution.py:191
  8.3 4.2 %collective-permute-start.1 = (bf16[128,1536]{1,0:T(8,128)(2,1)S(1)}, bf16[128,1536]{1,0:T(8,128)(2,1)S(1)}, u32[]{:S(2)}, u32[]{:S(2)}) collective-permute-start(bf16[128,1536]{1,0:T(8,128)(2,1)S(1)} %broadcast_multiply_fusion.refs_0_.m_ref), channel_id=1, source_target_pairs={{16,0},{49,1},{32,16},{1,17},{48,32},{17,33},{0,48},{33,49},{80,64... | collective-permute-start | bytes 1179656 | tf_op jit(solution)/shard_map/ppermute | solution.py:191
  13.9 1.4 %diag.1 = f32[128,128]{1,0:T(8,128)} custom-call(s32[2]{0:T(128)S(1)} %pad_add_fusion.ids, s32[1]{0:T(128)} %copy.8.period, f32[16]{0:T(128)S(1)} %copy-done, f32[1,1536]{1,0:T(1,128)S(1)} %reshape.27.d_ref, bf16[128,1536]{1,0:T(8,128)(2,1)S(1)} %broadcast_multiply_fusion.refs_0_.m_ref), custom_call_target="tpu_custom_call" | custom-call | tf_op jit(solution)/shard_map/diag/pallas_call | solution.py:199
  15.4 12.2 %all-to-all-start = ((f32[16,8,128]{2,1,0:T(8,128)}), f32[16,8,128]{2,1,0:T(8,128)S(1)}, u32[]{:S(2)}, u32[]{:S(2)}) async-start(f32[16,8,128]{2,1,0:T(8,128)} %bitcast.8), calls=%async_computation | async-start | bytes 131072 | tf_op jit(solution)/shard_map/all_to_all | solution.py:207
  27.6 3.1 %collective-permute-start.2 = (bf16[128,1536]{1,0:T(8,128)(2,1)S(1)}, bf16[128,1536]{1,0:T(8,128)(2,1)S(1)}, u32[]{:S(2)}, u32[]{:S(2)}) collective-permute-start(bf16[128,1536]{1,0:T(8,128)(2,1)S(1)} %broadcast_multiply_fusion.refs_0_.m_ref), channel_id=1, source_target_pairs={{64,0},{449,1},{80,16},{465,17},{96,32},{481,33},{112,48},{497,49}... | collective-permute-start | bytes 1179656 | tf_op jit(solution)/shard_map/ppermute | solution.py:191
  30.7 3.8 %collective-permute-start.3 = (bf16[128,1536]{1,0:T(8,128)(2,1)S(1)}, bf16[128,1536]{1,0:T(8,128)(2,1)S(1)}, u32[]{:S(2)}, u32[]{:S(2)}) collective-permute-start(bf16[128,1536]{1,0:T(8,128)(2,1)S(1)} %broadcast_multiply_fusion.refs_0_.m_ref), channel_id=1, source_target_pairs={{48,0},{17,1},{0,16},{33,17},{16,32},{49,33},{32,48},{1,49},{112,6... | collective-permute-start | bytes 1179656 | tf_op jit(solution)/shard_map/ppermute | solution.py:191
  34.4 1.9 %collective-permute-start.4 = (bf16[128,1536]{1,0:T(8,128)(2,1)S(1)}, bf16[128,1536]{1,0:T(8,128)(2,1)S(1)}, u32[]{:S(2)}, u32[]{:S(2)}) collective-permute-start(bf16[128,1536]{1,0:T(8,128)(2,1)S(1)} %collective-permute-done.refs_1_), channel_id=1, source_target_pairs={{128,0},{385,1},{144,16},{401,17},{160,32},{417,33},{176,48},{433,... | collective-permute-start | bytes 1179656 | tf_op jit(solution)/shard_map/ppermute | solution.py:191
  36.4 1.9 %collective-permute-start.6 = (bf16[128,1536]{1,0:T(8,128)(2,1)S(1)}, bf16[128,1536]{1,0:T(8,128)(2,1)S(1)}, u32[]{:S(2)}, u32[]{:S(2)}) collective-permute-start(bf16[128,1536]{1,0:T(8,128)(2,1)S(1)} %collective-permute-done.refs_1_), channel_id=1, source_target_pairs={{64,0},{449,1},{80,16},{465,17},{96,32},{481,33},{112,48},{497,49}... | collective-permute-start | bytes 1179656 | tf_op jit(solution)/shard_map/ppermute | solution.py:191
  38.3 2.4 %collective-permute-start.5 = (bf16[128,1536]{1,0:T(8,128)(2,1)S(1)}, bf16[128,1536]{1,0:T(8,128)(2,1)S(1)}, u32[]{:S(2)}, u32[]{:S(2)}) collective-permute-start(bf16[128,1536]{1,0:T(8,128)(2,1)S(1)} %collective-permute-done.1.refs_2_), channel_id=1, source_target_pairs={{16,0},{49,1},{32,16},{1,17},{48,32},{17,33},{0,48},{33,49},{80,64... | collective-permute-start | bytes 1179656 | tf_op jit(solution)/shard_map/ppermute | solution.py:191
  41.5 2.5 %collective-permute-done.3.refs_4_ = bf16[128,1536]{1,0:T(8,128)(2,1)S(1)} collective-permute-done((bf16[128,1536]{1,0:T(8,128)(2,1)S(1)}, bf16[128,1536]{1,0:T(8,128)(2,1)S(1)}, u32[]{:S(2)}, u32[]{:S(2)}) %collective-permute-start.3) | collective-permute-done | bytes 393248 | tf_op jit(solution)/shard_map/ppermute | solution.py:191
  44.0 2.2 %early.1 = (f32[8,128,128]{2,1,0:T(8,128)S(1)}, bf16[5,128,1536]{2,1,0:T(8,128)(2,1)S(1)}, bf16[5,128,1536]{2,1,0:T(8,128)(2,1)S(1)}) custom-call(s32[40]{0:T(128)S(1)} %dynamic-slice_bitcast_fusion.table, f32[1,1536]{1,0:T(1,128)S(1)} %reshape.27.d_ref, bf16[128,1536]{1,0:T(8,128)(2,1)S(1)} %broadcast_multiply_fusion.refs_0_.m_ref, ...), custom_call_target="tpu_custom_call" | custom-call | tf_op jit(solution)/shard_map/early/pallas_call | solution.py:213
  46.2 3.1 %collective-permute-done.4.refs_0_ = bf16[128,1536]{1,0:T(8,128)(2,1)S(1)} collective-permute-done((bf16[128,1536]{1,0:T(8,128)(2,1)S(1)}, bf16[128,1536]{1,0:T(8,128)(2,1)S(1)}, u32[]{:S(2)}, u32[]{:S(2)}) %collective-permute-start.4) | collective-permute-done | bytes 393248 | tf_op jit(solution)/shard_map/ppermute | solution.py:191
  49.4 3.1 %collective-permute-done.6.refs_2_ = bf16[128,1536]{1,0:T(8,128)(2,1)S(1)} collective-permute-done((bf16[128,1536]{1,0:T(8,128)(2,1)S(1)}, bf16[128,1536]{1,0:T(8,128)(2,1)S(1)}, u32[]{:S(2)}, u32[]{:S(2)}) %collective-permute-start.6) | collective-permute-done | bytes 393248 | tf_op jit(solution)/shard_map/ppermute | solution.py:191
  52.5 2.2 %late.1 = f32[8,272,128]{2,1,0:T(8,128)S(1)} custom-call(s32[40]{0:T(128)S(1)} %dynamic-slice_bitcast_fusion.table, f32[1,1536]{1,0:T(1,128)S(1)} %reshape.27.d_ref, bf16[5,128,1536]{2,1,0:T(8,128)(2,1)S(1)} %get-tuple-element.12.masked_in, bf16[5,128,1536]{2,1,0:T(8,128)(2,1)S(1)} %get-tuple-element.13.scaled_in, ...), custom_call_target="tpu_custom_call" | custom-call | tf_op jit(solution)/shard_map/late/pallas_call | solution.py:221
  54.8 13.0 %all_to_all.14 = f16[8,272,128]{2,1,0:T(8,128)(2,1)S(1)} all-to-all(f16[8,272,128]{2,1,0:T(8,128)(2,1)S(1)} %convert_element_type.13), channel_id=1, replica_groups=mesh['z'=8,'yh'=4,'x'=4,'yl'=2,'core'=2] {'x','yl'}, dimensions={0} | all-to-all | bytes 1114112 | tf_op jit(solution)/shard_map/all_to_all | solution.py:230
  68.5 1.3 %collective-permute-start.10 = (f32[128,128]{1,0:T(8,128)S(1)}, f32[128,128]{1,0:T(8,128)S(1)}, u32[]{:S(2)}, u32[]{:S(2)}) collective-permute-start(f32[128,128]{1,0:T(8,128)S(1)} %get-tuple-element.17), channel_id=1, source_target_pairs={{4,4},{2,2},{8,52},{10,50},{12,72},{6,22},{0,54},{14,38},{20,20},{... | collective-permute-start | bytes 196616 | tf_op jit(solution)/shard_map/ppermute | solution.py:241
  69.8 11.0 %collective-permute-start.11 = (f32[128,128]{1,0:T(8,128)S(1)}, f32[128,128]{1,0:T(8,128)S(1)}, u32[]{:S(2)}, u32[]{:S(2)}) collective-permute-start(f32[128,128]{1,0:T(8,128)S(1)} %get-tuple-element.18), channel_id=1, source_target_pairs={{8,8},{10,24},{2,34},{18,50},{40,41},{42,57},{34,3},{48,1},{58,35}... | collective-permute-start | bytes 196616 | tf_op jit(solution)/shard_map/ppermute | solution.py:241
  80.8 1.3 %collective-permute-start.8 = (f32[128,128]{1,0:T(8,128)S(1)}, f32[128,128]{1,0:T(8,128)S(1)}, u32[]{:S(2)}, u32[]{:S(2)}) collective-permute-start(f32[128,128]{1,0:T(8,128)S(1)} %get-tuple-element.15), channel_id=1, source_target_pairs={{16,6},{60,121},{48,39},{74,74},{66,138},{72,88},{92,72},{106,107}... | collective-permute-start | bytes 196616 | tf_op jit(solution)/shard_map/ppermute | solution.py:241
  82.1 1.9 %collective-permute-start.9 = (f32[128,128]{1,0:T(8,128)S(1)}, f32[128,128]{1,0:T(8,128)S(1)}, u32[]{:S(2)}, u32[]{:S(2)}) collective-permute-start(f32[128,128]{1,0:T(8,128)S(1)} %get-tuple-element.16), channel_id=1, source_target_pairs={{0,0},{6,20},{14,18},{12,17},{4,36},{24,4},{28,1},{26,2},{20,52},{... | collective-permute-start | bytes 196616 | tf_op jit(solution)/shard_map/ppermute | solution.py:241
  84.1 1.9 %collective-permute-start.7 = (f32[8,8,128]{2,1,0:T(8,128)S(1)}, f32[8,8,128]{2,1,0:T(8,128)S(1)}, u32[]{:S(2)}, u32[]{:S(2)}) collective-permute-start(f32[8,8,128]{2,1,0:T(8,128)S(1)} %slice_add_fusion.near), channel_id=1, source_target_pairs={{0,1},{1,0},{2,3},{3,2},{4,5},{5,4},{6,7},{7,6},{8,9},{9,8},{10,11... | collective-permute-start | bytes 98312 | tf_op jit(solution)/shard_map/ppermute | solution.py:242
  86.0 1.2 %collective-permute-done.7.far = f32[8,8,128]{2,1,0:T(8,128)S(1)} collective-permute-done((f32[8,8,128]{2,1,0:T(8,128)S(1)}, f32[8,8,128]{2,1,0:T(8,128)S(1)}, u32[]{:S(2)}, u32[]{:S(2)}) %collective-permute-start.7) | collective-permute-done | bytes 32800 | tf_op jit(solution)/shard_map/ppermute | solution.py:242
  87.2 1.7 %collective-permute-done.8.refs_0_ = f32[128,128]{1,0:T(8,128)S(1)} collective-permute-done((f32[128,128]{1,0:T(8,128)S(1)}, f32[128,128]{1,0:T(8,128)S(1)}, u32[]{:S(2)}, u32[]{:S(2)}) %collective-permute-start.8) | collective-permute-done | bytes 65568 | tf_op jit(solution)/shard_map/ppermute | solution.py:241
  88.8 5.0 %collective-permute-done.9.refs_1_ = f32[128,128]{1,0:T(8,128)S(1)} collective-permute-done((f32[128,128]{1,0:T(8,128)S(1)}, f32[128,128]{1,0:T(8,128)S(1)}, u32[]{:S(2)}, u32[]{:S(2)}) %collective-permute-start.9) | collective-permute-done | bytes 65568 | tf_op jit(solution)/shard_map/ppermute | solution.py:241
  93.8 1.3 %final.1 = f32[256,128]{1,0:T(8,128)} custom-call(s32[2]{0:T(128)S(1)} %pad_add_fusion.ids, s32[40]{0:T(128)S(1)} %dynamic-slice_bitcast_fusion.table, f32[8,8,128]{2,1,0:T(8,128)S(1)} %slice_add_fusion.near, f32[8,8,128]{2,1,0:T(8,128)S(1)} %collective-permute-done.7.far, f32[128,128]{1,0:T(8,128)S(1)} %collective-permute-done.8.refs_0_, ...), custom_call_target="tpu_custom_call" | custom-call | tf_op jit(solution)/shard_map/final/pallas_call | solution.py:243
  (23 shorter events, 4.7 us)
Async XLA Ops:
  2.4 32.0 %collective-permute-start = (bf16[128,1536]{1,0:T(8,128)(2,1)S(1)}, bf16[128,1536]{1,0:T(8,128)(2,1)S(1)}, u32[]{:S(2)}, u32[]{:S(2)}) collective-permute-start(bf16[128,1536]{1,0:T(8,128)(2,1)S(1)} %broadcast_multiply_fusion.refs_0_.m_ref), channel_id=1, source_target_pairs={{128,0},{385,1},{144,16},{401,17},{160,32},{417,33},{176,48},{433,... | collective-permute-start | bytes 1179656 | tf_op jit(solution)/shard_map/ppermute | solution.py:191
  8.3 30.0 %collective-permute-start.1 = (bf16[128,1536]{1,0:T(8,128)(2,1)S(1)}, bf16[128,1536]{1,0:T(8,128)(2,1)S(1)}, u32[]{:S(2)}, u32[]{:S(2)}) collective-permute-start(bf16[128,1536]{1,0:T(8,128)(2,1)S(1)} %broadcast_multiply_fusion.refs_0_.m_ref), channel_id=1, source_target_pairs={{16,0},{49,1},{32,16},{1,17},{48,32},{17,33},{0,48},{33,49},{80,64... | collective-permute-start | bytes 1179656 | tf_op jit(solution)/shard_map/ppermute | solution.py:191
  13.3 0.7 copy-start
  15.4 26.1 %all-to-all-start = ((f32[16,8,128]{2,1,0:T(8,128)}), f32[16,8,128]{2,1,0:T(8,128)S(1)}, u32[]{:S(2)}, u32[]{:S(2)}) async-start(f32[16,8,128]{2,1,0:T(8,128)} %bitcast.8), calls=%async_computation | async-start | bytes 131072 | tf_op jit(solution)/shard_map/all_to_all | solution.py:207
  27.6 13.9 %collective-permute-start.2 = (bf16[128,1536]{1,0:T(8,128)(2,1)S(1)}, bf16[128,1536]{1,0:T(8,128)(2,1)S(1)}, u32[]{:S(2)}, u32[]{:S(2)}) collective-permute-start(bf16[128,1536]{1,0:T(8,128)(2,1)S(1)} %broadcast_multiply_fusion.refs_0_.m_ref), channel_id=1, source_target_pairs={{64,0},{449,1},{80,16},{465,17},{96,32},{481,33},{112,48},{497,49}... | collective-permute-start | bytes 1179656 | tf_op jit(solution)/shard_map/ppermute | solution.py:191
  30.7 13.3 %collective-permute-start.3 = (bf16[128,1536]{1,0:T(8,128)(2,1)S(1)}, bf16[128,1536]{1,0:T(8,128)(2,1)S(1)}, u32[]{:S(2)}, u32[]{:S(2)}) collective-permute-start(bf16[128,1536]{1,0:T(8,128)(2,1)S(1)} %broadcast_multiply_fusion.refs_0_.m_ref), channel_id=1, source_target_pairs={{48,0},{17,1},{0,16},{33,17},{16,32},{49,33},{32,48},{1,49},{112,6... | collective-permute-start | bytes 1179656 | tf_op jit(solution)/shard_map/ppermute | solution.py:191
  34.4 15.0 %collective-permute-start.4 = (bf16[128,1536]{1,0:T(8,128)(2,1)S(1)}, bf16[128,1536]{1,0:T(8,128)(2,1)S(1)}, u32[]{:S(2)}, u32[]{:S(2)}) collective-permute-start(bf16[128,1536]{1,0:T(8,128)(2,1)S(1)} %collective-permute-done.refs_1_), channel_id=1, source_target_pairs={{128,0},{385,1},{144,16},{401,17},{160,32},{417,33},{176,48},{433,... | collective-permute-start | bytes 1179656 | tf_op jit(solution)/shard_map/ppermute | solution.py:191
  36.4 16.1 %collective-permute-start.6 = (bf16[128,1536]{1,0:T(8,128)(2,1)S(1)}, bf16[128,1536]{1,0:T(8,128)(2,1)S(1)}, u32[]{:S(2)}, u32[]{:S(2)}) collective-permute-start(bf16[128,1536]{1,0:T(8,128)(2,1)S(1)} %collective-permute-done.refs_1_), channel_id=1, source_target_pairs={{64,0},{449,1},{80,16},{465,17},{96,32},{481,33},{112,48},{497,49}... | collective-permute-start | bytes 1179656 | tf_op jit(solution)/shard_map/ppermute | solution.py:191
  38.3 14.2 %collective-permute-start.5 = (bf16[128,1536]{1,0:T(8,128)(2,1)S(1)}, bf16[128,1536]{1,0:T(8,128)(2,1)S(1)}, u32[]{:S(2)}, u32[]{:S(2)}) collective-permute-start(bf16[128,1536]{1,0:T(8,128)(2,1)S(1)} %collective-permute-done.1.refs_2_), channel_id=1, source_target_pairs={{16,0},{49,1},{32,16},{1,17},{48,32},{17,33},{0,48},{33,49},{80,64... | collective-permute-start | bytes 1179656 | tf_op jit(solution)/shard_map/ppermute | solution.py:191
  68.5 18.7 %collective-permute-start.10 = (f32[128,128]{1,0:T(8,128)S(1)}, f32[128,128]{1,0:T(8,128)S(1)}, u32[]{:S(2)}, u32[]{:S(2)}) collective-permute-start(f32[128,128]{1,0:T(8,128)S(1)} %get-tuple-element.17), channel_id=1, source_target_pairs={{4,4},{2,2},{8,52},{10,50},{12,72},{6,22},{0,54},{14,38},{20,20},{... | collective-permute-start | bytes 196616 | tf_op jit(solution)/shard_map/ppermute | solution.py:241
  69.8 17.4 %collective-permute-start.11 = (f32[128,128]{1,0:T(8,128)S(1)}, f32[128,128]{1,0:T(8,128)S(1)}, u32[]{:S(2)}, u32[]{:S(2)}) collective-permute-start(f32[128,128]{1,0:T(8,128)S(1)} %get-tuple-element.18), channel_id=1, source_target_pairs={{8,8},{10,24},{2,34},{18,50},{40,41},{42,57},{34,3},{48,1},{58,35}... | collective-permute-start | bytes 196616 | tf_op jit(solution)/shard_map/ppermute | solution.py:241
  80.8 8.0 %collective-permute-start.8 = (f32[128,128]{1,0:T(8,128)S(1)}, f32[128,128]{1,0:T(8,128)S(1)}, u32[]{:S(2)}, u32[]{:S(2)}) collective-permute-start(f32[128,128]{1,0:T(8,128)S(1)} %get-tuple-element.15), channel_id=1, source_target_pairs={{16,6},{60,121},{48,39},{74,74},{66,138},{72,88},{92,72},{106,107}... | collective-permute-start | bytes 196616 | tf_op jit(solution)/shard_map/ppermute | solution.py:241
  82.1 11.7 %collective-permute-start.9 = (f32[128,128]{1,0:T(8,128)S(1)}, f32[128,128]{1,0:T(8,128)S(1)}, u32[]{:S(2)}, u32[]{:S(2)}) collective-permute-start(f32[128,128]{1,0:T(8,128)S(1)} %get-tuple-element.16), channel_id=1, source_target_pairs={{0,0},{6,20},{14,18},{12,17},{4,36},{24,4},{28,1},{26,2},{20,52},{... | collective-permute-start | bytes 196616 | tf_op jit(solution)/shard_map/ppermute | solution.py:241
  84.1 3.1 %collective-permute-start.7 = (f32[8,8,128]{2,1,0:T(8,128)S(1)}, f32[8,8,128]{2,1,0:T(8,128)S(1)}, u32[]{:S(2)}, u32[]{:S(2)}) collective-permute-start(f32[8,8,128]{2,1,0:T(8,128)S(1)} %slice_add_fusion.near), channel_id=1, source_target_pairs={{0,1},{1,0},{2,3},{3,2},{4,5},{5,4},{6,7},{7,6},{8,9},{9,8},{10,11... | collective-permute-start | bytes 98312 | tf_op jit(solution)/shard_map/ppermute | solution.py:242

commit v7 on v5

--- a/solution.py
+++ b/solution.py
@@ -13,11 +13,14 @@
 BLK = 128
 KC = 1536
 
-HELD = ((0, 0), (1, 0), (5, 0), (0, 1), (0, 3), (2, 0), (4, 0), (0, 2))
+HELD = ((0, 0), (5, 0), (1, 0), (0, 1), (0, 3), (2, 0), (0, 2), (4, 0))
 NH = len(HELD)
 SWAP = (0, 1, 2, 4, 3, 5, 6, 7)
 EARLY = 5
 HALF = NCOL // 2
+LAST = NH - 1
+LATE = HALF - 2
+ROWS = BLK + 2 * BLK // NCOL
 
 
 def place(z, y):
@@ -55,12 +58,16 @@
                 (either if (dz, dy) == (0, 2) else early if t < EARLY else late).append(pair)
             for pair in either:
                 (early if len(early) < HALF else late).append(pair)
-            assert len(early) <= HALF and len(late) <= HALF
+            late.sort(key=lambda pair: LAST in pair[2:])
+            assert len(early) <= HALF and len(late) <= HALF and len(late) >= HALF - 1
             for base, todo in ((0, early), (1, late)):
+                fixed = LATE if base else len(todo)
                 cand = sorted(
-                    (col_distance(2 * i + base, blk[0] // 2), n, i) for n, blk in enumerate(todo) for i in range(HALF)
+                    (col_distance(2 * i + base, blk[0] // 2), n, i)
+                    for n, blk in enumerate(todo[:fixed])
+                    for i in range(LATE if base else HALF)
                 )
-                slot, used = {}, set()
+                slot, used = {n: n for n in range(fixed, len(todo))}, set()
                 for _, n, i in cand:
                     if n not in slot and i not in used:
                         slot[n] = i
@@ -87,7 +94,7 @@
     rows, (out, masked, scaled) = refs[:EARLY], refs[EARLY:]
     d = d_ref[...]
     for i in range(EARLY):
-        m = rows[i][...]
+        m = rows[i][:BLK]
         masked[i] = m
         scaled[i] = scale(m, d)
     for c in range(HALF):
@@ -95,20 +102,39 @@
 
 
 def late_kernel(left, right, d_ref, masked_in, scaled_in, early, riders, *refs):
-    rows, (out, masked, scaled) = refs[: NH - EARLY], refs[NH - EARLY :]
+    rows, (out, masked, scaled) = refs[: LAST - EARLY], refs[LAST - EARLY :]
     d = d_ref[...]
     for i in range(EARLY):
         masked[i] = masked_in[i]
         scaled[i] = scaled_in[i]
-    for i in range(EARLY, NH):
+    for i in range(EARLY, LAST):
         m = rows[i - EARLY][...]
         masked[i] = m
         scaled[i] = scale(m, d)
     for c in range(HALF):
         out[2 * c, :BLK] = early[c]
+    for c in range(LATE):
         out[2 * c + 1, :BLK] = product(masked[left[HALF + c]], scaled[right[HALF + c]])
     for c in range(NCOL):
         out[c, BLK:] = riders[...]
+
+
+def last_kernel(left, right, d_ref, masked, scaled, row, unused, out, scaled_row):
+    scaled_row[...] = scale(row[:BLK], d_ref[...])
+    for c in range(LATE, HALF):
+        l, r = left[HALF + c], right[HALF + c]
+
+        @pl.when(l == LAST)
+        def _():
+            out[2 * c + 1, :BLK] = product(row[:BLK], scaled[r])
+
+        @pl.when(r == LAST)
+        def _():
+            out[2 * c + 1, :BLK] = product(masked[l], scaled_row[...])
+
+        @pl.when((l != LAST) & (r != LAST))
+        def _():
+            out[2 * c + 1, :BLK] = product(masked[l], scaled[r])
 
 
 def diag_kernel(ids, period, damping, d_ref, m_ref, out):
@@ -146,8 +172,9 @@
         ]
         return lax.ppermute(x, ROW + ("core",), pairs)
 
-    held = [masked] + [move(masked, *at) for at in HELD[1:EARLY]]
-    held += [move(held[1], 1, 0), move(held[2], -1, 0), move(held[3], 0, 1)]
+    longer = jnp.pad(masked, ((0, 8), (0, 0)))
+    held = [masked] + [move(longer if at == HELD[1] else masked, *at) for at in HELD[1:EARLY]]
+    held += [move(held[2], 1, 0), move(held[3], 0, 1), move(held[1], -1, 0)]
 
     small = pltpu.CompilerParams(vmem_limit_bytes=4 * 2**20)
     d = scaling.reshape(1, KC)
@@ -178,15 +205,25 @@
         compiler_params=params,
         name="early",
     )(lt, rt, d, *held[:EARLY])
-    parts = pl.pallas_call(
+    known = jax.ShapeDtypeStruct((LAST, BLK, KC), jnp.bfloat16)
+    parts, masked_rows, scaled_rows = pl.pallas_call(
         late_kernel,
-        out_shape=jax.ShapeDtypeStruct((NCOL, BLK + 2 * BLK // NCOL, BLK), jnp.float32),
-        in_specs=[smem] * 2 + [vmem] * (5 + NH - EARLY),
-        out_specs=vmem,
-        scratch_shapes=[pltpu.VMEM((NH, BLK, KC), jnp.bfloat16)] * 2,
+        out_shape=(jax.ShapeDtypeStruct((NCOL, ROWS, BLK), jnp.float32), known, known),
+        in_specs=[smem] * 2 + [vmem] * (5 + LAST - EARLY),
+        out_specs=(vmem,) * 3,
         compiler_params=params,
         name="late",
-    )(lt, rt, d, masked_rows, scaled_rows, early, riders, *held[EARLY:])
+    )(lt, rt, d, masked_rows, scaled_rows, early, riders, *held[EARLY:LAST])
+    parts = pl.pallas_call(
+        last_kernel,
+        out_shape=jax.ShapeDtypeStruct((NCOL, ROWS, BLK), jnp.float32),
+        in_specs=[smem] * 2 + [vmem] * 5,
+        out_specs=vmem,
+        scratch_shapes=[pltpu.VMEM((BLK, KC), jnp.bfloat16)],
+        input_output_aliases={6: 0},
+        compiler_params=params,
+        name="last",
+    )(lt, rt, d, masked_rows, scaled_rows, held[LAST], parts)
     parts = parts.astype(jnp.float16)
     parts = lax.all_to_all(parts, COL, 0, 0, tiled=True).astype(jnp.float32)
     mine = jnp.sum(parts[:, :BLK], axis=0)

time: 96.8 us -> 89.2 us (0.921)
  the two profiles are of different devices: /device:TPU:9 before, /device:TPU:71 now
where the time goes in v7:
time: 89.2 us; the launch traced here: 88.7 us
  starting transfers between devices  39.9 us (45%)
  waiting for transfers between devices  20 us (22%)
  blocking collectives  17.1 us (19%)
  Pallas kernels  7.91 us (9%)
  other arithmetic  2.04 us (2%)
  between operations  0.91 us (1%)
    ppermute x7, starting transfers between devices, move(): return lax.ppermute(x, ROW + ('core',), pairs)  26.2 us
    all_to_all x1, blocking collectives, body(): parts = lax.all_to_all(parts, COL, 0, 0, tiled=True).astype(jnp.float32)  17.1 us
    ppermute x7, waiting for transfers between devices, move(): return lax.ppermute(x, ROW + ('core',), pairs)  10.3 us
    ppermute x1, waiting for transfers between devices, body(): even = lax.ppermute(mine, ROW + COL, sends[0])  7.47 us
    all_to_all x1, starting transfers between devices, body(): lax.all_to_all(diag, COL, 0, 0, tiled=True).reshape(NCOL, BLK // NCOL, BLK)  7.45 us
    ppermute x1, starting transfers between devices, body(): odd = lax.ppermute(mine, ROW + COL, sends[1])  5.03 us
    pallas_call x1, Pallas kernels, body(): pl.pallas_call(early_kernel, out_shape=(sums, stack, stack), in_specs=[sm...  2.26 us
    ppermute x1, waiting for transfers between devices, body(): odd = lax.ppermute(mine, ROW + COL, sends[1])  2.24 us
  transfers between devices with their start and end apart: 10, of which 4 were waited for; matrix products, arithmetic and copies ran while one was open for 1% of the time, Pallas kernels for 6%

profile of v7, /device:TPU:71, one launch (start us, length us, event | category | flops | bytes accessed | tf_op | source)
XLA Modules:
  0.0 88.7 jit_solution(7787537472303845452)
XLA Ops:
  0.7 0.7 convert_bitcast_fusion
  1.4 1.0 %broadcast_multiply_fusion.refs_0_.m_ref = bf16[128,1536]{1,0:T(8,128)(2,1)S(1)} fusion(bf16[128,1536]{1,0:T(8,128)(2,1)} %param.8, bf16[1536]{0:T(1024)(128)(2,1)S(1)} %broadcast_bitcast_fusion), kind=kLoop, calls=%fused_computation.1 | loop fusion | flops 196608 | bytes 789504 | tf_op jit(solution)/shard_map/mul | solution.py:164
  2.5 8.8 %collective-permute-start = (bf16[136,1536]{1,0:T(8,128)(2,1)S(1)}, bf16[136,1536]{1,0:T(8,128)(2,1)S(1)}, u32[]{:S(2)}, u32[]{:S(2)}) collective-permute-start(bf16[136,1536]{1,0:T(8,128)(2,1)S(1)} %pad.4), channel_id=1, source_target_pairs={{320,0},{321,1},{336,16},{337,17},{352,32},{353,33},{368,48},{369,... | collective-permute-start | bytes 1253384 | tf_op jit(solution)/shard_map/ppermute | solution.py:173
  11.3 4.2 %collective-permute-start.2 = (bf16[128,1536]{1,0:T(8,128)(2,1)S(1)}, bf16[128,1536]{1,0:T(8,128)(2,1)S(1)}, u32[]{:S(2)}, u32[]{:S(2)}) collective-permute-start(bf16[128,1536]{1,0:T(8,128)(2,1)S(1)} %broadcast_multiply_fusion.refs_0_.m_ref), channel_id=1, source_target_pairs={{16,0},{49,1},{32,16},{1,17},{48,32},{17,33},{0,48},{33,49},{80,64... | collective-permute-start | bytes 1179656 | tf_op jit(solution)/shard_map/ppermute | solution.py:173
  15.6 1.9 %collective-permute-start.1 = (bf16[128,1536]{1,0:T(8,128)(2,1)S(1)}, bf16[128,1536]{1,0:T(8,128)(2,1)S(1)}, u32[]{:S(2)}, u32[]{:S(2)}) collective-permute-start(bf16[128,1536]{1,0:T(8,128)(2,1)S(1)} %broadcast_multiply_fusion.refs_0_.m_ref), channel_id=1, source_target_pairs={{64,0},{65,1},{80,16},{81,17},{96,32},{97,33},{112,48},{113,49},{1... | collective-permute-start | bytes 1179656 | tf_op jit(solution)/shard_map/ppermute | solution.py:173
  17.6 1.4 %diag.1 = f32[128,128]{1,0:T(8,128)} custom-call(s32[2]{0:T(128)S(1)} %pad_add_fusion.ids, s32[1]{0:T(128)} %copy.11.period, f32[16]{0:T(128)S(1)} %copy-done, f32[1,1536]{1,0:T(1,128)S(1)} %reshape.34.d_ref, bf16[128,1536]{1,0:T(8,128)(2,1)S(1)} %broadcast_multiply_fusion.refs_0_.m_ref), custom_call_target="tpu_custom_call" | custom-call | tf_op jit(solution)/shard_map/diag/pallas_call | solution.py:182
  19.1 7.4 %all-to-all-start = ((f32[16,8,128]{2,1,0:T(8,128)}), f32[16,8,128]{2,1,0:T(8,128)S(1)}, u32[]{:S(2)}, u32[]{:S(2)}) async-start(f32[16,8,128]{2,1,0:T(8,128)} %bitcast.9), calls=%async_computation | async-start | bytes 131072 | tf_op jit(solution)/shard_map/all_to_all | solution.py:190
  26.5 3.8 %collective-permute-start.3 = (bf16[128,1536]{1,0:T(8,128)(2,1)S(1)}, bf16[128,1536]{1,0:T(8,128)(2,1)S(1)}, u32[]{:S(2)}, u32[]{:S(2)}) collective-permute-start(bf16[128,1536]{1,0:T(8,128)(2,1)S(1)} %broadcast_multiply_fusion.refs_0_.m_ref), channel_id=1, source_target_pairs={{48,0},{17,1},{0,16},{33,17},{16,32},{49,33},{32,48},{1,49},{112,6... | collective-permute-start | bytes 1179656 | tf_op jit(solution)/shard_map/ppermute | solution.py:173
  30.3 2.4 %collective-permute-start.5 = (bf16[128,1536]{1,0:T(8,128)(2,1)S(1)}, bf16[128,1536]{1,0:T(8,128)(2,1)S(1)}, u32[]{:S(2)}, u32[]{:S(2)}) collective-permute-start(bf16[128,1536]{1,0:T(8,128)(2,1)S(1)} %collective-permute-done.2.refs_3_), channel_id=1, source_target_pairs={{16,0},{49,1},{32,16},{1,17},{48,32},{17,33},{0,48},{33,49},{80,64... | collective-permute-start | bytes 1179656 | tf_op jit(solution)/shard_map/ppermute | solution.py:173
  32.7 3.1 %collective-permute-start.4 = (bf16[128,1536]{1,0:T(8,128)(2,1)S(1)}, bf16[128,1536]{1,0:T(8,128)(2,1)S(1)}, u32[]{:S(2)}, u32[]{:S(2)}) collective-permute-start(bf16[128,1536]{1,0:T(8,128)(2,1)S(1)} %collective-permute-done.1.refs_2_), channel_id=1, source_target_pairs={{64,0},{65,1},{80,16},{81,17},{96,32},{97,33},{112,48},{113,49},{1... | collective-permute-start | bytes 1179656 | tf_op jit(solution)/shard_map/ppermute | solution.py:173
  35.9 4.5 %collective-permute-done.refs_1_ = bf16[136,1536]{1,0:T(8,128)(2,1)S(1)} collective-permute-done((bf16[136,1536]{1,0:T(8,128)(2,1)S(1)}, bf16[136,1536]{1,0:T(8,128)(2,1)S(1)}, u32[]{:S(2)}, u32[]{:S(2)}) %collective-permute-start) | collective-permute-done | bytes 417824 | tf_op jit(solution)/shard_map/ppermute | solution.py:173
  40.3 1.9 %collective-permute-start.6 = (bf16[136,1536]{1,0:T(8,128)(2,1)S(1)}, bf16[136,1536]{1,0:T(8,128)(2,1)S(1)}, u32[]{:S(2)}, u32[]{:S(2)}) collective-permute-start(bf16[136,1536]{1,0:T(8,128)(2,1)S(1)} %collective-permute-done.refs_1_), channel_id=1, source_target_pairs={{448,0},{449,1},{464,16},{465,17},{480,32},{481,33},{496,48},{497,... | collective-permute-start | bytes 1253384 | tf_op jit(solution)/shard_map/ppermute | solution.py:173
  42.3 0.7 dynamic-slice_bitcast_fusion
  43.0 2.3 %early.1 = (f32[8,128,128]{2,1,0:T(8,128)S(1)}, bf16[5,128,1536]{2,1,0:T(8,128)(2,1)S(1)}, bf16[5,128,1536]{2,1,0:T(8,128)(2,1)S(1)}) custom-call(s32[16]{0:T(128)S(1)} %get-tuple-element.20.left, s32[16]{0:T(128)S(1)} %get-tuple-element.19.right, f32[1,1536]{1,0:T(1,128)S(1)} %reshape.34.d_ref, bf16[128,1536]{1,0:T(8,128)(2,1)S(1)} %broadcast_multiply_fusion.refs_0_.m_ref, ...), custom_call_target="tpu_custom_call" | custom-call | tf_op jit(solution)/shard_map/early/pallas_call | solution.py:200
  45.3 1.8 %late.1 = (f32[16,144,128]{2,1,0:T(8,128)S(1)}, bf16[7,128,1536]{2,1,0:T(8,128)(2,1)S(1)}, bf16[7,128,1536]{2,1,0:T(8,128)(2,1)S(1)}) custom-call(s32[16]{0:T(128)S(1)} %get-tuple-element.20.left, s32[16]{0:T(128)S(1)} %get-tuple-element.19.right, f32[1,1536]{1,0:T(1,128)S(1)} %reshape.34.d_ref, bf16[5,128,1536]{2,1,0:T(8,128)(2,1)S(1)} %get-tuple-element.11.masked_in, ...), custom_call_target="tpu_custom_call" | custom-call | tf_op jit(solution)/shard_map/late/pallas_call | solution.py:209
  47.2 5.8 %collective-permute-done.6.row = bf16[136,1536]{1,0:T(8,128)(2,1)S(1)} collective-permute-done((bf16[136,1536]{1,0:T(8,128)(2,1)S(1)}, bf16[136,1536]{1,0:T(8,128)(2,1)S(1)}, u32[]{:S(2)}, u32[]{:S(2)}) %collective-permute-start.6) | collective-permute-done | bytes 417824 | tf_op jit(solution)/shard_map/ppermute | solution.py:173
  53.0 1.1 %last.1 = f32[16,144,128]{2,1,0:T(8,128)S(1)} custom-call(s32[16]{0:T(128)S(1)} %get-tuple-element.20.left, s32[16]{0:T(128)S(1)} %get-tuple-element.19.right, f32[1,1536]{1,0:T(1,128)S(1)} %reshape.34.d_ref, bf16[7,128,1536]{2,1,0:T(8,128)(2,1)S(1)} %get-tuple-element.14.masked, ...), custom_call_target="tpu_custom_call", output_to_operand_aliasing={{}: (6, {})} | custom-call | tf_op jit(solution)/shard_map/last/pallas_call | solution.py:217
  54.1 0.1 convert_element_type.15
  54.2 17.1 %all_to_all.14 = f16[16,144,128]{2,1,0:T(8,128)(2,1)S(1)} all-to-all(f16[16,144,128]{2,1,0:T(8,128)(2,1)S(1)} %convert_element_type.15), channel_id=1, replica_groups=mesh['z'=8,'yh'=4,'x'=4,'yl'=2,'core'=2] {'x','yl','core'}, dimensions={0} | all-to-all | bytes 1179648 | tf_op jit(solution)/shard_map/all_to_all | solution.py:228
  71.4 5.0 %collective-permute-start.8 = (f32[128,128]{1,0:T(8,128)S(1)}, f32[128,128]{1,0:T(8,128)S(1)}, u32[]{:S(2)}, u32[]{:S(2)}) collective-permute-start(f32[128,128]{1,0:T(8,128)S(1)} %slice_reduce_fusion), channel_id=1, source_target_pairs={{0,0},{13,17},{26,26},{18,18},{22,90},{24,42},{30,34},{20,10},{28,... | collective-permute-start | bytes 196616 | tf_op jit(solution)/shard_map/ppermute | solution.py:233
  76.5 1.3 %collective-permute-start.7 = (f32[128,128]{1,0:T(8,128)S(1)}, f32[128,128]{1,0:T(8,128)S(1)}, u32[]{:S(2)}, u32[]{:S(2)}) collective-permute-start(f32[128,128]{1,0:T(8,128)S(1)} %slice_reduce_fusion), channel_id=1, source_target_pairs={{10,10},{2,2},{6,74},{8,26},{14,18},{4,58},{12,50},{5,4},{1,20},{7... | collective-permute-start | bytes 196616 | tf_op jit(solution)/shard_map/ppermute | solution.py:232
  77.8 2.2 %collective-permute-done.8.odd = f32[128,128]{1,0:T(8,128)S(1)} collective-permute-done((f32[128,128]{1,0:T(8,128)S(1)}, f32[128,128]{1,0:T(8,128)S(1)}, u32[]{:S(2)}, u32[]{:S(2)}) %collective-permute-start.8) | collective-permute-done | bytes 65568 | tf_op jit(solution)/shard_map/ppermute | solution.py:233
  80.0 7.5 %collective-permute-done.7.even = f32[128,128]{1,0:T(8,128)S(1)} collective-permute-done((f32[128,128]{1,0:T(8,128)S(1)}, f32[128,128]{1,0:T(8,128)S(1)}, u32[]{:S(2)}, u32[]{:S(2)}) %collective-permute-start.7) | collective-permute-done | bytes 65568 | tf_op jit(solution)/shard_map/ppermute | solution.py:232
  87.5 1.2 %final.1 = f32[256,128]{1,0:T(8,128)} custom-call(s32[2]{0:T(128)S(1)} %pad_add_fusion.ids, f32[128,128]{1,0:T(8,128)S(1)} %collective-permute-done.7.even, f32[128,128]{1,0:T(8,128)S(1)} %collective-permute-done.8.odd, f32[128,128]{1,0:T(8,128)S(1)} %fusion.diag), custom_call_target="tpu_custom_call" | custom-call | tf_op jit(solution)/shard_map/final/pallas_call | solution.py:234
  (20 shorter events, 0.4 us)
Async XLA Ops:
  0.0 17.5 %copy-start.1 = (f32[1536]{0:T(1024)S(1)}, f32[1536]{0:T(1024)}, u32[]{:S(2)}) copy-start(f32[1536]{0:T(1024)} %param.10) | copy-start | bytes 18436
  0.0 17.6 %copy-start = (f32[16]{0:T(128)S(1)}, f32[16]{0:T(128)}, u32[]{:S(2)}) copy-start(f32[16]{0:T(128)} %damping.1) | copy-start | bytes 196
  2.5 37.8 %collective-permute-start = (bf16[136,1536]{1,0:T(8,128)(2,1)S(1)}, bf16[136,1536]{1,0:T(8,128)(2,1)S(1)}, u32[]{:S(2)}, u32[]{:S(2)}) collective-permute-start(bf16[136,1536]{1,0:T(8,128)(2,1)S(1)} %pad.4), channel_id=1, source_target_pairs={{320,0},{321,1},{336,16},{337,17},{352,32},{353,33},{368,48},{369,... | collective-permute-start | bytes 1253384 | tf_op jit(solution)/shard_map/ppermute | solution.py:173
  11.3 18.9 %collective-permute-start.2 = (bf16[128,1536]{1,0:T(8,128)(2,1)S(1)}, bf16[128,1536]{1,0:T(8,128)(2,1)S(1)}, u32[]{:S(2)}, u32[]{:S(2)}) collective-permute-start(bf16[128,1536]{1,0:T(8,128)(2,1)S(1)} %broadcast_multiply_fusion.refs_0_.m_ref), channel_id=1, source_target_pairs={{16,0},{49,1},{32,16},{1,17},{48,32},{17,33},{0,48},{33,49},{80,64... | collective-permute-start | bytes 1179656 | tf_op jit(solution)/shard_map/ppermute | solution.py:173
  15.6 17.2 %collective-permute-start.1 = (bf16[128,1536]{1,0:T(8,128)(2,1)S(1)}, bf16[128,1536]{1,0:T(8,128)(2,1)S(1)}, u32[]{:S(2)}, u32[]{:S(2)}) collective-permute-start(bf16[128,1536]{1,0:T(8,128)(2,1)S(1)} %broadcast_multiply_fusion.refs_0_.m_ref), channel_id=1, source_target_pairs={{64,0},{65,1},{80,16},{81,17},{96,32},{97,33},{112,48},{113,49},{1... | collective-permute-start | bytes 1179656 | tf_op jit(solution)/shard_map/ppermute | solution.py:173
  19.1 23.9 %all-to-all-start = ((f32[16,8,128]{2,1,0:T(8,128)}), f32[16,8,128]{2,1,0:T(8,128)S(1)}, u32[]{:S(2)}, u32[]{:S(2)}) async-start(f32[16,8,128]{2,1,0:T(8,128)} %bitcast.9), calls=%async_computation | async-start | bytes 131072 | tf_op jit(solution)/shard_map/all_to_all | solution.py:190
  26.5 16.5 %collective-permute-start.3 = (bf16[128,1536]{1,0:T(8,128)(2,1)S(1)}, bf16[128,1536]{1,0:T(8,128)(2,1)S(1)}, u32[]{:S(2)}, u32[]{:S(2)}) collective-permute-start(bf16[128,1536]{1,0:T(8,128)(2,1)S(1)} %broadcast_multiply_fusion.refs_0_.m_ref), channel_id=1, source_target_pairs={{48,0},{17,1},{0,16},{33,17},{16,32},{49,33},{32,48},{1,49},{112,6... | collective-permute-start | bytes 1179656 | tf_op jit(solution)/shard_map/ppermute | solution.py:173
  30.3 15.0 %collective-permute-start.5 = (bf16[128,1536]{1,0:T(8,128)(2,1)S(1)}, bf16[128,1536]{1,0:T(8,128)(2,1)S(1)}, u32[]{:S(2)}, u32[]{:S(2)}) collective-permute-start(bf16[128,1536]{1,0:T(8,128)(2,1)S(1)} %collective-permute-done.2.refs_3_), channel_id=1, source_target_pairs={{16,0},{49,1},{32,16},{1,17},{48,32},{17,33},{0,48},{33,49},{80,64... | collective-permute-start | bytes 1179656 | tf_op jit(solution)/shard_map/ppermute | solution.py:173
  32.7 12.6 %collective-permute-start.4 = (bf16[128,1536]{1,0:T(8,128)(2,1)S(1)}, bf16[128,1536]{1,0:T(8,128)(2,1)S(1)}, u32[]{:S(2)}, u32[]{:S(2)}) collective-permute-start(bf16[128,1536]{1,0:T(8,128)(2,1)S(1)} %collective-permute-done.1.refs_2_), channel_id=1, source_target_pairs={{64,0},{65,1},{80,16},{81,17},{96,32},{97,33},{112,48},{113,49},{1... | collective-permute-start | bytes 1179656 | tf_op jit(solution)/shard_map/ppermute | solution.py:173
  40.3 12.6 %collective-permute-start.6 = (bf16[136,1536]{1,0:T(8,128)(2,1)S(1)}, bf16[136,1536]{1,0:T(8,128)(2,1)S(1)}, u32[]{:S(2)}, u32[]{:S(2)}) collective-permute-start(bf16[136,1536]{1,0:T(8,128)(2,1)S(1)} %collective-permute-done.refs_1_), channel_id=1, source_target_pairs={{448,0},{449,1},{464,16},{465,17},{480,32},{481,33},{496,48},{497,... | collective-permute-start | bytes 1253384 | tf_op jit(solution)/shard_map/ppermute | solution.py:173
  71.4 8.6 %collective-permute-start.8 = (f32[128,128]{1,0:T(8,128)S(1)}, f32[128,128]{1,0:T(8,128)S(1)}, u32[]{:S(2)}, u32[]{:S(2)}) collective-permute-start(f32[128,128]{1,0:T(8,128)S(1)} %slice_reduce_fusion), channel_id=1, source_target_pairs={{0,0},{13,17},{26,26},{18,18},{22,90},{24,42},{30,34},{20,10},{28,... | collective-permute-start | bytes 196616 | tf_op jit(solution)/shard_map/ppermute | solution.py:233
  76.5 11.0 %collective-permute-start.7 = (f32[128,128]{1,0:T(8,128)S(1)}, f32[128,128]{1,0:T(8,128)S(1)}, u32[]{:S(2)}, u32[]{:S(2)}) collective-permute-start(f32[128,128]{1,0:T(8,128)S(1)} %slice_reduce_fusion), channel_id=1, source_target_pairs={{10,10},{2,2},{6,74},{8,26},{14,18},{4,58},{12,50},{5,4},{1,20},{7... | collective-permute-start | bytes 196616 | tf_op jit(solution)/shard_map/ppermute | solution.py:232

commit v8 on v7

--- a/solution.py
+++ b/solution.py
@@ -145,13 +145,6 @@
     out[...] = product(m, scale(m, d_ref[...])) + jnp.where(i == j, damp, 0.0)
 
 
-def final_kernel(ids, even, odd, diag, out):
-    row, col = ids[0], ids[1]
-    own = row // 2 == col
-    out[0:BLK] = jnp.where(own & (row % 2 == 0), diag[...], even[...])
-    out[BLK : 2 * BLK] = jnp.where(own & (row % 2 == 1), diag[...], odd[...])
-
-
 def body(constraint, pattern, scaling, period, column_period, damping):
     left, right, sends = plan()
     row, col = lax.axis_index(ROW), lax.axis_index(COL)
@@ -231,14 +224,9 @@
     diag = (parts[:, BLK : BLK + step] + parts[:, BLK + step :]).reshape(BLK, BLK)
     even = lax.ppermute(mine, ROW + COL, sends[0])
     odd = lax.ppermute(mine, ROW + COL, sends[1])
-    return pl.pallas_call(
-        final_kernel,
-        out_shape=jax.ShapeDtypeStruct((2 * BLK, BLK), jnp.float32),
-        in_specs=[smem] + [vmem] * 3,
-        out_specs=vmem,
-        compiler_params=small,
-        name="final",
-    )(ids, even, odd, diag)
+    own = row // 2 == col
+    halves = [jnp.where(own & (row % 2 == h), diag, block) for h, block in enumerate((even, odd))]
+    return jnp.concatenate(halves, axis=0)
 
 
 def solution(mesh):

time: 89.2 us -> 88.7 us (level)
  Pallas kernels: 7.91 us -> 6.7 us
    pallas_call x1 -> x0, Pallas kernels: 1.22 us -> none  [body(): pl.pallas_call(final_kernel, out_shape=jax.ShapeDtypeStruct((2 * BLK, BLK...]
where the time goes in v8:
time: 88.7 us; the launch traced here: 88.2 us
  starting transfers between devices  39.9 us (45%)
  waiting for transfers between devices  20 us (23%)
  blocking collectives  17.1 us (19%)
  Pallas kernels  6.7 us (8%)
  other arithmetic  2.72 us (3%)
  between operations  0.93 us (1%)
    ppermute x7, starting transfers between devices, move(): return lax.ppermute(x, ROW + ('core',), pairs)  26.2 us
    all_to_all x1, blocking collectives, body(): parts = lax.all_to_all(parts, COL, 0, 0, tiled=True).astype(jnp.float32)  17.1 us
    ppermute x7, waiting for transfers between devices, move(): return lax.ppermute(x, ROW + ('core',), pairs)  10.3 us
    ppermute x1, waiting for transfers between devices, body(): even = lax.ppermute(mine, ROW + COL, sends[0])  7.47 us
    all_to_all x1, starting transfers between devices, body(): lax.all_to_all(diag, COL, 0, 0, tiled=True).reshape(NCOL, BLK // NCOL, BLK)  7.45 us
    ppermute x1, starting transfers between devices, body(): odd = lax.ppermute(mine, ROW + COL, sends[1])  5.03 us
    pallas_call x1, Pallas kernels, body(): pl.pallas_call(early_kernel, out_shape=(sums, stack, stack), in_specs=[sm...  2.26 us
    ppermute x1, waiting for transfers between devices, body(): odd = lax.ppermute(mine, ROW + COL, sends[1])  2.23 us
  transfers between devices with their start and end apart: 10, of which 4 were waited for; matrix products, arithmetic and copies ran while one was open for 1% of the time, Pallas kernels for 6%

profile of v8, /device:TPU:71, one launch (start us, length us, event | category | flops | bytes accessed | tf_op | source)
XLA Modules:
  0.0 88.2 jit_solution(6411954943748923974)
XLA Ops:
  0.7 0.7 convert_bitcast_fusion
  1.4 1.0 %broadcast_multiply_fusion.refs_0_.m_ref = bf16[128,1536]{1,0:T(8,128)(2,1)S(1)} fusion(bf16[128,1536]{1,0:T(8,128)(2,1)} %param.8, bf16[1536]{0:T(1024)(128)(2,1)S(1)} %broadcast_bitcast_fusion), kind=kLoop, calls=%fused_computation.1 | loop fusion | flops 196608 | bytes 789504 | tf_op jit(solution)/shard_map/mul | solution.py:157
  2.5 8.8 %collective-permute-start = (bf16[136,1536]{1,0:T(8,128)(2,1)S(1)}, bf16[136,1536]{1,0:T(8,128)(2,1)S(1)}, u32[]{:S(2)}, u32[]{:S(2)}) collective-permute-start(bf16[136,1536]{1,0:T(8,128)(2,1)S(1)} %pad.4), channel_id=1, source_target_pairs={{320,0},{321,1},{336,16},{337,17},{352,32},{353,33},{368,48},{369,... | collective-permute-start | bytes 1253384 | tf_op jit(solution)/shard_map/ppermute | solution.py:166
  11.3 4.2 %collective-permute-start.2 = (bf16[128,1536]{1,0:T(8,128)(2,1)S(1)}, bf16[128,1536]{1,0:T(8,128)(2,1)S(1)}, u32[]{:S(2)}, u32[]{:S(2)}) collective-permute-start(bf16[128,1536]{1,0:T(8,128)(2,1)S(1)} %broadcast_multiply_fusion.refs_0_.m_ref), channel_id=1, source_target_pairs={{16,0},{49,1},{32,16},{1,17},{48,32},{17,33},{0,48},{33,49},{80,64... | collective-permute-start | bytes 1179656 | tf_op jit(solution)/shard_map/ppermute | solution.py:166
  15.6 1.9 %collective-permute-start.1 = (bf16[128,1536]{1,0:T(8,128)(2,1)S(1)}, bf16[128,1536]{1,0:T(8,128)(2,1)S(1)}, u32[]{:S(2)}, u32[]{:S(2)}) collective-permute-start(bf16[128,1536]{1,0:T(8,128)(2,1)S(1)} %broadcast_multiply_fusion.refs_0_.m_ref), channel_id=1, source_target_pairs={{64,0},{65,1},{80,16},{81,17},{96,32},{97,33},{112,48},{113,49},{1... | collective-permute-start | bytes 1179656 | tf_op jit(solution)/shard_map/ppermute | solution.py:166
  17.6 1.4 %diag.1 = f32[128,128]{1,0:T(8,128)} custom-call(s32[2]{0:T(128)S(1)} %pad_add_fusion.ids, s32[1]{0:T(128)} %copy.11.period, f32[16]{0:T(128)S(1)} %copy-done, f32[1,1536]{1,0:T(1,128)S(1)} %reshape.34.d_ref, bf16[128,1536]{1,0:T(8,128)(2,1)S(1)} %broadcast_multiply_fusion.refs_0_.m_ref), custom_call_target="tpu_custom_call" | custom-call | tf_op jit(solution)/shard_map/diag/pallas_call | solution.py:175
  19.1 7.4 %all-to-all-start = ((f32[16,8,128]{2,1,0:T(8,128)}), f32[16,8,128]{2,1,0:T(8,128)S(1)}, u32[]{:S(2)}, u32[]{:S(2)}) async-start(f32[16,8,128]{2,1,0:T(8,128)} %bitcast.9), calls=%async_computation | async-start | bytes 131072 | tf_op jit(solution)/shard_map/all_to_all | solution.py:183
  26.5 3.8 %collective-permute-start.3 = (bf16[128,1536]{1,0:T(8,128)(2,1)S(1)}, bf16[128,1536]{1,0:T(8,128)(2,1)S(1)}, u32[]{:S(2)}, u32[]{:S(2)}) collective-permute-start(bf16[128,1536]{1,0:T(8,128)(2,1)S(1)} %broadcast_multiply_fusion.refs_0_.m_ref), channel_id=1, source_target_pairs={{48,0},{17,1},{0,16},{33,17},{16,32},{49,33},{32,48},{1,49},{112,6... | collective-permute-start | bytes 1179656 | tf_op jit(solution)/shard_map/ppermute | solution.py:166
  30.3 2.4 %collective-permute-start.5 = (bf16[128,1536]{1,0:T(8,128)(2,1)S(1)}, bf16[128,1536]{1,0:T(8,128)(2,1)S(1)}, u32[]{:S(2)}, u32[]{:S(2)}) collective-permute-start(bf16[128,1536]{1,0:T(8,128)(2,1)S(1)} %collective-permute-done.2.refs_3_), channel_id=1, source_target_pairs={{16,0},{49,1},{32,16},{1,17},{48,32},{17,33},{0,48},{33,49},{80,64... | collective-permute-start | bytes 1179656 | tf_op jit(solution)/shard_map/ppermute | solution.py:166
  32.7 3.1 %collective-permute-start.4 = (bf16[128,1536]{1,0:T(8,128)(2,1)S(1)}, bf16[128,1536]{1,0:T(8,128)(2,1)S(1)}, u32[]{:S(2)}, u32[]{:S(2)}) collective-permute-start(bf16[128,1536]{1,0:T(8,128)(2,1)S(1)} %collective-permute-done.1.refs_2_), channel_id=1, source_target_pairs={{64,0},{65,1},{80,16},{81,17},{96,32},{97,33},{112,48},{113,49},{1... | collective-permute-start | bytes 1179656 | tf_op jit(solution)/shard_map/ppermute | solution.py:166
  35.9 4.5 %collective-permute-done.refs_1_ = bf16[136,1536]{1,0:T(8,128)(2,1)S(1)} collective-permute-done((bf16[136,1536]{1,0:T(8,128)(2,1)S(1)}, bf16[136,1536]{1,0:T(8,128)(2,1)S(1)}, u32[]{:S(2)}, u32[]{:S(2)}) %collective-permute-start) | collective-permute-done | bytes 417824 | tf_op jit(solution)/shard_map/ppermute | solution.py:166
  40.3 1.9 %collective-permute-start.6 = (bf16[136,1536]{1,0:T(8,128)(2,1)S(1)}, bf16[136,1536]{1,0:T(8,128)(2,1)S(1)}, u32[]{:S(2)}, u32[]{:S(2)}) collective-permute-start(bf16[136,1536]{1,0:T(8,128)(2,1)S(1)} %collective-permute-done.refs_1_), channel_id=1, source_target_pairs={{448,0},{449,1},{464,16},{465,17},{480,32},{481,33},{496,48},{497,... | collective-permute-start | bytes 1253384 | tf_op jit(solution)/shard_map/ppermute | solution.py:166
  42.3 0.7 dynamic-slice_bitcast_fusion
  43.0 2.3 %early.1 = (f32[8,128,128]{2,1,0:T(8,128)S(1)}, bf16[5,128,1536]{2,1,0:T(8,128)(2,1)S(1)}, bf16[5,128,1536]{2,1,0:T(8,128)(2,1)S(1)}) custom-call(s32[16]{0:T(128)S(1)} %get-tuple-element.22.left, s32[16]{0:T(128)S(1)} %get-tuple-element.21.right, f32[1,1536]{1,0:T(1,128)S(1)} %reshape.34.d_ref, bf16[128,1536]{1,0:T(8,128)(2,1)S(1)} %broadcast_multiply_fusion.refs_0_.m_ref, ...), custom_call_target="tpu_custom_call" | custom-call | tf_op jit(solution)/shard_map/early/pallas_call | solution.py:193
  45.3 1.8 %late.1 = (f32[16,144,128]{2,1,0:T(8,128)S(1)}, bf16[7,128,1536]{2,1,0:T(8,128)(2,1)S(1)}, bf16[7,128,1536]{2,1,0:T(8,128)(2,1)S(1)}) custom-call(s32[16]{0:T(128)S(1)} %get-tuple-element.22.left, s32[16]{0:T(128)S(1)} %get-tuple-element.21.right, f32[1,1536]{1,0:T(1,128)S(1)} %reshape.34.d_ref, bf16[5,128,1536]{2,1,0:T(8,128)(2,1)S(1)} %get-tuple-element.11.masked_in, ...), custom_call_target="tpu_custom_call" | custom-call | tf_op jit(solution)/shard_map/late/pallas_call | solution.py:202
  47.2 5.8 %collective-permute-done.6.row = bf16[136,1536]{1,0:T(8,128)(2,1)S(1)} collective-permute-done((bf16[136,1536]{1,0:T(8,128)(2,1)S(1)}, bf16[136,1536]{1,0:T(8,128)(2,1)S(1)}, u32[]{:S(2)}, u32[]{:S(2)}) %collective-permute-start.6) | collective-permute-done | bytes 417824 | tf_op jit(solution)/shard_map/ppermute | solution.py:166
  53.0 1.1 %last.1 = f32[16,144,128]{2,1,0:T(8,128)S(1)} custom-call(s32[16]{0:T(128)S(1)} %get-tuple-element.22.left, s32[16]{0:T(128)S(1)} %get-tuple-element.21.right, f32[1,1536]{1,0:T(1,128)S(1)} %reshape.34.d_ref, bf16[7,128,1536]{2,1,0:T(8,128)(2,1)S(1)} %get-tuple-element.14.masked, ...), custom_call_target="tpu_custom_call", output_to_operand_aliasing={{}: (6, {})} | custom-call | tf_op jit(solution)/shard_map/last/pallas_call | solution.py:210
  54.1 0.1 convert_element_type.15
  54.2 17.1 %all_to_all.14 = f16[16,144,128]{2,1,0:T(8,128)(2,1)S(1)} all-to-all(f16[16,144,128]{2,1,0:T(8,128)(2,1)S(1)} %convert_element_type.15), channel_id=1, replica_groups=mesh['z'=8,'yh'=4,'x'=4,'yl'=2,'core'=2] {'x','yl','core'}, dimensions={0} | all-to-all | bytes 1179648 | tf_op jit(solution)/shard_map/all_to_all | solution.py:221
  71.4 5.0 %collective-permute-start.8 = (f32[128,128]{1,0:T(8,128)S(1)}, f32[128,128]{1,0:T(8,128)S(1)}, u32[]{:S(2)}, u32[]{:S(2)}) collective-permute-start(f32[128,128]{1,0:T(8,128)S(1)} %slice_reduce_fusion), channel_id=1, source_target_pairs={{0,0},{13,17},{26,26},{18,18},{22,90},{24,42},{30,34},{20,10},{28,... | collective-permute-start | bytes 196616 | tf_op jit(solution)/shard_map/ppermute | solution.py:226
  76.5 1.3 %collective-permute-start.7 = (f32[128,128]{1,0:T(8,128)S(1)}, f32[128,128]{1,0:T(8,128)S(1)}, u32[]{:S(2)}, u32[]{:S(2)}) collective-permute-start(f32[128,128]{1,0:T(8,128)S(1)} %slice_reduce_fusion), channel_id=1, source_target_pairs={{10,10},{2,2},{6,74},{8,26},{14,18},{4,58},{12,50},{5,4},{1,20},{7... | collective-permute-start | bytes 196616 | tf_op jit(solution)/shard_map/ppermute | solution.py:225
  77.8 2.2 %collective-permute-done.8 = f32[128,128]{1,0:T(8,128)S(1)} collective-permute-done((f32[128,128]{1,0:T(8,128)S(1)}, f32[128,128]{1,0:T(8,128)S(1)}, u32[]{:S(2)}, u32[]{:S(2)}) %collective-permute-start.8) | collective-permute-done | bytes 65568 | tf_op jit(solution)/shard_map/ppermute | solution.py:226
  80.0 7.5 %collective-permute-done.7 = f32[128,128]{1,0:T(8,128)S(1)} collective-permute-done((f32[128,128]{1,0:T(8,128)S(1)}, f32[128,128]{1,0:T(8,128)S(1)}, u32[]{:S(2)}, u32[]{:S(2)}) %collective-permute-start.7) | collective-permute-done | bytes 65568 | tf_op jit(solution)/shard_map/ppermute | solution.py:225
  87.5 0.7 pad_maximum_fusion
  (20 shorter events, 0.4 us)
Async XLA Ops:
  0.0 17.5 %copy-start.1 = (f32[1536]{0:T(1024)S(1)}, f32[1536]{0:T(1024)}, u32[]{:S(2)}) copy-start(f32[1536]{0:T(1024)} %param.10) | copy-start | bytes 18436
  0.0 17.6 %copy-start = (f32[16]{0:T(128)S(1)}, f32[16]{0:T(128)}, u32[]{:S(2)}) copy-start(f32[16]{0:T(128)} %damping.1) | copy-start | bytes 196
  2.5 37.8 %collective-permute-start = (bf16[136,1536]{1,0:T(8,128)(2,1)S(1)}, bf16[136,1536]{1,0:T(8,128)(2,1)S(1)}, u32[]{:S(2)}, u32[]{:S(2)}) collective-permute-start(bf16[136,1536]{1,0:T(8,128)(2,1)S(1)} %pad.4), channel_id=1, source_target_pairs={{320,0},{321,1},{336,16},{337,17},{352,32},{353,33},{368,48},{369,... | collective-permute-start | bytes 1253384 | tf_op jit(solution)/shard_map/ppermute | solution.py:166
  11.3 18.9 %collective-permute-start.2 = (bf16[128,1536]{1,0:T(8,128)(2,1)S(1)}, bf16[128,1536]{1,0:T(8,128)(2,1)S(1)}, u32[]{:S(2)}, u32[]{:S(2)}) collective-permute-start(bf16[128,1536]{1,0:T(8,128)(2,1)S(1)} %broadcast_multiply_fusion.refs_0_.m_ref), channel_id=1, source_target_pairs={{16,0},{49,1},{32,16},{1,17},{48,32},{17,33},{0,48},{33,49},{80,64... | collective-permute-start | bytes 1179656 | tf_op jit(solution)/shard_map/ppermute | solution.py:166
  15.6 17.2 %collective-permute-start.1 = (bf16[128,1536]{1,0:T(8,128)(2,1)S(1)}, bf16[128,1536]{1,0:T(8,128)(2,1)S(1)}, u32[]{:S(2)}, u32[]{:S(2)}) collective-permute-start(bf16[128,1536]{1,0:T(8,128)(2,1)S(1)} %broadcast_multiply_fusion.refs_0_.m_ref), channel_id=1, source_target_pairs={{64,0},{65,1},{80,16},{81,17},{96,32},{97,33},{112,48},{113,49},{1... | collective-permute-start | bytes 1179656 | tf_op jit(solution)/shard_map/ppermute | solution.py:166
  19.1 23.9 %all-to-all-start = ((f32[16,8,128]{2,1,0:T(8,128)}), f32[16,8,128]{2,1,0:T(8,128)S(1)}, u32[]{:S(2)}, u32[]{:S(2)}) async-start(f32[16,8,128]{2,1,0:T(8,128)} %bitcast.9), calls=%async_computation | async-start | bytes 131072 | tf_op jit(solution)/shard_map/all_to_all | solution.py:183
  26.5 16.5 %collective-permute-start.3 = (bf16[128,1536]{1,0:T(8,128)(2,1)S(1)}, bf16[128,1536]{1,0:T(8,128)(2,1)S(1)}, u32[]{:S(2)}, u32[]{:S(2)}) collective-permute-start(bf16[128,1536]{1,0:T(8,128)(2,1)S(1)} %broadcast_multiply_fusion.refs_0_.m_ref), channel_id=1, source_target_pairs={{48,0},{17,1},{0,16},{33,17},{16,32},{49,33},{32,48},{1,49},{112,6... | collective-permute-start | bytes 1179656 | tf_op jit(solution)/shard_map/ppermute | solution.py:166
  30.3 15.0 %collective-permute-start.5 = (bf16[128,1536]{1,0:T(8,128)(2,1)S(1)}, bf16[128,1536]{1,0:T(8,128)(2,1)S(1)}, u32[]{:S(2)}, u32[]{:S(2)}) collective-permute-start(bf16[128,1536]{1,0:T(8,128)(2,1)S(1)} %collective-permute-done.2.refs_3_), channel_id=1, source_target_pairs={{16,0},{49,1},{32,16},{1,17},{48,32},{17,33},{0,48},{33,49},{80,64... | collective-permute-start | bytes 1179656 | tf_op jit(solution)/shard_map/ppermute | solution.py:166
  32.7 12.6 %collective-permute-start.4 = (bf16[128,1536]{1,0:T(8,128)(2,1)S(1)}, bf16[128,1536]{1,0:T(8,128)(2,1)S(1)}, u32[]{:S(2)}, u32[]{:S(2)}) collective-permute-start(bf16[128,1536]{1,0:T(8,128)(2,1)S(1)} %collective-permute-done.1.refs_2_), channel_id=1, source_target_pairs={{64,0},{65,1},{80,16},{81,17},{96,32},{97,33},{112,48},{113,49},{1... | collective-permute-start | bytes 1179656 | tf_op jit(solution)/shard_map/ppermute | solution.py:166
  40.3 12.6 %collective-permute-start.6 = (bf16[136,1536]{1,0:T(8,128)(2,1)S(1)}, bf16[136,1536]{1,0:T(8,128)(2,1)S(1)}, u32[]{:S(2)}, u32[]{:S(2)}) collective-permute-start(bf16[136,1536]{1,0:T(8,128)(2,1)S(1)} %collective-permute-done.refs_1_), channel_id=1, source_target_pairs={{448,0},{449,1},{464,16},{465,17},{480,32},{481,33},{496,48},{497,... | collective-permute-start | bytes 1253384 | tf_op jit(solution)/shard_map/ppermute | solution.py:166
  71.4 8.6 %collective-permute-start.8 = (f32[128,128]{1,0:T(8,128)S(1)}, f32[128,128]{1,0:T(8,128)S(1)}, u32[]{:S(2)}, u32[]{:S(2)}) collective-permute-start(f32[128,128]{1,0:T(8,128)S(1)} %slice_reduce_fusion), channel_id=1, source_target_pairs={{0,0},{13,17},{26,26},{18,18},{22,90},{24,42},{30,34},{20,10},{28,... | collective-permute-start | bytes 196616 | tf_op jit(solution)/shard_map/ppermute | solution.py:226
  76.5 11.0 %collective-permute-start.7 = (f32[128,128]{1,0:T(8,128)S(1)}, f32[128,128]{1,0:T(8,128)S(1)}, u32[]{:S(2)}, u32[]{:S(2)}) collective-permute-start(f32[128,128]{1,0:T(8,128)S(1)} %slice_reduce_fusion), channel_id=1, source_target_pairs={{10,10},{2,2},{6,74},{8,26},{14,18},{4,58},{12,50},{5,4},{1,20},{7... | collective-permute-start | bytes 196616 | tf_op jit(solution)/shard_map/ppermute | solution.py:225

commit v9 on v8

--- a/solution.py
+++ b/solution.py
@@ -20,7 +20,7 @@
 HALF = NCOL // 2
 LAST = NH - 1
 LATE = HALF - 2
-ROWS = BLK + 2 * BLK // NCOL
+ROWS = BLK + BLK // NCOL
 
 
 def place(z, y):
@@ -116,7 +116,7 @@
     for c in range(LATE):
         out[2 * c + 1, :BLK] = product(masked[left[HALF + c]], scaled[right[HALF + c]])
     for c in range(NCOL):
-        out[c, BLK:] = riders[...]
+        out[c, BLK:] = riders[: BLK // NCOL]
 
 
 def last_kernel(left, right, d_ref, masked, scaled, row, unused, out, scaled_row):
@@ -220,8 +220,7 @@
     parts = parts.astype(jnp.float16)
     parts = lax.all_to_all(parts, COL, 0, 0, tiled=True).astype(jnp.float32)
     mine = jnp.sum(parts[:, :BLK], axis=0)
-    step = BLK // NCOL
-    diag = (parts[:, BLK : BLK + step] + parts[:, BLK + step :]).reshape(BLK, BLK)
+    diag = parts[:, BLK:].reshape(BLK, BLK)
     even = lax.ppermute(mine, ROW + COL, sends[0])
     odd = lax.ppermute(mine, ROW + COL, sends[1])
     own = row // 2 == col

time: 88.7 us -> 88.2 us (level)
  no operation moved by 1% of the time
where the time goes in v9:
time: 88.2 us; the launch traced here: 87.7 us
  starting transfers between devices  39.7 us (45%)
  waiting for transfers between devices  20 us (23%)
  blocking collectives  16.9 us (19%)
  Pallas kernels  6.7 us (8%)
  other arithmetic  2.7 us (3%)
  between operations  0.93 us (1%)
    ppermute x7, starting transfers between devices, move(): return lax.ppermute(x, ROW + ('core',), pairs)  26.2 us
    all_to_all x1, blocking collectives, body(): parts = lax.all_to_all(parts, COL, 0, 0, tiled=True).astype(jnp.float32)  16.9 us
    ppermute x7, waiting for transfers between devices, move(): return lax.ppermute(x, ROW + ('core',), pairs)  10.3 us
    all_to_all x1, starting transfers between devices, body(): lax.all_to_all(diag, COL, 0, 0, tiled=True).reshape(NCOL, BLK // NCOL, BLK)  7.45 us
    ppermute x1, waiting for transfers between devices, body(): even = lax.ppermute(mine, ROW + COL, sends[0])  7.24 us
    ppermute x1, starting transfers between devices, body(): odd = lax.ppermute(mine, ROW + COL, sends[1])  4.8 us
    ppermute x1, waiting for transfers between devices, body(): odd = lax.ppermute(mine, ROW + COL, sends[1])  2.45 us
    pallas_call x1, Pallas kernels, body(): pl.pallas_call(early_kernel, out_shape=(sums, stack, stack), in_specs=[sm...  2.26 us
  transfers between devices with their start and end apart: 10, of which 4 were waited for; matrix products, arithmetic and copies ran while one was open for 1% of the time, Pallas kernels for 6%

profile of v9, /device:TPU:71, one launch (start us, length us, event | category | flops | bytes accessed | tf_op | source)
XLA Modules:
  0.0 87.7 jit_solution(18390818902762660298)
XLA Ops:
  0.7 0.7 convert_bitcast_fusion
  1.4 1.0 %broadcast_multiply_fusion.refs_0_.m_ref = bf16[128,1536]{1,0:T(8,128)(2,1)S(1)} fusion(bf16[128,1536]{1,0:T(8,128)(2,1)} %param.8, bf16[1536]{0:T(1024)(128)(2,1)S(1)} %broadcast_bitcast_fusion), kind=kLoop, calls=%fused_computation.1 | loop fusion | flops 196608 | bytes 789504 | tf_op jit(solution)/shard_map/mul | solution.py:157
  2.5 8.8 %collective-permute-start = (bf16[136,1536]{1,0:T(8,128)(2,1)S(1)}, bf16[136,1536]{1,0:T(8,128)(2,1)S(1)}, u32[]{:S(2)}, u32[]{:S(2)}) collective-permute-start(bf16[136,1536]{1,0:T(8,128)(2,1)S(1)} %pad.4), channel_id=1, source_target_pairs={{320,0},{321,1},{336,16},{337,17},{352,32},{353,33},{368,48},{369,... | collective-permute-start | bytes 1253384 | tf_op jit(solution)/shard_map/ppermute | solution.py:166
  11.3 4.2 %collective-permute-start.2 = (bf16[128,1536]{1,0:T(8,128)(2,1)S(1)}, bf16[128,1536]{1,0:T(8,128)(2,1)S(1)}, u32[]{:S(2)}, u32[]{:S(2)}) collective-permute-start(bf16[128,1536]{1,0:T(8,128)(2,1)S(1)} %broadcast_multiply_fusion.refs_0_.m_ref), channel_id=1, source_target_pairs={{16,0},{49,1},{32,16},{1,17},{48,32},{17,33},{0,48},{33,49},{80,64... | collective-permute-start | bytes 1179656 | tf_op jit(solution)/shard_map/ppermute | solution.py:166
  15.6 1.9 %collective-permute-start.1 = (bf16[128,1536]{1,0:T(8,128)(2,1)S(1)}, bf16[128,1536]{1,0:T(8,128)(2,1)S(1)}, u32[]{:S(2)}, u32[]{:S(2)}) collective-permute-start(bf16[128,1536]{1,0:T(8,128)(2,1)S(1)} %broadcast_multiply_fusion.refs_0_.m_ref), channel_id=1, source_target_pairs={{64,0},{65,1},{80,16},{81,17},{96,32},{97,33},{112,48},{113,49},{1... | collective-permute-start | bytes 1179656 | tf_op jit(solution)/shard_map/ppermute | solution.py:166
  17.6 1.4 %diag.1 = f32[128,128]{1,0:T(8,128)} custom-call(s32[2]{0:T(128)S(1)} %pad_add_fusion.ids, s32[1]{0:T(128)} %copy.11.period, f32[16]{0:T(128)S(1)} %copy-done, f32[1,1536]{1,0:T(1,128)S(1)} %reshape.34.d_ref, bf16[128,1536]{1,0:T(8,128)(2,1)S(1)} %broadcast_multiply_fusion.refs_0_.m_ref), custom_call_target="tpu_custom_call" | custom-call | tf_op jit(solution)/shard_map/diag/pallas_call | solution.py:175
  19.1 7.4 %all-to-all-start = ((f32[16,8,128]{2,1,0:T(8,128)}), f32[16,8,128]{2,1,0:T(8,128)S(1)}, u32[]{:S(2)}, u32[]{:S(2)}) async-start(f32[16,8,128]{2,1,0:T(8,128)} %bitcast.9), calls=%async_computation | async-start | bytes 131072 | tf_op jit(solution)/shard_map/all_to_all | solution.py:183
  26.5 3.8 %collective-permute-start.3 = (bf16[128,1536]{1,0:T(8,128)(2,1)S(1)}, bf16[128,1536]{1,0:T(8,128)(2,1)S(1)}, u32[]{:S(2)}, u32[]{:S(2)}) collective-permute-start(bf16[128,1536]{1,0:T(8,128)(2,1)S(1)} %broadcast_multiply_fusion.refs_0_.m_ref), channel_id=1, source_target_pairs={{48,0},{17,1},{0,16},{33,17},{16,32},{49,33},{32,48},{1,49},{112,6... | collective-permute-start | bytes 1179656 | tf_op jit(solution)/shard_map/ppermute | solution.py:166
  30.3 2.4 %collective-permute-start.5 = (bf16[128,1536]{1,0:T(8,128)(2,1)S(1)}, bf16[128,1536]{1,0:T(8,128)(2,1)S(1)}, u32[]{:S(2)}, u32[]{:S(2)}) collective-permute-start(bf16[128,1536]{1,0:T(8,128)(2,1)S(1)} %collective-permute-done.2.refs_3_), channel_id=1, source_target_pairs={{16,0},{49,1},{32,16},{1,17},{48,32},{17,33},{0,48},{33,49},{80,64... | collective-permute-start | bytes 1179656 | tf_op jit(solution)/shard_map/ppermute | solution.py:166
  32.7 3.1 %collective-permute-start.4 = (bf16[128,1536]{1,0:T(8,128)(2,1)S(1)}, bf16[128,1536]{1,0:T(8,128)(2,1)S(1)}, u32[]{:S(2)}, u32[]{:S(2)}) collective-permute-start(bf16[128,1536]{1,0:T(8,128)(2,1)S(1)} %collective-permute-done.1.refs_2_), channel_id=1, source_target_pairs={{64,0},{65,1},{80,16},{81,17},{96,32},{97,33},{112,48},{113,49},{1... | collective-permute-start | bytes 1179656 | tf_op jit(solution)/shard_map/ppermute | solution.py:166
  35.9 4.5 %collective-permute-done.refs_1_ = bf16[136,1536]{1,0:T(8,128)(2,1)S(1)} collective-permute-done((bf16[136,1536]{1,0:T(8,128)(2,1)S(1)}, bf16[136,1536]{1,0:T(8,128)(2,1)S(1)}, u32[]{:S(2)}, u32[]{:S(2)}) %collective-permute-start) | collective-permute-done | bytes 417824 | tf_op jit(solution)/shard_map/ppermute | solution.py:166
  40.3 1.9 %collective-permute-start.6 = (bf16[136,1536]{1,0:T(8,128)(2,1)S(1)}, bf16[136,1536]{1,0:T(8,128)(2,1)S(1)}, u32[]{:S(2)}, u32[]{:S(2)}) collective-permute-start(bf16[136,1536]{1,0:T(8,128)(2,1)S(1)} %collective-permute-done.refs_1_), channel_id=1, source_target_pairs={{448,0},{449,1},{464,16},{465,17},{480,32},{481,33},{496,48},{497,... | collective-permute-start | bytes 1253384 | tf_op jit(solution)/shard_map/ppermute | solution.py:166
  42.3 0.7 dynamic-slice_bitcast_fusion
  43.0 2.3 %early.1 = (f32[8,128,128]{2,1,0:T(8,128)S(1)}, bf16[5,128,1536]{2,1,0:T(8,128)(2,1)S(1)}, bf16[5,128,1536]{2,1,0:T(8,128)(2,1)S(1)}) custom-call(s32[16]{0:T(128)S(1)} %get-tuple-element.22.left, s32[16]{0:T(128)S(1)} %get-tuple-element.21.right, f32[1,1536]{1,0:T(1,128)S(1)} %reshape.34.d_ref, bf16[128,1536]{1,0:T(8,128)(2,1)S(1)} %broadcast_multiply_fusion.refs_0_.m_ref, ...), custom_call_target="tpu_custom_call" | custom-call | tf_op jit(solution)/shard_map/early/pallas_call | solution.py:193
  45.3 1.8 %late.1 = (f32[16,136,128]{2,1,0:T(8,128)S(1)}, bf16[7,128,1536]{2,1,0:T(8,128)(2,1)S(1)}, bf16[7,128,1536]{2,1,0:T(8,128)(2,1)S(1)}) custom-call(s32[16]{0:T(128)S(1)} %get-tuple-element.22.left, s32[16]{0:T(128)S(1)} %get-tuple-element.21.right, f32[1,1536]{1,0:T(1,128)S(1)} %reshape.34.d_ref, bf16[5,128,1536]{2,1,0:T(8,128)(2,1)S(1)} %get-tuple-element.11.masked_in, ...), custom_call_target="tpu_custom_call" | custom-call | tf_op jit(solution)/shard_map/late/pallas_call | solution.py:202
  47.2 5.8 %collective-permute-done.6.row = bf16[136,1536]{1,0:T(8,128)(2,1)S(1)} collective-permute-done((bf16[136,1536]{1,0:T(8,128)(2,1)S(1)}, bf16[136,1536]{1,0:T(8,128)(2,1)S(1)}, u32[]{:S(2)}, u32[]{:S(2)}) %collective-permute-start.6) | collective-permute-done | bytes 417824 | tf_op jit(solution)/shard_map/ppermute | solution.py:166
  53.0 1.1 %last.1 = f32[16,136,128]{2,1,0:T(8,128)S(1)} custom-call(s32[16]{0:T(128)S(1)} %get-tuple-element.22.left, s32[16]{0:T(128)S(1)} %get-tuple-element.21.right, f32[1,1536]{1,0:T(1,128)S(1)} %reshape.34.d_ref, bf16[7,128,1536]{2,1,0:T(8,128)(2,1)S(1)} %get-tuple-element.14.masked, ...), custom_call_target="tpu_custom_call", output_to_operand_aliasing={{}: (6, {})} | custom-call | tf_op jit(solution)/shard_map/last/pallas_call | solution.py:210
  54.1 0.1 convert_element_type.15
  54.2 16.9 %all_to_all.14 = f16[16,136,128]{2,1,0:T(8,128)(2,1)S(1)} all-to-all(f16[16,136,128]{2,1,0:T(8,128)(2,1)S(1)} %convert_element_type.15), channel_id=1, replica_groups=mesh['z'=8,'yh'=4,'x'=4,'yl'=2,'core'=2] {'x','yl','core'}, dimensions={0} | all-to-all | bytes 1114112 | tf_op jit(solution)/shard_map/all_to_all | solution.py:221
  71.2 4.8 %collective-permute-start.8 = (f32[128,128]{1,0:T(8,128)S(1)}, f32[128,128]{1,0:T(8,128)S(1)}, u32[]{:S(2)}, u32[]{:S(2)}) collective-permute-start(f32[128,128]{1,0:T(8,128)S(1)} %slice_reduce_fusion), channel_id=1, source_target_pairs={{0,0},{13,17},{26,26},{18,18},{22,90},{24,42},{30,34},{20,10},{28,... | collective-permute-start | bytes 196616 | tf_op jit(solution)/shard_map/ppermute | solution.py:225
  76.0 1.3 %collective-permute-start.7 = (f32[128,128]{1,0:T(8,128)S(1)}, f32[128,128]{1,0:T(8,128)S(1)}, u32[]{:S(2)}, u32[]{:S(2)}) collective-permute-start(f32[128,128]{1,0:T(8,128)S(1)} %slice_reduce_fusion), channel_id=1, source_target_pairs={{10,10},{2,2},{6,74},{8,26},{14,18},{4,58},{12,50},{5,4},{1,20},{7... | collective-permute-start | bytes 196616 | tf_op jit(solution)/shard_map/ppermute | solution.py:224
  77.3 2.5 %collective-permute-done.8 = f32[128,128]{1,0:T(8,128)S(1)} collective-permute-done((f32[128,128]{1,0:T(8,128)S(1)}, f32[128,128]{1,0:T(8,128)S(1)}, u32[]{:S(2)}, u32[]{:S(2)}) %collective-permute-start.8) | collective-permute-done | bytes 65568 | tf_op jit(solution)/shard_map/ppermute | solution.py:225
  79.8 7.2 %collective-permute-done.7 = f32[128,128]{1,0:T(8,128)S(1)} collective-permute-done((f32[128,128]{1,0:T(8,128)S(1)}, f32[128,128]{1,0:T(8,128)S(1)}, u32[]{:S(2)}, u32[]{:S(2)}) %collective-permute-start.7) | collective-permute-done | bytes 65568 | tf_op jit(solution)/shard_map/ppermute | solution.py:224
  87.1 0.7 pad_maximum_fusion
  (20 shorter events, 0.4 us)
Async XLA Ops:
  0.0 17.5 %copy-start.1 = (f32[1536]{0:T(1024)S(1)}, f32[1536]{0:T(1024)}, u32[]{:S(2)}) copy-start(f32[1536]{0:T(1024)} %param.10) | copy-start | bytes 18436
  0.0 17.6 %copy-start = (f32[16]{0:T(128)S(1)}, f32[16]{0:T(128)}, u32[]{:S(2)}) copy-start(f32[16]{0:T(128)} %damping.1) | copy-start | bytes 196
  2.5 37.8 %collective-permute-start = (bf16[136,1536]{1,0:T(8,128)(2,1)S(1)}, bf16[136,1536]{1,0:T(8,128)(2,1)S(1)}, u32[]{:S(2)}, u32[]{:S(2)}) collective-permute-start(bf16[136,1536]{1,0:T(8,128)(2,1)S(1)} %pad.4), channel_id=1, source_target_pairs={{320,0},{321,1},{336,16},{337,17},{352,32},{353,33},{368,48},{369,... | collective-permute-start | bytes 1253384 | tf_op jit(solution)/shard_map/ppermute | solution.py:166
  11.3 18.9 %collective-permute-start.2 = (bf16[128,1536]{1,0:T(8,128)(2,1)S(1)}, bf16[128,1536]{1,0:T(8,128)(2,1)S(1)}, u32[]{:S(2)}, u32[]{:S(2)}) collective-permute-start(bf16[128,1536]{1,0:T(8,128)(2,1)S(1)} %broadcast_multiply_fusion.refs_0_.m_ref), channel_id=1, source_target_pairs={{16,0},{49,1},{32,16},{1,17},{48,32},{17,33},{0,48},{33,49},{80,64... | collective-permute-start | bytes 1179656 | tf_op jit(solution)/shard_map/ppermute | solution.py:166
  15.6 17.2 %collective-permute-start.1 = (bf16[128,1536]{1,0:T(8,128)(2,1)S(1)}, bf16[128,1536]{1,0:T(8,128)(2,1)S(1)}, u32[]{:S(2)}, u32[]{:S(2)}) collective-permute-start(bf16[128,1536]{1,0:T(8,128)(2,1)S(1)} %broadcast_multiply_fusion.refs_0_.m_ref), channel_id=1, source_target_pairs={{64,0},{65,1},{80,16},{81,17},{96,32},{97,33},{112,48},{113,49},{1... | collective-permute-start | bytes 1179656 | tf_op jit(solution)/shard_map/ppermute | solution.py:166
  19.1 23.9 %all-to-all-start = ((f32[16,8,128]{2,1,0:T(8,128)}), f32[16,8,128]{2,1,0:T(8,128)S(1)}, u32[]{:S(2)}, u32[]{:S(2)}) async-start(f32[16,8,128]{2,1,0:T(8,128)} %bitcast.9), calls=%async_computation | async-start | bytes 131072 | tf_op jit(solution)/shard_map/all_to_all | solution.py:183
  26.5 16.5 %collective-permute-start.3 = (bf16[128,1536]{1,0:T(8,128)(2,1)S(1)}, bf16[128,1536]{1,0:T(8,128)(2,1)S(1)}, u32[]{:S(2)}, u32[]{:S(2)}) collective-permute-start(bf16[128,1536]{1,0:T(8,128)(2,1)S(1)} %broadcast_multiply_fusion.refs_0_.m_ref), channel_id=1, source_target_pairs={{48,0},{17,1},{0,16},{33,17},{16,32},{49,33},{32,48},{1,49},{112,6... | collective-permute-start | bytes 1179656 | tf_op jit(solution)/shard_map/ppermute | solution.py:166
  30.3 15.0 %collective-permute-start.5 = (bf16[128,1536]{1,0:T(8,128)(2,1)S(1)}, bf16[128,1536]{1,0:T(8,128)(2,1)S(1)}, u32[]{:S(2)}, u32[]{:S(2)}) collective-permute-start(bf16[128,1536]{1,0:T(8,128)(2,1)S(1)} %collective-permute-done.2.refs_3_), channel_id=1, source_target_pairs={{16,0},{49,1},{32,16},{1,17},{48,32},{17,33},{0,48},{33,49},{80,64... | collective-permute-start | bytes 1179656 | tf_op jit(solution)/shard_map/ppermute | solution.py:166
  32.7 12.6 %collective-permute-start.4 = (bf16[128,1536]{1,0:T(8,128)(2,1)S(1)}, bf16[128,1536]{1,0:T(8,128)(2,1)S(1)}, u32[]{:S(2)}, u32[]{:S(2)}) collective-permute-start(bf16[128,1536]{1,0:T(8,128)(2,1)S(1)} %collective-permute-done.1.refs_2_), channel_id=1, source_target_pairs={{64,0},{65,1},{80,16},{81,17},{96,32},{97,33},{112,48},{113,49},{1... | collective-permute-start | bytes 1179656 | tf_op jit(solution)/shard_map/ppermute | solution.py:166
  40.3 12.6 %collective-permute-start.6 = (bf16[136,1536]{1,0:T(8,128)(2,1)S(1)}, bf16[136,1536]{1,0:T(8,128)(2,1)S(1)}, u32[]{:S(2)}, u32[]{:S(2)}) collective-permute-start(bf16[136,1536]{1,0:T(8,128)(2,1)S(1)} %collective-permute-done.refs_1_), channel_id=1, source_target_pairs={{448,0},{449,1},{464,16},{465,17},{480,32},{481,33},{496,48},{497,... | collective-permute-start | bytes 1253384 | tf_op jit(solution)/shard_map/ppermute | solution.py:166
  71.2 8.6 %collective-permute-start.8 = (f32[128,128]{1,0:T(8,128)S(1)}, f32[128,128]{1,0:T(8,128)S(1)}, u32[]{:S(2)}, u32[]{:S(2)}) collective-permute-start(f32[128,128]{1,0:T(8,128)S(1)} %slice_reduce_fusion), channel_id=1, source_target_pairs={{0,0},{13,17},{26,26},{18,18},{22,90},{24,42},{30,34},{20,10},{28,... | collective-permute-start | bytes 196616 | tf_op jit(solution)/shard_map/ppermute | solution.py:225
  76.0 11.0 %collective-permute-start.7 = (f32[128,128]{1,0:T(8,128)S(1)}, f32[128,128]{1,0:T(8,128)S(1)}, u32[]{:S(2)}, u32[]{:S(2)}) collective-permute-start(f32[128,128]{1,0:T(8,128)S(1)} %slice_reduce_fusion), channel_id=1, source_target_pairs={{10,10},{2,2},{6,74},{8,26},{14,18},{4,58},{12,50},{5,4},{1,20},{7... | collective-permute-start | bytes 196616 | tf_op jit(solution)/shard_map/ppermute | solution.py:224
